TPU v7x, 32 devices: a whole 2x2x4 slice. The times are simulated.
32 devices in a mesh: sec: 2 (over y), row: 8 (over z, x), col: 2 (over core).
Axes of the slice: x: 2, y: 2, z: 4, core: 2. Of those that a mesh axis runs over, the one named last changes fastest.
Arguments:
- basis_matrix: bfloat16 [10240, 4096], P('row', 'col'), may hold values from -6 to 6
- operator_blocks: bfloat16 [80, 7, 128, 128], P('row', None, 'sec'), may hold values from -0.1875 to 0.1875
- neighbours: int32 [80, 7], P('row'), may hold values from 0 to 79, as said below
- neighbour_mask: int32 [80, 7], P('row'), may hold values from 0 to 1, as said below
Outputs:
- reduced: float32 [4096, 4096], P(('sec', 'row'), 'col')
Inputs may be any that keep to these rules, and one draw needn't show every extreme that they name: `neighbours`: slot 0 of row block b is b; slots 1 to 4 are b - 1, b + 1, b - 2, b + 2; slots 5 and 6 lie within 2 blocks of b; a slot whose mask is 0 holds b. `neighbour_mask`: 0 exactly where slots 1 to 4 fall outside the slab, and at random in slots 5 and 6 (also where they fall outside); slot 0 is always 1.
All inputs are finite; a program needn't handle non-finite values.
Results may differ from a plain program's by a relative error of at most 0.0029.
Values may be sent and summed in bfloat16 or wider, within the bound.
No kernel may reach another device: no remote copies, remote signals or barrier semaphores. Data moves between devices by JAX's collectives and lax.ppermute only.
A program may use at most 192 MiB of HBM per device.

v0:
```python
import math

import jax
import jax.numpy as jnp
from jax import lax
from jax.sharding import PartitionSpec as P

REACH = 2


def padded(shard, sides, width):
    for axis, dim in sides:
        count, length = (lax.axis_size(axis), shard.shape[dim])
        up = [(i, (i + 1) % count) for i in range(count - 1)]
        down = [(j, i) for i, j in up]
        last = lax.slice_in_dim(shard, length - width, length, axis=dim)
        leading = lax.slice_in_dim(shard, 0, width, axis=dim)
        before = lax.ppermute(last, axis, up)
        after = lax.ppermute(leading, axis, down)
        shard = jnp.concatenate([before, shard, after], axis=dim)
    return shard


def slot_product(operator_blocks, reduced_basis_tiles, neighbour, coupling_weight):
    sparse_block_list = operator_blocks[:, neighbour]
    operator_product = jnp.einsum(
        "hol,hla->hoa", sparse_block_list, reduced_basis_tiles, preferred_element_type=jnp.float32
    )
    return coupling_weight[:, None, None] * operator_product


def per_device(basis_matrix, operator_blocks, neighbours, neighbour_mask):
    local_rows, column_count = basis_matrix.shape
    block_count, slot_count, half_rows, block_rows = operator_blocks.shape
    weights = neighbour_mask.astype(jnp.float32)
    applied_total_sum = jnp.zeros((block_count, half_rows, column_count), jnp.float32)
    first_slot = 0
    extended = padded(basis_matrix, (("row", 0),), REACH * block_rows)
    rim_tiles = extended.reshape(block_count + 2 * REACH, block_rows, column_count)
    offset_index = neighbours - lax.axis_index("row") * block_count + REACH
    for neighbour in range(first_slot, slot_count):
        selected_entries = jnp.take(rim_tiles, offset_index[:, neighbour], axis=0)
        applied_total_sum = applied_total_sum + slot_product(
            operator_blocks, selected_entries, neighbour, weights[:, neighbour]
        )
    applied_half = applied_total_sum.astype(jnp.bfloat16)
    applied = lax.all_gather(applied_half, "sec", axis=1, tiled=True).reshape(
        local_rows, column_count
    )
    left_width = column_count * lax.axis_size("col") // lax.axis_size("sec")
    everything = lax.all_gather(basis_matrix, "col", axis=1, tiled=True)
    left_projector = lax.dynamic_slice_in_dim(
        everything, lax.axis_index("sec") * left_width, left_width, 1
    )
    scaling = 1.0 / math.sqrt(local_rows * lax.axis_size("row"))
    partial_tile = scaling * lax.dot_general(
        left_projector, applied, (((0,), (0,)), ((), ())), preferred_element_type=jnp.float32
    )
    reduced = lax.psum_scatter(partial_tile, "row", scatter_dimension=0, tiled=True)
    return reduced


def solution(mesh):
    return jax.shard_map(
        per_device,
        mesh=mesh,
        in_specs=(P("row", "col"), P("row", None, "sec", None), P("row", None), P("row", None)),
        out_specs=P(("sec", "row"), "col"),
        check_vma=False,
    )
```

profile of v0, /device:TPU:0, one launch (start us, length us, event | category | flops | bytes accessed | tf_op | source)
XLA Modules:
  0.0 554.7 jit_solution(7774492357886018531)
XLA Ops:
  6.5 2.7 fusion.54
  9.2 4.9 collective-permute-start
  14.1 1.3 collective-permute-start.1
  16.9 42.3 %collective-permute-done = bf16[256,2048]{1,0:T(8,128)(2,1)S(1)} collective-permute-done((bf16[256,2048]{1,0:T(8,128)(2,1)}, bf16[256,2048]{1,0:T(8,128)(2,1)S(1)}, u32[]{:S(2)}, u32[]{:S(2)}) %collective-permute-start) | collective-permute-done | bytes 1048608 | tf_op jit(solution)/shard_map/ppermute | solution.py:18
  59.3 6.0 %pad_maximum_fusion = bf16[1792,2048]{1,0:T(8,128)(2,1)} fusion(bf16[256,2048]{1,0:T(8,128)(2,1)S(1)} %collective-permute-done.1, bf16[1280,2048]{1,0:T(8,128)(2,1)} %param.6, bf16[256,2048]{1,0:T(8,128)(2,1)S(1)} %collective-permute-done), kind=kLoop, calls=%fused_computation.8 | loop fusion | flops 22020096 | bytes 14680064 | tf_op jit(solution)/shard_map/concatenate | solution.py:20
  65.3 6.9 %gather_fusion.1 = bf16[10,128,2048]{2,1,0:T(8,128)(2,1)} fusion(bf16[14,128,2048]{2,1,0:T(8,128)(2,1)} %bitcast.75, s32[1024]{0:T(1024)S(1)} %get-tuple-element.46), kind=kCustom, calls=%fused_computation.1.clone | custom fusion | bytes 10485800 | tf_op jit(solution)/shard_map/jit(_take)/gather | solution.py:42
  72.2 7.0 %gather_fusion.4 = bf16[10,128,2048]{2,1,0:T(8,128)(2,1)} fusion(bf16[14,128,2048]{2,1,0:T(8,128)(2,1)} %bitcast.76, s32[1024]{0:T(1024)S(1)} %get-tuple-element.43), kind=kCustom, calls=%fused_computation.4.clone | custom fusion | bytes 10485800 | tf_op jit(solution)/shard_map/jit(_take)/gather | solution.py:42
  79.2 7.0 %gather_fusion.3 = bf16[10,128,2048]{2,1,0:T(8,128)(2,1)} fusion(bf16[14,128,2048]{2,1,0:T(8,128)(2,1)} %bitcast.77, s32[1024]{0:T(1024)S(1)} %get-tuple-element.44), kind=kCustom, calls=%fused_computation.3.clone | custom fusion | bytes 10485800 | tf_op jit(solution)/shard_map/jit(_take)/gather | solution.py:42
  86.2 6.9 %gather_fusion.2 = bf16[10,128,2048]{2,1,0:T(8,128)(2,1)} fusion(bf16[14,128,2048]{2,1,0:T(8,128)(2,1)} %bitcast.78, s32[1024]{0:T(1024)S(1)} %get-tuple-element.45), kind=kCustom, calls=%fused_computation.2.clone | custom fusion | bytes 10485800 | tf_op jit(solution)/shard_map/jit(_take)/gather | solution.py:42
  93.1 6.9 %gather_fusion.5 = bf16[10,128,2048]{2,1,0:T(8,128)(2,1)} fusion(bf16[14,128,2048]{2,1,0:T(8,128)(2,1)} %bitcast.79, s32[1024]{0:T(1024)S(1)} %get-tuple-element.42), kind=kCustom, calls=%fused_computation.5.clone | custom fusion | bytes 10485800 | tf_op jit(solution)/shard_map/jit(_take)/gather | solution.py:42
  100.0 6.9 %gather_fusion.6 = bf16[10,128,2048]{2,1,0:T(8,128)(2,1)} fusion(bf16[14,128,2048]{2,1,0:T(8,128)(2,1)} %bitcast.80, s32[1024]{0:T(1024)S(1)} %get-tuple-element.41), kind=kCustom, calls=%fused_computation.6.clone | custom fusion | bytes 10485800 | tf_op jit(solution)/shard_map/jit(_take)/gather | solution.py:42
  106.9 7.0 %gather_fusion = bf16[10,128,2048]{2,1,0:T(8,128)(2,1)} fusion(bf16[14,128,2048]{2,1,0:T(8,128)(2,1)} %bitcast.81, s32[1024]{0:T(1024)S(1)} %pad_clamp_fusion.6), kind=kCustom, calls=%fused_computation.clone | custom fusion | bytes 10485800 | tf_op jit(solution)/shard_map/jit(_take)/gather | solution.py:42
  113.9 3.7 fusion.10
  117.7 6.1 %fusion.4 = f32[10,2048,64]{1,2,0:T(8,128)} fusion(bf16[10,128,2048]{2,1,0:T(8,128)(2,1)} %gather_fusion.4, pred[10]{0:T(512)(128)(4,1)S(1)} %get-tuple-element.24, bf16[10,7,64,128]{3,2,1,0:T(8,128)(2,1)S(1)} %copy-done), kind=kOutput, calls=%fused_computation.13 | convolution fusion | flops 338165760 | bytes 10650112 | tf_op jit(solution)/shard_map/hol,hla->hoa/dot_general | solution.py:26
  123.7 3.5 fusion.6
  127.2 3.4 fusion.8
  130.6 3.4 fusion.2
  134.0 3.4 fusion.12
  137.4 13.9 %fusion.29 = bf16[10,64,2048]{2,1,0:T(8,128)(2,1)} fusion(f32[10]{0:T(128)S(1)} %get-tuple-element.35, f32[10,2048,64]{1,2,0:T(8,128)} %fusion.2, f32[10]{0:T(128)S(1)} %get-tuple-element.36, f32[10,2048,64]{1,2,0:T(8,128)} %fusion.4, f32[10]{0:T(128)S(1)} %get-tuple-element.37, f32[10,2048,64]{1,2,0:T(8,128)} %fusion.6, f32[10]{0:T(128)S(1)} %get-tuple-element.38, ...), kind=kOutput, calls=%fused_computation.39 | convolution fusion | flops 356515840 | bytes 39489536 | tf_op jit(solution)/shard_map/hol,hla->hoa/dot_general | solution.py:26
  151.4 0.7 all-gather.3.cloned.1.call-update
  152.2 70.0 %all-gather.5.cloned.1.call-done = bf16[10,128,2048]{2,1,0:T(8,128)(2,1)} async-done(((bf16[10,64,2048]{2,1,0:T(8,128)(2,1)}), bf16[10,128,2048]{2,1,0:T(8,128)(2,1)}) %all-gather.5.cloned.1.call-update) | async-done | bytes 5242896 | tf_op jit(solution)/shard_map/all_gather | solution.py:47
  222.2 24.5 %all-gather.3.cloned.1.call-done = bf16[1280,4096]{1,0:T(8,128)(2,1)} async-done(((bf16[1280,2048]{1,0:T(8,128)(2,1)}), bf16[1280,4096]{1,0:T(8,128)(2,1)}) %all-gather.3.cloned.1.call-update) | async-done | bytes 10485776 | tf_op jit(solution)/shard_map/all_gather | solution.py:51
  246.6 17.9 %convolution_multiply_fusion = f32[2048,2048]{1,0:T(8,128)} fusion(bf16[1280,2048]{1,0:T(8,128)(2,1)} %bitcast.90, bf16[1280,4096]{1,0:T(8,128)(2,1)} %all-gather.3.cloned.1.call-done, s32[]{:T(128)S(6)} %select_n.10), kind=kOutput, calls=%fused_computation.7 | convolution fusion | flops 10741612544 | bytes 27262980 | tf_op jit(solution)/shard_map/dot_general | solution.py:56
  264.5 283.6 %reduce-scatter.2.cloned.1.call-done = f32[256,2048]{1,0:T(8,128)} async-done(((f32[2048,2048]{1,0:T(8,128)}), f32[256,2048]{1,0:T(8,128)}) %reduce-scatter.2.cloned.1.call-update) | async-done | bytes 2097168 | tf_op jit(solution)/shard_map/reduce_scatter | solution.py:59
  (36 shorter events, 1.6 us)
Async XLA Ops:
  6.5 215.6 %all-gather.5.cloned.1.call-start = ((), (), s32[]{:S(2)}) async-start(), calls=%async_computation.2 | async-start | bytes 7864320 | tf_op jit(solution)/shard_map/all_gather | solution.py:47
  9.2 50.0 %collective-permute-start = (bf16[256,2048]{1,0:T(8,128)(2,1)}, bf16[256,2048]{1,0:T(8,128)(2,1)S(1)}, u32[]{:S(2)}, u32[]{:S(2)}) collective-permute-start(bf16[256,2048]{1,0:T(8,128)(2,1)} %get-tuple-element.20), channel_id=1, source_target_pairs={{0,2},{2,4},{4,6},{6,8},{8,10},{10,12},{12,14},{1,3},{3,5},{5,7},{... | collective-permute-start | bytes 3145736 | tf_op jit(solution)/shard_map/ppermute | solution.py:18
  14.1 45.1 %collective-permute-start.1 = (bf16[256,2048]{1,0:T(8,128)(2,1)S(1)}, bf16[256,2048]{1,0:T(8,128)(2,1)S(1)}, u32[]{:S(2)}, u32[]{:S(2)}) collective-permute-start(bf16[256,2048]{1,0:T(8,128)(2,1)S(1)} %get-tuple-element.21), channel_id=1, source_target_pairs={{2,0},{4,2},{6,4},{8,6},{10,8},{12,10},{14,12},{3,1},{5,3},{7,5},{... | collective-permute-start | bytes 3145736 | tf_op jit(solution)/shard_map/ppermute | solution.py:19
  106.9 7.0 %copy-start = (bf16[10,7,64,128]{3,2,1,0:T(8,128)(2,1)S(1)}, bf16[10,7,64,128]{3,2,1,0:T(8,128)(2,1)}, u32[]{:S(2)}) copy-start(bf16[10,7,64,128]{3,2,1,0:T(8,128)(2,1)} %param.7) | copy-start | bytes 3440644
  113.9 9.8 %slice-start.2 = ((s8[5242880]{0:T(1024)(128)(4,1)}), s8[4194304]{0:T(1024)(128)(4,1)S(1)}, s32[]{:S(2)}) async-start(s8[5242880]{0:T(1024)(128)(4,1)} %bitcast.84), calls=%async_computation.6 | async-start | bytes 8388608
  117.7 6.1 %slice-start.3 = ((s8[5242880]{0:T(1024)(128)(4,1)}), s8[1048576]{0:T(1024)(128)(4,1)S(1)}, s32[]{:S(2)}) async-start(s8[5242880]{0:T(1024)(128)(4,1)} %bitcast.84), calls=%async_computation.7 | async-start | bytes 2097152
  117.7 9.5 %slice-start.4 = ((s8[5242880]{0:T(1024)(128)(4,1)}), s8[4194304]{0:T(1024)(128)(4,1)S(1)}, s32[]{:S(2)}) async-start(s8[5242880]{0:T(1024)(128)(4,1)} %bitcast.86), calls=%async_computation.8 | async-start | bytes 8388608
  123.7 3.5 slice-start.5
  123.7 6.9 %slice-start = ((s8[5242880]{0:T(1024)(128)(4,1)}), s8[4194304]{0:T(1024)(128)(4,1)S(1)}, s32[]{:S(2)}) async-start(s8[5242880]{0:T(1024)(128)(4,1)} %bitcast.82), calls=%async_computation.4 | async-start | bytes 8388608
  127.2 3.4 slice-start.1
  127.2 6.8 %slice-start.6 = ((s8[5242880]{0:T(1024)(128)(4,1)}), s8[4194304]{0:T(1024)(128)(4,1)S(1)}, s32[]{:S(2)}) async-start(s8[5242880]{0:T(1024)(128)(4,1)} %bitcast.88), calls=%async_computation.10 | async-start | bytes 8388608
  130.6 3.4 slice-start.7
  151.4 95.3 %all-gather.3.cloned.1.call-start = ((), (), s32[]{:S(2)}) async-start(), calls=%async_computation.1 | async-start | bytes 15728640 | tf_op jit(solution)/shard_map/all_gather | solution.py:51
  152.1 396.0 %reduce-scatter.2.cloned.1.call-start = ((), (), s32[]{:S(2)}) async-start(), calls=%async_computation.3 | async-start | bytes 18874368 | tf_op jit(solution)/shard_map/reduce_scatter | solution.py:59
Sparse Core Ops, SparseCore 0:
  151.5 70.6 all-gather.4
  223.7 22.8 all-gather.2
  264.7 283.4 reduce-scatter.1
where the time goes:
time: 555 us
  waiting for transfers between devices  421 us (76%)
  matrix products  55.2 us (10%)
  local copies, waits for them, and re-layouts  51.4 us (9%)
  between operations  13.2 us (2%)
  other arithmetic  7.46 us (1%)
  starting transfers between devices  6.27 us (1%)
    reduce_scatter x1, waiting for transfers between devices, per_device(): lax.psum_scatter(partial_tile, 'row', scatter_dimension=0, tiled=True)  284 us
    all_gather x1, waiting for transfers between devices, per_device(): lax.all_gather(applied_half, 'sec', axis=1, tiled=True)  70 us
    gather x7, local copies, waits for them, and re-layouts, per_device(): selected_entries = jnp.take(rim_tiles, offset_index[:, neighbour], axis=0)  48.6 us
    ppermute x1, waiting for transfers between devices, padded(): before = lax.ppermute(last, axis, up)  42.3 us
    dot_general x7, matrix products, slot_product(): jnp.einsum('hol,hla->hoa', sparse_block_list, reduced_basis_tiles, prefer...  37.3 us
    all_gather x1, waiting for transfers between devices, per_device(): everything = lax.all_gather(basis_matrix, 'col', axis=1, tiled=True)  24.5 us
    dot_general x1, matrix products, per_device(): lax.dot_general(left_projector, applied, (((0,), (0,)), ((), ())), prefer...  17.9 us
  transfers between devices with their start and end apart: 5, of which 4 were waited for; matrix products, arithmetic and copies ran while one was open for 0% of the time, Pallas kernels for 0%

commit v1 on v0

v1 whole, which is shorter than its diff:
```python
import math

import jax
import jax.numpy as jnp
from jax import lax
from jax.experimental import pallas as pl
from jax.experimental.pallas import tpu as pltpu
from jax.sharding import PartitionSpec as P

REACH = 2
VMEM_LIMIT = 48 * 1024 * 1024


def apply_operator(basis, before, after, own_ops, other_ops, offsets, weights, order):
    rows, width = basis.shape
    blocks, slots, half, block = own_ops.shape
    rim = before.shape[0]
    tile = min(512, width)

    def kernel(off_ref, w_ref, order_ref, basis_ref, before_ref, after_ref, own_ref, other_ref, out_ref, ext):
        ext[pl.ds(0, rim), :] = before_ref[...]
        ext[pl.ds(rim, rows), :] = basis_ref[...]
        ext[pl.ds(rim + rows, rim), :] = after_ref[...]
        first = pl.multiple_of(order_ref[0] * half, half)
        second = pl.multiple_of((1 - order_ref[0]) * half, half)

        def body(b, carry):
            rhs = [
                ext[pl.ds(pl.multiple_of(off_ref[b, s] * block, block), block), :]
                for s in range(slots)
            ]
            lhs = [
                jnp.concatenate([own_ref[b, s], other_ref[b, s]], axis=0)
                * w_ref[b, s].astype(jnp.bfloat16)
                for s in range(slots)
            ]
            total = jnp.dot(
                jnp.concatenate(lhs, axis=1),
                jnp.concatenate(rhs, axis=0),
                preferred_element_type=jnp.float32,
            ).astype(jnp.bfloat16)
            base = pl.multiple_of(b * block, block)
            out_ref[pl.ds(base + first, half), :] = total[:half]
            out_ref[pl.ds(base + second, half), :] = total[half:]
            return carry

        lax.fori_loop(0, blocks, body, 0)

    return pl.pallas_call(
        kernel,
        grid_spec=pltpu.PrefetchScalarGridSpec(
            num_scalar_prefetch=3,
            grid=(width // tile,),
            in_specs=[
                pl.BlockSpec((rows, tile), lambda j, *_: (0, j)),
                pl.BlockSpec((rim, tile), lambda j, *_: (0, j)),
                pl.BlockSpec((rim, tile), lambda j, *_: (0, j)),
                pl.BlockSpec(own_ops.shape, lambda j, *_: (0, 0, 0, 0)),
                pl.BlockSpec(other_ops.shape, lambda j, *_: (0, 0, 0, 0)),
            ],
            out_specs=pl.BlockSpec((rows, tile), lambda j, *_: (0, j)),
            scratch_shapes=[pltpu.VMEM((rows + 2 * rim, tile), jnp.bfloat16)],
        ),
        out_shape=jax.ShapeDtypeStruct((rows, width), jnp.bfloat16),
        compiler_params=pltpu.CompilerParams(vmem_limit_bytes=VMEM_LIMIT),
        cost_estimate=pl.CostEstimate(
            flops=2 * rows * slots * block * width,
            bytes_accessed=2 * (2 * rows * width + 2 * rim * width + 2 * own_ops.size),
            transcendentals=0,
        ),
        name="apply_operator",
    )(offsets, weights, order, basis, before, after, own_ops, other_ops)


def tile_chunk(left, applied, chunk, height, addend, out_dtype):
    rows, width = applied.shape
    tile = min(512, width)

    def kernel(chunk_ref, left_ref, applied_ref, *rest):
        out_ref = rest[-1]
        total = lax.dot_general(
            left_ref[...], applied_ref[...], (((0,), (0,)), ((), ())),
            preferred_element_type=jnp.float32,
        )
        if len(rest) == 2:
            total = total + rest[0][...].astype(jnp.float32)
        out_ref[...] = total.astype(out_ref.dtype)

    in_specs = [
        pl.BlockSpec((rows, height), lambda j, c: (0, c[0])),
        pl.BlockSpec((rows, tile), lambda j, c: (0, j)),
    ]
    operands = [left, applied]
    if addend is not None:
        in_specs.append(pl.BlockSpec((height, tile), lambda j, c: (0, j)))
        operands.append(addend)
    return pl.pallas_call(
        kernel,
        grid_spec=pltpu.PrefetchScalarGridSpec(
            num_scalar_prefetch=1,
            grid=(width // tile,),
            in_specs=in_specs,
            out_specs=pl.BlockSpec((height, tile), lambda j, c: (0, j)),
        ),
        out_shape=jax.ShapeDtypeStruct((height, width), out_dtype),
        compiler_params=pltpu.CompilerParams(vmem_limit_bytes=VMEM_LIMIT),
        cost_estimate=pl.CostEstimate(
            flops=2 * rows * height * width,
            bytes_accessed=2 * rows * (height + width) + 6 * height * width,
            transcendentals=0,
        ),
        name="tile_chunk",
    )(chunk, left, applied, *([] if addend is None else [addend]))


def per_device(basis, own_ops, neighbours, mask):
    rows, width = basis.shape
    blocks, slots, half, block = own_ops.shape
    sec, row, col = (lax.axis_index(name) for name in ("sec", "row", "col"))
    count = lax.axis_size("row")
    rim = REACH * block

    up = [(i, i + 1) for i in range(count - 1)]
    down = [(i + 1, i) for i in range(count - 1)]
    before = lax.ppermute(basis[rows - rim:], "row", up)
    after = lax.ppermute(basis[:rim], "row", down)
    other_ops = lax.ppermute(own_ops, "sec", [(0, 1), (1, 0)])
    moved = lax.ppermute(basis, ("sec", "col"), [(0, 1), (3, 2)])
    left = jnp.where(sec == col, basis, moved)

    offsets = neighbours - row * blocks + REACH
    applied = apply_operator(
        basis, before, after, own_ops, other_ops, offsets,
        mask.astype(jnp.float32), sec.astype(jnp.int32)[None],
    )

    groups = count // 2
    group, side = row // 2, row % 2
    height = width * lax.axis_size("col") // lax.axis_size("sec") // count
    pack = min(groups, max(1, 256 // height))
    packs = groups // pack
    if pack > 1:
        left = left.reshape(rows, groups, 2, height).swapaxes(1, 2).reshape(rows, -1)

    def column_block(step, which):
        target = (group // pack + step) % packs
        return (2 * target + which if pack == 1 else which * packs + target)[None]

    swap = [(i, i ^ 1) for i in range(count)]
    steps = sorted(range(1, packs), key=lambda k: -min(k, packs - k)) + [0]

    sums = {}
    for step in steps:
        away = tile_chunk(
            left, applied, column_block(step, 1 - side), pack * height, None, jnp.bfloat16
        )
        sums[step] = lax.ppermute(away, "row", swap)
    total = None
    arrived = []
    for step in steps:
        mine = tile_chunk(
            left, applied, column_block(step, side), pack * height, sums[step],
            jnp.float32 if step == 0 else jnp.bfloat16,
        )
        for i in range(pack):
            part = mine
            if pack > 1:
                place = (group + i) % pack * height
                part = lax.dynamic_slice_in_dim(mine, place, height, axis=0)
            if step == 0 and i == 0:
                total = part
                continue
            route = []
            for g in range(groups):
                to = (g // pack + step) % packs * pack + (g + i) % pack
                route += [(2 * g, 2 * to), (2 * g + 1, 2 * to + 1)]
            arrived.append(lax.ppermute(part.astype(jnp.bfloat16), "row", route))
    for part in arrived:
        total = total + part.astype(jnp.float32)
    return total * (1.0 / math.sqrt(rows * count))


def solution(mesh):
    return jax.shard_map(
        per_device,
        mesh=mesh,
        in_specs=(P("row", "col"), P("row", None, "sec", None), P("row", None), P("row", None)),
        out_specs=P(("sec", "row"), "col"),
        check_vma=False,
    )
```

time: 555 us -> 215 us (0.39)
  waiting for transfers between devices: 421 us -> 116 us
  Pallas kernels: 0 us -> 56.4 us
  matrix products: 55.2 us -> 0 us
  local copies, waits for them, and re-layouts: 51.4 us -> 3.35 us
  starting transfers between devices: 6.27 us -> 32.8 us
  between operations: 13.2 us -> 0.19 us
    reduce_scatter x1 -> x0, waiting for transfers between devices: 284 us -> none  [per_device(): lax.psum_scatter(partial_tile, 'row', scatter_dimension=0, tiled=True)]
    all_gather x2 -> x0, waiting for transfers between devices: 94.5 us -> none  [the longest x1 70 us: per_device(): lax.all_gather(applied_half, 'sec', axis=1, tiled=True)]
    ppermute x2 -> x11, waiting for transfers between devices: 42.3 us -> 116 us  [the longest x1 43.7 us: per_device(): before = lax.ppermute(basis[rows - rim:], 'row', up)]
    pallas_call x0 -> x9, Pallas kernels: none -> 56.4 us  [the longest x8 39.6 us: tile_chunk(): pl.pallas_call(kernel, grid_spec=pltpu.PrefetchScalarGridSpec(num_scalar_...]
    dot_general x8 -> x0, matrix products: 55.2 us -> none  [the longest x7 37.3 us: slot_product(): jnp.einsum('hol,hla->hoa', sparse_block_list, reduced_basis_tiles, prefer...]
    gather x7 -> x0, local copies, waits for them, and re-layouts: 48.6 us -> none  [per_device(): selected_entries = jnp.take(rim_tiles, offset_index[:, neighbour], axis=0)]
    ppermute x2 -> x11, starting transfers between devices: 6.19 us -> 32.8 us  [the longest x3 17.8 us: per_device(): arrived.append(lax.ppermute(part.astype(jnp.bfloat16), 'row', route))]
    concatenate x1 -> x0, other arithmetic: 6.04 us -> none  [padded(): shard = jnp.concatenate([before, shard, after], axis=dim)]
  transfers between devices with their start and end apart: 5 -> 11, of which waited for: 4 -> 6; matrix products, arithmetic and copies ran while one was open for 0% -> 2% of each run, Pallas kernels for 0% -> 24%
where the time goes in v1:
time: 215 us
  waiting for transfers between devices  116 us (54%)
  Pallas kernels  56.4 us (26%)
  starting transfers between devices  32.8 us (15%)
  other arithmetic  6.4 us (3%)
  local copies, waits for them, and re-layouts  3.35 us (2%)
    ppermute x1, waiting for transfers between devices, per_device(): before = lax.ppermute(basis[rows - rim:], 'row', up)  43.7 us
    pallas_call x8, Pallas kernels, tile_chunk(): pl.pallas_call(kernel, grid_spec=pltpu.PrefetchScalarGridSpec(num_scalar_...  39.6 us
    ppermute x4, waiting for transfers between devices, per_device(): sums[step] = lax.ppermute(away, 'row', swap)  39.6 us
    ppermute x3, waiting for transfers between devices, per_device(): arrived.append(lax.ppermute(part.astype(jnp.bfloat16), 'row', route))  32.2 us
    ppermute x3, starting transfers between devices, per_device(): arrived.append(lax.ppermute(part.astype(jnp.bfloat16), 'row', route))  17.8 us
    pallas_call x1, Pallas kernels, apply_operator(): pl.pallas_call(kernel, grid_spec=pltpu.PrefetchScalarGridSpec(num_scalar_...  16.7 us
    ppermute x1, starting transfers between devices, per_device(): moved = lax.ppermute(basis, ('sec', 'col'), [(0, 1), (3, 2)])  4.86 us
    ppermute x4, starting transfers between devices, per_device(): sums[step] = lax.ppermute(away, 'row', swap)  4.57 us
  transfers between devices with their start and end apart: 11, of which 6 were waited for; matrix products, arithmetic and copies ran while one was open for 2% of the time, Pallas kernels for 24%

profile of v1, /device:TPU:0, one launch (start us, length us, event | category | flops | bytes accessed | tf_op | source)
XLA Modules:
  0.0 214.7 jit_solution(3031719145302742687)
XLA Ops:
  0.0 4.9 %collective-permute-start = (bf16[1280,2048]{1,0:T(8,128)(2,1)}, bf16[1280,2048]{1,0:T(8,128)(2,1)}, u32[]{:S(2)}, u32[]{:S(2)}) collective-permute-start(bf16[1280,2048]{1,0:T(8,128)(2,1)} %basis_ref.1), channel_id=1, source_target_pairs={{0,1},{17,16},{2,3},{19,18},{4,5},{21,20},{6,7},{23,22},{8,9},{25,... | collective-permute-start | bytes 15728648 | tf_op jit(solution)/shard_map/ppermute | solution.py:128
  4.9 3.1 %fusion = (bf16[256,2048]{1,0:T(8,128)(2,1)}, bf16[256,2048]{1,0:T(8,128)(2,1)}) fusion(bf16[1280,2048]{1,0:T(8,128)(2,1)} %basis_ref.1), kind=kLoop, calls=%fused_computation.3 | loop fusion | bytes 4194304 | tf_op jit(solution)/shard_map/slice | solution.py:126
  8.0 4.3 %collective-permute-start.1 = (bf16[256,2048]{1,0:T(8,128)(2,1)}, bf16[256,2048]{1,0:T(8,128)(2,1)S(1)}, u32[]{:S(2)}, u32[]{:S(2)}) collective-permute-start(bf16[256,2048]{1,0:T(8,128)(2,1)} %get-tuple-element.6), channel_id=1, source_target_pairs={{0,2},{2,4},{4,6},{6,8},{8,10},{10,12},{12,14},{1,3},{3,5},{5,7},{... | collective-permute-start | bytes 3145736 | tf_op jit(solution)/shard_map/ppermute | solution.py:125
  13.9 43.7 %collective-permute-done.1.before_ref = bf16[256,2048]{1,0:T(8,128)(2,1)S(1)} collective-permute-done((bf16[256,2048]{1,0:T(8,128)(2,1)}, bf16[256,2048]{1,0:T(8,128)(2,1)S(1)}, u32[]{:S(2)}, u32[]{:S(2)}) %collective-permute-start.1) | collective-permute-done | bytes 1048608 | tf_op jit(solution)/shard_map/ppermute | solution.py:125
  57.6 16.7 %apply_operator.1.applied_ref = bf16[1280,2048]{1,0:T(8,128)(2,1)} custom-call(s32[10,7]{1,0:T(8,128)S(1)} %subtract_add_fusion.off_ref, f32[10,7]{1,0:T(8,128)S(1)} %copy.9.w_ref, s32[1]{0:T(128)} %bitcast.1.order_ref, bf16[1280,2048]{1,0:T(8,128)(2,1)} %basis_ref.1, bf16[256,2048]{1,0:T(8,128)(2,1)S(1)} %collective-permute-done.1.before_ref, ...), custom_call_target="tpu_custom_call" | custom-call | flops 4697620480 | bytes 14876672 | tf_op jit(solution)/shard_map/apply_operator/pallas_call | solution.py:49
  74.4 2.9 %broadcast_select_fusion.left_ref = bf16[1280,2048]{1,0:T(8,128)(2,1)} fusion(bf16[1280,2048]{1,0:T(8,128)(2,1)S(1)} %copy-done.1, bf16[1280,2048]{1,0:T(8,128)(2,1)} %collective-permute-done, pred[]{:T(512)S(6)} %eq.13), kind=kLoop, calls=%fused_computation | loop fusion | flops 2621440 | bytes 15728641 | tf_op jit(solution)/shard_map/jit(_where)/select_n | solution.py:129
  77.3 5.4 %tile_chunk.14 = bf16[256,2048]{1,0:T(8,128)(2,1)} custom-call(s32[1]{0:T(128)} %bitcast.8.chunk_ref, bf16[1280,2048]{1,0:T(8,128)(2,1)} %broadcast_select_fusion.left_ref, bf16[1280,2048]{1,0:T(8,128)(2,1)} %apply_operator.1.applied_ref), custom_call_target="tpu_custom_call" | custom-call | flops 1342177280 | bytes 9043968 | tf_op jit(solution)/shard_map/tile_chunk/pallas_call | solution.py:97
  82.7 2.4 %collective-permute-start.9 = (bf16[256,2048]{1,0:T(8,128)(2,1)}, bf16[256,2048]{1,0:T(8,128)(2,1)}, u32[]{:S(2)}, u32[]{:S(2)}) collective-permute-start(bf16[256,2048]{1,0:T(8,128)(2,1)} %tile_chunk.14), channel_id=1, source_target_pairs={{0,2},{2,0},{4,6},{6,4},{8,10},{10,8},{12,14},{14,12},{1,3},{3,1},... | collective-permute-start | bytes 3145736 | tf_op jit(solution)/shard_map/ppermute | solution.py:157
  85.0 4.6 %tile_chunk.12 = bf16[256,2048]{1,0:T(8,128)(2,1)S(1)} custom-call(s32[1]{0:T(128)} %bitcast.6.chunk_ref, bf16[1280,2048]{1,0:T(8,128)(2,1)} %broadcast_select_fusion.left_ref, bf16[1280,2048]{1,0:T(8,128)(2,1)} %apply_operator.1.applied_ref), custom_call_target="tpu_custom_call" | custom-call | flops 1342177280 | bytes 9043968 | tf_op jit(solution)/shard_map/tile_chunk/pallas_call | solution.py:97
  89.7 4.6 %tile_chunk.10 = bf16[256,2048]{1,0:T(8,128)(2,1)S(1)} custom-call(s32[1]{0:T(128)} %bitcast.4.chunk_ref, bf16[1280,2048]{1,0:T(8,128)(2,1)} %broadcast_select_fusion.left_ref, bf16[1280,2048]{1,0:T(8,128)(2,1)} %apply_operator.1.applied_ref), custom_call_target="tpu_custom_call" | custom-call | flops 1342177280 | bytes 9043968 | tf_op jit(solution)/shard_map/tile_chunk/pallas_call | solution.py:97
  96.3 5.4 %tile_chunk.8 = bf16[256,2048]{1,0:T(8,128)(2,1)} custom-call(s32[1]{0:T(128)} %bitcast.2.chunk_ref, bf16[1280,2048]{1,0:T(8,128)(2,1)} %broadcast_select_fusion.left_ref, bf16[1280,2048]{1,0:T(8,128)(2,1)} %apply_operator.1.applied_ref), custom_call_target="tpu_custom_call" | custom-call | flops 1342177280 | bytes 9043968 | tf_op jit(solution)/shard_map/tile_chunk/pallas_call | solution.py:97
  101.8 4.9 %collective-permute-done.9.rest_0_ = bf16[256,2048]{1,0:T(8,128)(2,1)} collective-permute-done((bf16[256,2048]{1,0:T(8,128)(2,1)}, bf16[256,2048]{1,0:T(8,128)(2,1)}, u32[]{:S(2)}, u32[]{:S(2)}) %collective-permute-start.9) | collective-permute-done | bytes 1048608 | tf_op jit(solution)/shard_map/ppermute | solution.py:157
  106.7 5.5 %tile_chunk.15 = bf16[256,2048]{1,0:T(8,128)(2,1)} custom-call(s32[1]{0:T(128)} %bitcast.7.chunk_ref, bf16[1280,2048]{1,0:T(8,128)(2,1)} %broadcast_select_fusion.left_ref, bf16[1280,2048]{1,0:T(8,128)(2,1)} %apply_operator.1.applied_ref, bf16[256,2048]{1,0:T(8,128)(2,1)} %collective-permute-done.9.rest_0_), custom_call_target="tpu_custom_call" | custom-call | flops 1342177280 | bytes 9043968 | tf_op jit(solution)/shard_map/tile_chunk/pallas_call | solution.py:97
  112.3 6.9 %collective-permute-start.10 = (bf16[256,2048]{1,0:T(8,128)(2,1)}, bf16[256,2048]{1,0:T(8,128)(2,1)}, u32[]{:S(2)}, u32[]{:S(2)}) collective-permute-start(bf16[256,2048]{1,0:T(8,128)(2,1)} %tile_chunk.15), channel_id=1, source_target_pairs={{0,12},{2,14},{4,0},{6,2},{8,4},{10,6},{12,8},{14,10},{1,13},{3,15... | collective-permute-start | bytes 3145736 | tf_op jit(solution)/shard_map/ppermute | solution.py:177
  119.2 10.0 %collective-permute-done.7.rest_0_ = bf16[256,2048]{1,0:T(8,128)(2,1)} collective-permute-done((bf16[256,2048]{1,0:T(8,128)(2,1)S(1)}, bf16[256,2048]{1,0:T(8,128)(2,1)}, u32[]{:S(2)}, u32[]{:S(2)}) %collective-permute-start.7) | collective-permute-done | bytes 1048608 | tf_op jit(solution)/shard_map/ppermute | solution.py:157
  129.2 4.7 %tile_chunk.13 = bf16[256,2048]{1,0:T(8,128)(2,1)S(1)} custom-call(s32[1]{0:T(128)} %bitcast.5.chunk_ref, bf16[1280,2048]{1,0:T(8,128)(2,1)} %broadcast_select_fusion.left_ref, bf16[1280,2048]{1,0:T(8,128)(2,1)} %apply_operator.1.applied_ref, bf16[256,2048]{1,0:T(8,128)(2,1)} %collective-permute-done.7.rest_0_), custom_call_target="tpu_custom_call" | custom-call | flops 1342177280 | bytes 9043968 | tf_op jit(solution)/shard_map/tile_chunk/pallas_call | solution.py:97
  134.0 4.9 %collective-permute-start.8 = (bf16[256,2048]{1,0:T(8,128)(2,1)S(1)}, bf16[256,2048]{1,0:T(8,128)(2,1)}, u32[]{:S(2)}, u32[]{:S(2)}) collective-permute-start(bf16[256,2048]{1,0:T(8,128)(2,1)S(1)} %tile_chunk.13), channel_id=1, source_target_pairs={{0,4},{2,6},{4,8},{6,10},{8,12},{10,14},{12,0},{14,2},{1,5},{3,7},... | collective-permute-start | bytes 3145736 | tf_op jit(solution)/shard_map/ppermute | solution.py:177
  138.9 12.7 %collective-permute-done.5.rest_0_ = bf16[256,2048]{1,0:T(8,128)(2,1)S(1)} collective-permute-done((bf16[256,2048]{1,0:T(8,128)(2,1)S(1)}, bf16[256,2048]{1,0:T(8,128)(2,1)S(1)}, u32[]{:S(2)}, u32[]{:S(2)}) %collective-permute-start.5) | collective-permute-done | bytes 1048608 | tf_op jit(solution)/shard_map/ppermute | solution.py:157
  151.6 4.6 %tile_chunk.11 = bf16[256,2048]{1,0:T(8,128)(2,1)S(1)} custom-call(s32[1]{0:T(128)} %bitcast.3.chunk_ref, bf16[1280,2048]{1,0:T(8,128)(2,1)} %broadcast_select_fusion.left_ref, bf16[1280,2048]{1,0:T(8,128)(2,1)} %apply_operator.1.applied_ref, bf16[256,2048]{1,0:T(8,128)(2,1)S(1)} %collective-permute-done.5.rest_0_), custom_call_target="tpu_custom_call" | custom-call | flops 1342177280 | bytes 9043968 | tf_op jit(solution)/shard_map/tile_chunk/pallas_call | solution.py:97
  156.2 6.0 %collective-permute-start.6 = (bf16[256,2048]{1,0:T(8,128)(2,1)S(1)}, bf16[256,2048]{1,0:T(8,128)(2,1)S(1)}, u32[]{:S(2)}, u32[]{:S(2)}) collective-permute-start(bf16[256,2048]{1,0:T(8,128)(2,1)S(1)} %tile_chunk.11), channel_id=1, source_target_pairs={{0,8},{2,10},{4,12},{6,14},{8,0},{10,2},{12,4},{14,6},{1,9},{3,11}... | collective-permute-start | bytes 3145736 | tf_op jit(solution)/shard_map/ppermute | solution.py:177
  162.2 12.0 %collective-permute-done.4.rest_0_ = bf16[256,2048]{1,0:T(8,128)(2,1)} collective-permute-done((bf16[256,2048]{1,0:T(8,128)(2,1)}, bf16[256,2048]{1,0:T(8,128)(2,1)}, u32[]{:S(2)}, u32[]{:S(2)}) %collective-permute-start.4) | collective-permute-done | bytes 1048608 | tf_op jit(solution)/shard_map/ppermute | solution.py:157
  174.2 4.8 %tile_chunk.9 = f32[256,2048]{1,0:T(8,128)S(1)} custom-call(s32[1]{0:T(128)} %bitcast.chunk_ref, bf16[1280,2048]{1,0:T(8,128)(2,1)} %broadcast_select_fusion.left_ref, bf16[1280,2048]{1,0:T(8,128)(2,1)} %apply_operator.1.applied_ref, bf16[256,2048]{1,0:T(8,128)(2,1)} %collective-permute-done.4.rest_0_), custom_call_target="tpu_custom_call" | custom-call | flops 1342177280 | bytes 9043968 | tf_op jit(solution)/shard_map/tile_chunk/pallas_call | solution.py:97
  179.0 32.2 %collective-permute-done.6 = bf16[256,2048]{1,0:T(8,128)(2,1)S(1)} collective-permute-done((bf16[256,2048]{1,0:T(8,128)(2,1)S(1)}, bf16[256,2048]{1,0:T(8,128)(2,1)S(1)}, u32[]{:S(2)}, u32[]{:S(2)}) %collective-permute-start.6) | collective-permute-done | bytes 1048608 | tf_op jit(solution)/shard_map/ppermute | solution.py:177
  211.2 3.5 %add_multiply_fusion = f32[256,2048]{1,0:T(8,128)} fusion(bf16[256,2048]{1,0:T(8,128)(2,1)} %collective-permute-done.10, bf16[256,2048]{1,0:T(8,128)(2,1)} %collective-permute-done.8, f32[256,2048]{1,0:T(8,128)S(1)} %tile_chunk.9, bf16[256,2048]{1,0:T(8,128)(2,1)S(1)} %collective-permute-done.6), kind=kLoop, calls=%fused_computation.1 | loop fusion | flops 3670016 | bytes 7340032 | tf_op jit(solution)/shard_map/mul | solution.py:180
  (22 shorter events, 3.7 us)
Async XLA Ops:
  0.0 57.6 %copy-start = (bf16[10,7,64,128]{3,2,1,0:T(8,128)(2,1)S(1)}, bf16[10,7,64,128]{3,2,1,0:T(8,128)(2,1)}, u32[]{:S(2)}) copy-start(bf16[10,7,64,128]{3,2,1,0:T(8,128)(2,1)} %own_ref.1) | copy-start | bytes 3440644
  0.0 13.7 %copy-start.2 = (s32[10,7]{0,1:T(8,128)S(1)}, s32[10,7]{0,1:T(8,128)}, u32[]{:S(2)}) copy-start(s32[10,7]{0,1:T(8,128)} %param.6) | copy-start | bytes 844
  0.0 13.8 %copy-start.3 = (s32[10,7]{0,1:T(8,128)S(1)}, s32[10,7]{0,1:T(8,128)}, u32[]{:S(2)}) copy-start(s32[10,7]{0,1:T(8,128)} %param.7) | copy-start | bytes 844
  0.0 74.4 %collective-permute-start = (bf16[1280,2048]{1,0:T(8,128)(2,1)}, bf16[1280,2048]{1,0:T(8,128)(2,1)}, u32[]{:S(2)}, u32[]{:S(2)}) collective-permute-start(bf16[1280,2048]{1,0:T(8,128)(2,1)} %basis_ref.1), channel_id=1, source_target_pairs={{0,1},{17,16},{2,3},{19,18},{4,5},{21,20},{6,7},{23,22},{8,9},{25,... | collective-permute-start | bytes 15728648 | tf_op jit(solution)/shard_map/ppermute | solution.py:128
  4.9 52.8 %collective-permute-start.3 = (bf16[10,7,64,128]{3,2,1,0:T(8,128)(2,1)}, bf16[10,7,64,128]{3,2,1,0:T(8,128)(2,1)S(1)}, u32[]{:S(2)}, u32[]{:S(2)}) collective-permute-start(bf16[10,7,64,128]{3,2,1,0:T(8,128)(2,1)} %own_ref.1), channel_id=1, source_target_pairs={{0,16},{16,0},{1,17},{17,1},{2,18},{18,2},{3,19},{19,3},{4,20},{20... | collective-permute-start | bytes 3440648 | tf_op jit(solution)/shard_map/ppermute | solution.py:127
  8.0 49.6 %collective-permute-start.1 = (bf16[256,2048]{1,0:T(8,128)(2,1)}, bf16[256,2048]{1,0:T(8,128)(2,1)S(1)}, u32[]{:S(2)}, u32[]{:S(2)}) collective-permute-start(bf16[256,2048]{1,0:T(8,128)(2,1)} %get-tuple-element.6), channel_id=1, source_target_pairs={{0,2},{2,4},{4,6},{6,8},{8,10},{10,12},{12,14},{1,3},{3,5},{5,7},{... | collective-permute-start | bytes 3145736 | tf_op jit(solution)/shard_map/ppermute | solution.py:125
  12.3 45.3 %collective-permute-start.2 = (bf16[256,2048]{1,0:T(8,128)(2,1)}, bf16[256,2048]{1,0:T(8,128)(2,1)}, u32[]{:S(2)}, u32[]{:S(2)}) collective-permute-start(bf16[256,2048]{1,0:T(8,128)(2,1)} %get-tuple-element.5), channel_id=1, source_target_pairs={{2,0},{4,2},{6,4},{8,6},{10,8},{12,10},{14,12},{3,1},{5,3},{7,5},{... | collective-permute-start | bytes 3145736 | tf_op jit(solution)/shard_map/ppermute | solution.py:126
  57.6 16.7 %copy-start.1 = (bf16[1280,2048]{1,0:T(8,128)(2,1)S(1)}, bf16[1280,2048]{1,0:T(8,128)(2,1)}, u32[]{:S(2)}) copy-start(bf16[1280,2048]{1,0:T(8,128)(2,1)} %basis_ref.1) | copy-start | bytes 15728644
  82.7 24.1 %collective-permute-start.9 = (bf16[256,2048]{1,0:T(8,128)(2,1)}, bf16[256,2048]{1,0:T(8,128)(2,1)}, u32[]{:S(2)}, u32[]{:S(2)}) collective-permute-start(bf16[256,2048]{1,0:T(8,128)(2,1)} %tile_chunk.14), channel_id=1, source_target_pairs={{0,2},{2,0},{4,6},{6,4},{8,10},{10,8},{12,14},{14,12},{1,3},{3,1},... | collective-permute-start | bytes 3145736 | tf_op jit(solution)/shard_map/ppermute | solution.py:157
  89.6 39.6 %collective-permute-start.7 = (bf16[256,2048]{1,0:T(8,128)(2,1)S(1)}, bf16[256,2048]{1,0:T(8,128)(2,1)}, u32[]{:S(2)}, u32[]{:S(2)}) collective-permute-start(bf16[256,2048]{1,0:T(8,128)(2,1)S(1)} %tile_chunk.12), channel_id=1, source_target_pairs={{0,2},{2,0},{4,6},{6,4},{8,10},{10,8},{12,14},{14,12},{1,3},{3,1},... | collective-permute-start | bytes 3145736 | tf_op jit(solution)/shard_map/ppermute | solution.py:157
  94.3 57.3 %collective-permute-start.5 = (bf16[256,2048]{1,0:T(8,128)(2,1)S(1)}, bf16[256,2048]{1,0:T(8,128)(2,1)S(1)}, u32[]{:S(2)}, u32[]{:S(2)}) collective-permute-start(bf16[256,2048]{1,0:T(8,128)(2,1)S(1)} %tile_chunk.10), channel_id=1, source_target_pairs={{0,2},{2,0},{4,6},{6,4},{8,10},{10,8},{12,14},{14,12},{1,3},{3,1},... | collective-permute-start | bytes 3145736 | tf_op jit(solution)/shard_map/ppermute | solution.py:157
  101.8 72.4 %collective-permute-start.4 = (bf16[256,2048]{1,0:T(8,128)(2,1)}, bf16[256,2048]{1,0:T(8,128)(2,1)}, u32[]{:S(2)}, u32[]{:S(2)}) collective-permute-start(bf16[256,2048]{1,0:T(8,128)(2,1)} %tile_chunk.8), channel_id=1, source_target_pairs={{0,2},{2,0},{4,6},{6,4},{8,10},{10,8},{12,14},{14,12},{1,3},{3,1},... | collective-permute-start | bytes 3145736 | tf_op jit(solution)/shard_map/ppermute | solution.py:157
  112.3 66.7 %collective-permute-start.10 = (bf16[256,2048]{1,0:T(8,128)(2,1)}, bf16[256,2048]{1,0:T(8,128)(2,1)}, u32[]{:S(2)}, u32[]{:S(2)}) collective-permute-start(bf16[256,2048]{1,0:T(8,128)(2,1)} %tile_chunk.15), channel_id=1, source_target_pairs={{0,12},{2,14},{4,0},{6,2},{8,4},{10,6},{12,8},{14,10},{1,13},{3,15... | collective-permute-start | bytes 3145736 | tf_op jit(solution)/shard_map/ppermute | solution.py:177
  134.0 45.0 %collective-permute-start.8 = (bf16[256,2048]{1,0:T(8,128)(2,1)S(1)}, bf16[256,2048]{1,0:T(8,128)(2,1)}, u32[]{:S(2)}, u32[]{:S(2)}) collective-permute-start(bf16[256,2048]{1,0:T(8,128)(2,1)S(1)} %tile_chunk.13), channel_id=1, source_target_pairs={{0,4},{2,6},{4,8},{6,10},{8,12},{10,14},{12,0},{14,2},{1,5},{3,7},... | collective-permute-start | bytes 3145736 | tf_op jit(solution)/shard_map/ppermute | solution.py:177
  156.2 55.0 %collective-permute-start.6 = (bf16[256,2048]{1,0:T(8,128)(2,1)S(1)}, bf16[256,2048]{1,0:T(8,128)(2,1)S(1)}, u32[]{:S(2)}, u32[]{:S(2)}) collective-permute-start(bf16[256,2048]{1,0:T(8,128)(2,1)S(1)} %tile_chunk.11), channel_id=1, source_target_pairs={{0,8},{2,10},{4,12},{6,14},{8,0},{10,2},{12,4},{14,6},{1,9},{3,11}... | collective-permute-start | bytes 3145736 | tf_op jit(solution)/shard_map/ppermute | solution.py:177

commit v2 on v1

--- a/solution.py
+++ b/solution.py
@@ -134,49 +134,47 @@
         mask.astype(jnp.float32), sec.astype(jnp.int32)[None],
     )
 
-    groups = count // 2
-    group, side = row // 2, row % 2
     height = width * lax.axis_size("col") // lax.axis_size("sec") // count
-    pack = min(groups, max(1, 256 // height))
-    packs = groups // pack
-    if pack > 1:
-        left = left.reshape(rows, groups, 2, height).swapaxes(1, 2).reshape(rows, -1)
+    fars = count // 4
+    far, pair, side = row // 4, row // 2 % 2, row % 2
+    swap_side = [(i, i ^ 1) for i in range(count)]
+    swap_pair = [(i, i ^ 2) for i in range(count)]
 
-    def column_block(step, which):
-        target = (group // pack + step) % packs
-        return (2 * target + which if pack == 1 else which * packs + target)[None]
+    def block(steps, pair, side, dtype):
+        where = [((far + step) % fars * 2 + pair) * 2 + side for step in steps]
+        if len(steps) == 1 and height % 128 == 0:
+            return tile_chunk(left, applied, where[0][None], height, None, dtype)
+        columns = [lax.dynamic_slice_in_dim(left, w * height, height, 1) for w in where]
+        wide = -len(steps) * height % 128
+        if wide:
+            columns.append(jnp.zeros((rows, wide), left.dtype))
+        made = tile_chunk(
+            jnp.concatenate(columns, 1), applied, jnp.zeros((1,), jnp.int32),
+            len(steps) * height + wide, None, dtype,
+        )
+        return made[: len(steps) * height]
 
-    swap = [(i, i ^ 1) for i in range(count)]
-    steps = sorted(range(1, packs), key=lambda k: -min(k, packs - k)) + [0]
+    def add(first, *others):
+        for other in others:
+            first = first + other.astype(jnp.float32)
+        return first
 
-    sums = {}
-    for step in steps:
-        away = tile_chunk(
-            left, applied, column_block(step, 1 - side), pack * height, None, jnp.bfloat16
-        )
-        sums[step] = lax.ppermute(away, "row", swap)
-    total = None
-    arrived = []
-    for step in steps:
-        mine = tile_chunk(
-            left, applied, column_block(step, side), pack * height, sums[step],
-            jnp.float32 if step == 0 else jnp.bfloat16,
-        )
-        for i in range(pack):
-            part = mine
-            if pack > 1:
-                place = (group + i) % pack * height
-                part = lax.dynamic_slice_in_dim(mine, place, height, axis=0)
-            if step == 0 and i == 0:
-                total = part
-                continue
-            route = []
-            for g in range(groups):
-                to = (g // pack + step) % packs * pack + (g + i) % pack
-                route += [(2 * g, 2 * to), (2 * g + 1, 2 * to + 1)]
-            arrived.append(lax.ppermute(part.astype(jnp.bfloat16), "row", route))
-    for part in arrived:
-        total = total + part.astype(jnp.float32)
+    away = list(range(1, fars))
+    f32, bf16 = jnp.float32, jnp.bfloat16
+    far_a = lax.ppermute(block(away, 1 - pair, 1 - side, bf16), "row", swap_side)
+    near_a = lax.ppermute(block([0], 1 - pair, 1 - side, bf16), "row", swap_pair)
+    far_b = lax.ppermute(block(away, pair, 1 - side, bf16), "row", swap_side)
+    far_c = add(block(away, 1 - pair, side, f32), far_a).astype(bf16)
+    far_c = lax.ppermute(far_c, "row", swap_pair)
+    near_b = lax.ppermute(block([0], 1 - pair, side, bf16), "row", swap_pair)
+    near_c = add(block([0], pair, 1 - side, f32), near_a).astype(bf16)
+    near_c = lax.ppermute(near_c, "row", swap_side)
+    far_d = add(block(away, pair, side, f32), far_b, far_c).astype(bf16)
+    parts = []
+    for i, step in enumerate(away):
+        route = [(g, (g + 4 * step) % count) for g in range(count)]
+        parts.append(lax.ppermute(far_d[i * height : (i + 1) * height], "row", route))
+    total = add(block([0], pair, side, f32), near_b, near_c, *parts)
     return total * (1.0 / math.sqrt(rows * count))
 
 

time: 215 us -> 195 us (0.907)
  the two profiles are of different devices: /device:TPU:0 before, /device:TPU:6 now
where the time goes in v2:
time: 195 us; the launch traced here: 194 us
  waiting for transfers between devices  102 us (52%)
  Pallas kernels  53.6 us (27%)
  starting transfers between devices  19 us (10%)
  other arithmetic  16 us (8%)
  local copies, waits for them, and re-layouts  3.35 us (2%)
    ppermute x1, waiting for transfers between devices, per_device(): before = lax.ppermute(basis[rows - rim:], 'row', up)  43.6 us
    pallas_call x8, Pallas kernels, tile_chunk(): pl.pallas_call(kernel, grid_spec=pltpu.PrefetchScalarGridSpec(num_scalar_...  36.9 us
    ppermute x1, waiting for transfers between devices, per_device(): far_c = lax.ppermute(far_c, 'row', swap_pair)  18 us
    ppermute x1, waiting for transfers between devices, per_device(): parts.append(lax.ppermute(far_d[i * height:(i + 1) * height], 'row', route))  18 us
    pallas_call x1, Pallas kernels, apply_operator(): pl.pallas_call(kernel, grid_spec=pltpu.PrefetchScalarGridSpec(num_scalar_...  16.7 us
    ppermute x1, waiting for transfers between devices, per_device(): near_b = lax.ppermute(block([0], 1 - pair, side, bf16), 'row', swap_pair)  13.4 us
    ppermute x1, waiting for transfers between devices, per_device(): lax.ppermute(block(away, 1 - pair, 1 - side, bf16), 'row', swap_side)  8.64 us
    select_n x1, other arithmetic, per_device(): left = jnp.where(sec == col, basis, moved)  5.38 us
  transfers between devices with their start and end apart: 11, of which 5 were waited for; matrix products, arithmetic and copies ran while one was open for 5% of the time, Pallas kernels for 25%

profile of v2, /device:TPU:6, one launch (start us, length us, event | category | flops | bytes accessed | tf_op | source)
XLA Modules:
  0.0 193.9 jit_solution(9124427440203252479)
XLA Ops:
  1.4 3.3 %collective-permute-start.3 = (bf16[10,7,64,128]{3,2,1,0:T(8,128)(2,1)}, bf16[10,7,64,128]{3,2,1,0:T(8,128)(2,1)S(1)}, u32[]{:S(2)}, u32[]{:S(2)}) collective-permute-start(bf16[10,7,64,128]{3,2,1,0:T(8,128)(2,1)} %own_ref.1), channel_id=1, source_target_pairs={{0,16},{16,0},{1,17},{17,1},{2,18},{18,2},{3,19},{19,3},{4,20},{20... | collective-permute-start | bytes 3440648 | tf_op jit(solution)/shard_map/ppermute | solution.py:127
  4.8 3.1 %fusion = (bf16[256,2048]{1,0:T(8,128)(2,1)}, bf16[256,2048]{1,0:T(8,128)(2,1)}) fusion(bf16[1280,2048]{1,0:T(8,128)(2,1)} %basis_ref.1), kind=kLoop, calls=%fused_computation.6 | loop fusion | bytes 4194304 | tf_op jit(solution)/shard_map/slice | solution.py:126
  7.9 3.4 %collective-permute-start.1 = (bf16[256,2048]{1,0:T(8,128)(2,1)}, bf16[256,2048]{1,0:T(8,128)(2,1)S(1)}, u32[]{:S(2)}, u32[]{:S(2)}) collective-permute-start(bf16[256,2048]{1,0:T(8,128)(2,1)} %get-tuple-element.6), channel_id=1, source_target_pairs={{0,2},{2,4},{4,6},{6,8},{8,10},{10,12},{12,14},{1,3},{3,5},{5,7},{... | collective-permute-start | bytes 3145736 | tf_op jit(solution)/shard_map/ppermute | solution.py:125
  11.3 2.5 %collective-permute-start.2 = (bf16[256,2048]{1,0:T(8,128)(2,1)}, bf16[256,2048]{1,0:T(8,128)(2,1)}, u32[]{:S(2)}, u32[]{:S(2)}) collective-permute-start(bf16[256,2048]{1,0:T(8,128)(2,1)} %get-tuple-element.5), channel_id=1, source_target_pairs={{2,0},{4,2},{6,4},{8,6},{10,8},{12,10},{14,12},{3,1},{5,3},{7,5},{... | collective-permute-start | bytes 3145736 | tf_op jit(solution)/shard_map/ppermute | solution.py:126
  14.1 43.6 %collective-permute-done.1.before_ref = bf16[256,2048]{1,0:T(8,128)(2,1)S(1)} collective-permute-done((bf16[256,2048]{1,0:T(8,128)(2,1)}, bf16[256,2048]{1,0:T(8,128)(2,1)S(1)}, u32[]{:S(2)}, u32[]{:S(2)}) %collective-permute-start.1) | collective-permute-done | bytes 1048608 | tf_op jit(solution)/shard_map/ppermute | solution.py:125
  57.7 16.7 %apply_operator.1.applied_ref = bf16[1280,2048]{1,0:T(8,128)(2,1)} custom-call(s32[10,7]{1,0:T(8,128)S(1)} %subtract_add_fusion.off_ref, f32[10,7]{1,0:T(8,128)S(1)} %copy.9.w_ref, s32[1]{0:T(128)} %bitcast.1.order_ref, bf16[1280,2048]{1,0:T(8,128)(2,1)} %basis_ref.1, bf16[256,2048]{1,0:T(8,128)(2,1)S(1)} %collective-permute-done.1.before_ref, ...), custom_call_target="tpu_custom_call" | custom-call | flops 4697620480 | bytes 14876672 | tf_op jit(solution)/shard_map/apply_operator/pallas_call | solution.py:49
  74.5 5.4 %broadcast_select_fusion.left_ref = bf16[1280,2048]{1,0:T(8,128)(2,1)} fusion(bf16[1280,2048]{1,0:T(8,128)(2,1)S(1)} %copy-done.1, bf16[1280,2048]{1,0:T(8,128)(2,1)} %collective-permute-done, pred[]{:T(512)S(6)} %eq.14), kind=kLoop, calls=%fused_computation | loop fusion | flops 2621440 | bytes 15728641 | tf_op jit(solution)/shard_map/jit(_where)/select_n | solution.py:129
  79.8 4.6 %tile_chunk.15 = bf16[256,2048]{1,0:T(8,128)(2,1)S(1)} custom-call(s32[1]{0:T(128)} %bitcast.8.chunk_ref, bf16[1280,2048]{1,0:T(8,128)(2,1)} %broadcast_select_fusion.left_ref, bf16[1280,2048]{1,0:T(8,128)(2,1)} %apply_operator.1.applied_ref), custom_call_target="tpu_custom_call" | custom-call | flops 1342177280 | bytes 9043968 | tf_op jit(solution)/shard_map/tile_chunk/pallas_call | solution.py:97
  84.5 4.6 %tile_chunk.11 = bf16[256,2048]{1,0:T(8,128)(2,1)S(1)} custom-call(s32[1]{0:T(128)} %bitcast.4.chunk_ref, bf16[1280,2048]{1,0:T(8,128)(2,1)} %broadcast_select_fusion.left_ref, bf16[1280,2048]{1,0:T(8,128)(2,1)} %apply_operator.1.applied_ref), custom_call_target="tpu_custom_call" | custom-call | flops 1342177280 | bytes 9043968 | tf_op jit(solution)/shard_map/tile_chunk/pallas_call | solution.py:97
  89.1 3.1 %collective-permute-start.5 = (bf16[256,2048]{1,0:T(8,128)(2,1)S(1)}, bf16[256,2048]{1,0:T(8,128)(2,1)}, u32[]{:S(2)}, u32[]{:S(2)}) collective-permute-start(bf16[256,2048]{1,0:T(8,128)(2,1)S(1)} %tile_chunk.11), channel_id=1, source_target_pairs={{0,4},{2,6},{4,0},{6,2},{8,12},{10,14},{12,8},{14,10},{1,5},{3,7},... | collective-permute-start | bytes 3145736 | tf_op jit(solution)/shard_map/ppermute | solution.py:165
  92.2 4.7 %tile_chunk.14 = f32[256,2048]{1,0:T(8,128)S(1)} custom-call(s32[1]{0:T(128)} %bitcast.7.chunk_ref, bf16[1280,2048]{1,0:T(8,128)(2,1)} %broadcast_select_fusion.left_ref, bf16[1280,2048]{1,0:T(8,128)(2,1)} %apply_operator.1.applied_ref), custom_call_target="tpu_custom_call" | custom-call | flops 1342177280 | bytes 9043968 | tf_op jit(solution)/shard_map/tile_chunk/pallas_call | solution.py:97
  96.9 4.6 %tile_chunk.13 = bf16[256,2048]{1,0:T(8,128)(2,1)S(1)} custom-call(s32[1]{0:T(128)} %bitcast.6.chunk_ref, bf16[1280,2048]{1,0:T(8,128)(2,1)} %broadcast_select_fusion.left_ref, bf16[1280,2048]{1,0:T(8,128)(2,1)} %apply_operator.1.applied_ref), custom_call_target="tpu_custom_call" | custom-call | flops 1342177280 | bytes 9043968 | tf_op jit(solution)/shard_map/tile_chunk/pallas_call | solution.py:97
  102.0 8.6 %collective-permute-done.8 = bf16[256,2048]{1,0:T(8,128)(2,1)} collective-permute-done((bf16[256,2048]{1,0:T(8,128)(2,1)S(1)}, bf16[256,2048]{1,0:T(8,128)(2,1)}, u32[]{:S(2)}, u32[]{:S(2)}) %collective-permute-start.8) | collective-permute-done | bytes 1048608 | tf_op jit(solution)/shard_map/ppermute | solution.py:164
  110.7 2.5 %add_convert_fusion.1 = bf16[256,2048]{1,0:T(8,128)(2,1)} fusion(f32[256,2048]{1,0:T(8,128)S(1)} %tile_chunk.14, bf16[256,2048]{1,0:T(8,128)(2,1)} %collective-permute-done.8), kind=kLoop, calls=%fused_computation.3 | loop fusion | flops 1572864 | bytes 4194304 | tf_op jit(solution)/shard_map/convert_element_type | solution.py:167
  114.8 4.6 %tile_chunk.9 = bf16[256,2048]{1,0:T(8,128)(2,1)S(1)} custom-call(s32[1]{0:T(128)} %bitcast.2.chunk_ref, bf16[1280,2048]{1,0:T(8,128)(2,1)} %broadcast_select_fusion.left_ref, bf16[1280,2048]{1,0:T(8,128)(2,1)} %apply_operator.1.applied_ref), custom_call_target="tpu_custom_call" | custom-call | flops 1342177280 | bytes 9043968 | tf_op jit(solution)/shard_map/tile_chunk/pallas_call | solution.py:97
  119.9 4.6 %tile_chunk.12 = f32[256,2048]{1,0:T(8,128)S(1)} custom-call(s32[1]{0:T(128)} %bitcast.5.chunk_ref, bf16[1280,2048]{1,0:T(8,128)(2,1)} %broadcast_select_fusion.left_ref, bf16[1280,2048]{1,0:T(8,128)(2,1)} %apply_operator.1.applied_ref), custom_call_target="tpu_custom_call" | custom-call | flops 1342177280 | bytes 9043968 | tf_op jit(solution)/shard_map/tile_chunk/pallas_call | solution.py:97
  124.5 4.7 %tile_chunk.10 = f32[256,2048]{1,0:T(8,128)S(1)} custom-call(s32[1]{0:T(128)} %bitcast.3.chunk_ref, bf16[1280,2048]{1,0:T(8,128)(2,1)} %broadcast_select_fusion.left_ref, bf16[1280,2048]{1,0:T(8,128)(2,1)} %apply_operator.1.applied_ref), custom_call_target="tpu_custom_call" | custom-call | flops 1342177280 | bytes 9043968 | tf_op jit(solution)/shard_map/tile_chunk/pallas_call | solution.py:97
  129.2 2.5 %add_convert_fusion.2 = bf16[256,2048]{1,0:T(8,128)(2,1)} fusion(f32[256,2048]{1,0:T(8,128)S(1)} %tile_chunk.10, bf16[256,2048]{1,0:T(8,128)(2,1)} %collective-permute-done.5), kind=kLoop, calls=%fused_computation.4 | loop fusion | flops 1572864 | bytes 4194304 | tf_op jit(solution)/shard_map/convert_element_type | solution.py:170
  132.9 18.0 %collective-permute-done.9 = bf16[256,2048]{1,0:T(8,128)(2,1)} collective-permute-done((bf16[256,2048]{1,0:T(8,128)(2,1)}, bf16[256,2048]{1,0:T(8,128)(2,1)}, u32[]{:S(2)}, u32[]{:S(2)}) %collective-permute-start.9) | collective-permute-done | bytes 1048608 | tf_op jit(solution)/shard_map/ppermute | solution.py:168
  150.8 2.1 %add_convert_fusion = bf16[256,2048]{1,0:T(8,128)(2,1)S(1)} fusion(bf16[256,2048]{1,0:T(8,128)(2,1)} %collective-permute-done.9, f32[256,2048]{1,0:T(8,128)S(1)} %tile_chunk.12, bf16[256,2048]{1,0:T(8,128)(2,1)} %collective-permute-done.7), kind=kLoop, calls=%fused_computation.2 | loop fusion | flops 2621440 | bytes 5242880 | tf_op jit(solution)/shard_map/convert_element_type | solution.py:172
  154.4 4.6 %tile_chunk.8 = f32[256,2048]{1,0:T(8,128)S(1)} custom-call(s32[1]{0:T(128)} %bitcast.chunk_ref, bf16[1280,2048]{1,0:T(8,128)(2,1)} %broadcast_select_fusion.left_ref, bf16[1280,2048]{1,0:T(8,128)(2,1)} %apply_operator.1.applied_ref), custom_call_target="tpu_custom_call" | custom-call | flops 1342177280 | bytes 9043968 | tf_op jit(solution)/shard_map/tile_chunk/pallas_call | solution.py:97
  159.0 13.4 %collective-permute-done.4 = bf16[256,2048]{1,0:T(8,128)(2,1)} collective-permute-done((bf16[256,2048]{1,0:T(8,128)(2,1)S(1)}, bf16[256,2048]{1,0:T(8,128)(2,1)}, u32[]{:S(2)}, u32[]{:S(2)}) %collective-permute-start.4) | collective-permute-done | bytes 1048608 | tf_op jit(solution)/shard_map/ppermute | solution.py:169
  172.5 18.0 %collective-permute-done.10 = bf16[256,2048]{1,0:T(8,128)(2,1)} collective-permute-done((bf16[256,2048]{1,0:T(8,128)(2,1)S(1)}, bf16[256,2048]{1,0:T(8,128)(2,1)}, u32[]{:S(2)}, u32[]{:S(2)}) %collective-permute-start.10) | collective-permute-done | bytes 1048608 | tf_op jit(solution)/shard_map/ppermute | solution.py:176
  190.4 3.5 %add_multiply_fusion = f32[256,2048]{1,0:T(8,128)} fusion(bf16[256,2048]{1,0:T(8,128)(2,1)} %collective-permute-done.10, bf16[256,2048]{1,0:T(8,128)(2,1)S(1)} %collective-permute-done.6, f32[256,2048]{1,0:T(8,128)S(1)} %tile_chunk.8, bf16[256,2048]{1,0:T(8,128)(2,1)} %collective-permute-done.4), kind=kLoop, calls=%fused_computation.1 | loop fusion | flops 3670016 | bytes 7340032 | tf_op jit(solution)/shard_map/mul | solution.py:178
  (25 shorter events, 6.9 us)
Async XLA Ops:
  0.0 57.7 %copy-start = (bf16[10,7,64,128]{3,2,1,0:T(8,128)(2,1)S(1)}, bf16[10,7,64,128]{3,2,1,0:T(8,128)(2,1)}, u32[]{:S(2)}) copy-start(bf16[10,7,64,128]{3,2,1,0:T(8,128)(2,1)} %own_ref.1) | copy-start | bytes 3440644
  0.0 13.9 %copy-start.2 = (s32[10,7]{0,1:T(8,128)S(1)}, s32[10,7]{0,1:T(8,128)}, u32[]{:S(2)}) copy-start(s32[10,7]{0,1:T(8,128)} %param.6) | copy-start | bytes 844
  0.0 14.0 %copy-start.3 = (s32[10,7]{0,1:T(8,128)S(1)}, s32[10,7]{0,1:T(8,128)}, u32[]{:S(2)}) copy-start(s32[10,7]{0,1:T(8,128)} %param.7) | copy-start | bytes 844
  0.0 74.4 %collective-permute-start = (bf16[1280,2048]{1,0:T(8,128)(2,1)}, bf16[1280,2048]{1,0:T(8,128)(2,1)}, u32[]{:S(2)}, u32[]{:S(2)}) collective-permute-start(bf16[1280,2048]{1,0:T(8,128)(2,1)} %basis_ref.1), channel_id=1, source_target_pairs={{0,1},{17,16},{2,3},{19,18},{4,5},{21,20},{6,7},{23,22},{8,9},{25,... | collective-permute-start | bytes 15728648 | tf_op jit(solution)/shard_map/ppermute | solution.py:128
  1.4 56.3 %collective-permute-start.3 = (bf16[10,7,64,128]{3,2,1,0:T(8,128)(2,1)}, bf16[10,7,64,128]{3,2,1,0:T(8,128)(2,1)S(1)}, u32[]{:S(2)}, u32[]{:S(2)}) collective-permute-start(bf16[10,7,64,128]{3,2,1,0:T(8,128)(2,1)} %own_ref.1), channel_id=1, source_target_pairs={{0,16},{16,0},{1,17},{17,1},{2,18},{18,2},{3,19},{19,3},{4,20},{20... | collective-permute-start | bytes 3440648 | tf_op jit(solution)/shard_map/ppermute | solution.py:127
  7.9 49.8 %collective-permute-start.1 = (bf16[256,2048]{1,0:T(8,128)(2,1)}, bf16[256,2048]{1,0:T(8,128)(2,1)S(1)}, u32[]{:S(2)}, u32[]{:S(2)}) collective-permute-start(bf16[256,2048]{1,0:T(8,128)(2,1)} %get-tuple-element.6), channel_id=1, source_target_pairs={{0,2},{2,4},{4,6},{6,8},{8,10},{10,12},{12,14},{1,3},{3,5},{5,7},{... | collective-permute-start | bytes 3145736 | tf_op jit(solution)/shard_map/ppermute | solution.py:125
  11.3 46.4 %collective-permute-start.2 = (bf16[256,2048]{1,0:T(8,128)(2,1)}, bf16[256,2048]{1,0:T(8,128)(2,1)}, u32[]{:S(2)}, u32[]{:S(2)}) collective-permute-start(bf16[256,2048]{1,0:T(8,128)(2,1)} %get-tuple-element.5), channel_id=1, source_target_pairs={{2,0},{4,2},{6,4},{8,6},{10,8},{12,10},{14,12},{3,1},{5,3},{7,5},{... | collective-permute-start | bytes 3145736 | tf_op jit(solution)/shard_map/ppermute | solution.py:126
  57.7 16.7 %copy-start.1 = (bf16[1280,2048]{1,0:T(8,128)(2,1)S(1)}, bf16[1280,2048]{1,0:T(8,128)(2,1)}, u32[]{:S(2)}) copy-start(bf16[1280,2048]{1,0:T(8,128)(2,1)} %basis_ref.1) | copy-start | bytes 15728644
  84.4 26.3 %collective-permute-start.8 = (bf16[256,2048]{1,0:T(8,128)(2,1)S(1)}, bf16[256,2048]{1,0:T(8,128)(2,1)}, u32[]{:S(2)}, u32[]{:S(2)}) collective-permute-start(bf16[256,2048]{1,0:T(8,128)(2,1)S(1)} %tile_chunk.15), channel_id=1, source_target_pairs={{0,2},{2,0},{4,6},{6,4},{8,10},{10,8},{12,14},{14,12},{1,3},{3,1},... | collective-permute-start | bytes 3145736 | tf_op jit(solution)/shard_map/ppermute | solution.py:164
  89.1 40.1 %collective-permute-start.5 = (bf16[256,2048]{1,0:T(8,128)(2,1)S(1)}, bf16[256,2048]{1,0:T(8,128)(2,1)}, u32[]{:S(2)}, u32[]{:S(2)}) collective-permute-start(bf16[256,2048]{1,0:T(8,128)(2,1)S(1)} %tile_chunk.11), channel_id=1, source_target_pairs={{0,4},{2,6},{4,0},{6,2},{8,12},{10,14},{12,8},{14,10},{1,5},{3,7},... | collective-permute-start | bytes 3145736 | tf_op jit(solution)/shard_map/ppermute | solution.py:165
  101.5 31.4 %collective-permute-start.7 = (bf16[256,2048]{1,0:T(8,128)(2,1)S(1)}, bf16[256,2048]{1,0:T(8,128)(2,1)}, u32[]{:S(2)}, u32[]{:S(2)}) collective-permute-start(bf16[256,2048]{1,0:T(8,128)(2,1)S(1)} %tile_chunk.13), channel_id=1, source_target_pairs={{0,2},{2,0},{4,6},{6,4},{8,10},{10,8},{12,14},{14,12},{1,3},{3,1},... | collective-permute-start | bytes 3145736 | tf_op jit(solution)/shard_map/ppermute | solution.py:166
  113.2 37.6 %collective-permute-start.9 = (bf16[256,2048]{1,0:T(8,128)(2,1)}, bf16[256,2048]{1,0:T(8,128)(2,1)}, u32[]{:S(2)}, u32[]{:S(2)}) collective-permute-start(bf16[256,2048]{1,0:T(8,128)(2,1)} %add_convert_fusion.1), channel_id=1, source_target_pairs={{0,4},{2,6},{4,0},{6,2},{8,12},{10,14},{12,8},{14,10},{1,5},{3,7},... | collective-permute-start | bytes 3145736 | tf_op jit(solution)/shard_map/ppermute | solution.py:168
  119.4 53.1 %collective-permute-start.4 = (bf16[256,2048]{1,0:T(8,128)(2,1)S(1)}, bf16[256,2048]{1,0:T(8,128)(2,1)}, u32[]{:S(2)}, u32[]{:S(2)}) collective-permute-start(bf16[256,2048]{1,0:T(8,128)(2,1)S(1)} %tile_chunk.9), channel_id=1, source_target_pairs={{0,4},{2,6},{4,0},{6,2},{8,12},{10,14},{12,8},{14,10},{1,5},{3,7},... | collective-permute-start | bytes 3145736 | tf_op jit(solution)/shard_map/ppermute | solution.py:169
  131.7 40.7 %collective-permute-start.6 = (bf16[256,2048]{1,0:T(8,128)(2,1)}, bf16[256,2048]{1,0:T(8,128)(2,1)S(1)}, u32[]{:S(2)}, u32[]{:S(2)}) collective-permute-start(bf16[256,2048]{1,0:T(8,128)(2,1)} %add_convert_fusion.2), channel_id=1, source_target_pairs={{0,2},{2,0},{4,6},{6,4},{8,10},{10,8},{12,14},{14,12},{1,3},{3,1},... | collective-permute-start | bytes 3145736 | tf_op jit(solution)/shard_map/ppermute | solution.py:171
  152.9 37.5 %collective-permute-start.10 = (bf16[256,2048]{1,0:T(8,128)(2,1)S(1)}, bf16[256,2048]{1,0:T(8,128)(2,1)}, u32[]{:S(2)}, u32[]{:S(2)}) collective-permute-start(bf16[256,2048]{1,0:T(8,128)(2,1)S(1)} %add_convert_fusion), channel_id=1, source_target_pairs={{0,8},{2,10},{4,12},{6,14},{8,0},{10,2},{12,4},{14,6},{1,9},{3,11}... | collective-permute-start | bytes 3145736 | tf_op jit(solution)/shard_map/ppermute | solution.py:176

commit v3 on v0

v3 whole, which is shorter than its diff:
```python
import math

import jax
import jax.numpy as jnp
from jax import lax
from jax.experimental import pallas as pl
from jax.experimental.pallas import tpu as pltpu
from jax.sharding import PartitionSpec as P

REACH = 2
BACK = (1, 3, 5, 6)
VMEM_LIMIT = 48 * 1024 * 1024
F32, BF16 = jnp.float32, jnp.bfloat16


def call(kernel, scalars, grid, in_specs, operands, out_spec, out_shape, scratch, flops, name):
    moved = sum(x.size * x.dtype.itemsize for x in operands)
    return pl.pallas_call(
        kernel,
        grid_spec=pltpu.PrefetchScalarGridSpec(
            num_scalar_prefetch=len(scalars), grid=grid, in_specs=in_specs,
            out_specs=out_spec, scratch_shapes=scratch,
        ),
        out_shape=out_shape,
        compiler_params=pltpu.CompilerParams(vmem_limit_bytes=VMEM_LIMIT),
        cost_estimate=pl.CostEstimate(flops=flops, bytes_accessed=moved, transcendentals=0),
        name=name,
    )(*scalars, *operands)


def apply_block(picks, halves, sec, rows_ref, out_ref, base):
    half, block = halves(picks[0][0])[0].shape
    rhs, lhs = [], []
    for slot, place, weight in picks:
        rhs.append(rows_ref[pl.ds(pl.multiple_of(place * block, block), block), :])
        lhs.append(jnp.concatenate(halves(slot), axis=0) * weight.astype(F32).astype(BF16))
    total = jnp.dot(
        jnp.concatenate(lhs, axis=1), jnp.concatenate(rhs, axis=0), preferred_element_type=F32
    ).astype(BF16)
    for i, place in enumerate((sec, 1 - sec)):
        start = pl.multiple_of(base + place * half, half)
        out_ref[pl.ds(start, half), :] = total[i * half : (i + 1) * half]


def apply_inner(basis, own_ops, share, rest, neighbours, mask, ids):
    rows, width = basis.shape
    blocks, slots, half, block = own_ops.shape
    inner, part = blocks - REACH, blocks // 2
    tile = min(512, width)

    def kernel(nb_ref, mask_ref, sec_ref, col_ref, row_ref, rows_ref, own_ref, share_ref, rest_ref, out_ref):
        first = row_ref[0] * blocks

        def body(b, carry):
            shared = b // part == col_ref[0]
            picks = []
            for s in range(slots):
                place = nb_ref[b, s] - first
                weight = jnp.where(place < 0, 0, mask_ref[b, s])
                picks.append((s, jnp.maximum(place, 0), weight))

            def halves(s):
                other = jnp.where(shared, share_ref[b % part, s], rest_ref[b % part, s])
                return own_ref[b, s], other

            apply_block(picks, halves, sec_ref[0], rows_ref, out_ref, b * block)
            return carry

        lax.fori_loop(0, inner, body, 0)

    share_spec = pl.BlockSpec(share.shape, lambda j, *_: (0, 0, 0, 0))
    return call(
        kernel, (neighbours, mask, *ids), (width // tile,),
        [pl.BlockSpec((rows, tile), lambda j, *_: (0, j)),
         pl.BlockSpec((inner, slots, half, block), lambda j, *_: (0, 0, 0, 0)),
         share_spec, share_spec],
        (basis, own_ops, share, rest),
        pl.BlockSpec((inner * block, tile), lambda j, *_: (0, j)),
        jax.ShapeDtypeStruct((inner * block, width), BF16), [],
        2 * inner * slots * block * block * width, "apply_inner",
    )


def apply_rim(basis, after, own_ops, share, rest, neighbours, mask, next_own, next_other,
              next_neighbours, next_mask, ids):
    rows, width = basis.shape
    blocks, slots, half, block = own_ops.shape
    rim, inner, part = REACH * block, blocks - REACH, blocks // 2
    base = blocks - 2 * REACH
    tile = min(512, width)

    def kernel(nb_ref, mask_ref, nnb_ref, nmask_ref, sec_ref, col_ref, row_ref, a_ref, b_ref, c_ref,
               own_ref, share_ref, rest_ref, next_ref, next_other_ref, out_ref, ext):
        first = row_ref[0] * blocks
        for i, ref in enumerate((a_ref, b_ref, c_ref)):
            ext[pl.ds(i * rim, rim), :] = ref[...]
        for i in range(REACH):
            picks = []
            for s in range(slots):
                place = nb_ref[inner + i, s] - first - base
                picks.append((s, jnp.maximum(place, 0), mask_ref[inner + i, s]))

            def halves(s, i=i):
                b = inner + i - part
                other = jnp.where(col_ref[0] == 1, share_ref[b, s], rest_ref[b, s])
                return own_ref[i, s], other

            apply_block(picks, halves, sec_ref[0], ext, out_ref, i * block)
        for i in range(REACH):
            picks = []
            for s in BACK:
                place = nnb_ref[i, s] - first - base
                weight = jnp.where(place < 2 * REACH, nmask_ref[i, s], 0)
                picks.append((s, jnp.clip(place, 0, 3 * REACH - 1), weight))

            def halves(s, i=i):
                return next_ref[i, s], next_other_ref[i, s]

            apply_block(picks, halves, sec_ref[0], ext, out_ref, rim + i * block)

    last = rows // rim - 1
    share_spec = pl.BlockSpec(share.shape, lambda j, *_: (0, 0, 0, 0))
    next_spec = pl.BlockSpec(next_own.shape, lambda j, *_: (0, 0, 0, 0))
    return call(
        kernel, (neighbours, mask, next_neighbours, next_mask, *ids), (width // tile,),
        [pl.BlockSpec((rim, tile), lambda j, *_: (last - 1, j)),
         pl.BlockSpec((rim, tile), lambda j, *_: (last, j)),
         pl.BlockSpec((rim, tile), lambda j, *_: (0, j)),
         pl.BlockSpec((REACH, slots, half, block), lambda j, *_: (inner // REACH, 0, 0, 0)),
         share_spec, share_spec] + [next_spec] * 2,
        (basis, basis, after, own_ops, share, rest, next_own, next_other),
        pl.BlockSpec((2 * rim, tile), lambda j, *_: (0, j)),
        jax.ShapeDtypeStruct((2 * rim, width), BF16),
        [pltpu.VMEM((3 * rim, tile), BF16)],
        2 * REACH * (slots + len(BACK)) * block * block * width, "apply_rim",
    )


def tile_chunk(terms, scalars, height, addend, dtype):
    width = terms[0][4].shape[1]
    tile = min(512, width)
    count = len(terms)

    def kernel(chunk_ref, mine_ref, *refs):
        out_ref = refs[-1]
        total = None if addend is None else refs[3 * count][...].astype(F32)
        for i in range(count):
            mine, moved, applied = refs[3 * i : 3 * i + 3]
            left = jnp.where(mine_ref[0] == 1, mine[...], moved[...])
            part = lax.dot_general(
                left, applied[...], (((0,), (0,)), ((), ())), preferred_element_type=F32
            )
            total = part if total is None else total + part
        out_ref[...] = total.astype(out_ref.dtype)

    in_specs, operands = [], []
    for mine, moved, first, rows, applied, place in terms:
        spec = pl.BlockSpec((rows, height), lambda j, c, m, first=first: (first, c[0]))
        in_specs += [spec, spec, pl.BlockSpec((rows, tile), lambda j, c, m, place=place: (place, j))]
        operands += [mine, moved, applied]
    out_spec = pl.BlockSpec((height, tile), lambda j, *_: (0, j))
    if addend is not None:
        in_specs.append(out_spec)
        operands.append(addend)
    return call(
        kernel, scalars, (width // tile,), in_specs, operands, out_spec,
        jax.ShapeDtypeStruct((height, width), dtype), [],
        2 * sum(t[3] for t in terms) * height * width, "tile_chunk",
    )


def per_device(basis, own_ops, neighbours, mask):
    rows, width = basis.shape
    blocks, slots, half, block = own_ops.shape
    sec, row, col = (lax.axis_index(name) for name in ("sec", "row", "col"))
    count = lax.axis_size("row")
    rim = REACH * block
    inner = blocks - REACH
    swap = [(0, 1), (1, 0)]
    down = [(i + 1, i) for i in range(count - 1)]
    to_other = [(0, 1), (3, 2)]

    part = blocks // 2
    share = lax.dynamic_slice_in_dim(own_ops, col * part, part, 0)
    behind, share = lax.optimization_barrier((basis, share))
    next_own = lax.ppermute(own_ops[:REACH], "row", down)
    after = lax.ppermute(basis[:rim], "row", down)
    share = lax.ppermute(share, "sec", swap)
    next_neighbours = lax.ppermute(neighbours, "row", down)
    next_mask = lax.ppermute(mask, "row", down)
    moved = lax.ppermute(behind, ("sec", "col"), to_other)
    share, next_own, next_neighbours, next_mask = lax.optimization_barrier(
        (share, next_own, next_neighbours, next_mask)
    )
    rest = lax.ppermute(share, "col", swap)
    next_other = lax.ppermute(next_own, "sec", swap)
    rest, next_other = lax.optimization_barrier((rest, next_other))

    ids = tuple(x.astype(jnp.int32)[None] for x in (sec, col, row))
    applied = apply_inner(basis, own_ops, share, rest, neighbours, mask, ids)
    after, applied = lax.optimization_barrier((after, applied))
    after_moved = lax.ppermute(after, ("sec", "col"), to_other)

    height = width * lax.axis_size("col") // lax.axis_size("sec") // count
    fars = count // 4
    far, pair, side = row // 4, row // 2 % 2, row % 2
    swap_side = [(i, i ^ 1) for i in range(count)]
    swap_pair = [(i, i ^ 2) for i in range(count)]
    is_mine = (sec == col).astype(jnp.int32)[None]

    def chunk(steps, pair, side, dtype, which="all", addend=None):
        where = [((far + step) % fars * 2 + pair) * 2 + side for step in steps]
        size = len(steps) * height
        lefts = [basis, moved, after, after_moved]
        if len(steps) == 1 and height % 128 == 0:
            index = where[0][None]
        else:
            index = jnp.zeros((1,), jnp.int32)
            fill = -size % 128
            size += fill
            lefts = [
                jnp.concatenate(
                    [lax.dynamic_slice_in_dim(x, w * height, height, 1) for w in where]
                    + [jnp.zeros((x.shape[0], fill), x.dtype)], 1)
                for x in lefts
            ]
        mine, other, mine_after, other_after = lefts
        terms = []
        if which != "rim":
            terms += [(mine, other, 0, inner * block, applied, 0)]
        if which != "inner":
            terms += [(mine, other, rows // rim - 1, rim, applied_rim, 0),
                      (mine_after, other_after, 0, rim, applied_rim, 1)]
        return tile_chunk(terms, (index, is_mine), size, addend, dtype)[: len(steps) * height]

    def add(first, *others):
        for other in others:
            first = first + other.astype(F32)
        return first

    away = list(range(1, fars))
    early = [chunk(away, 1 - pair, 1 - side, F32, "inner"), chunk([0], 1 - pair, 1 - side, F32, "inner")]
    *early, late = lax.optimization_barrier((*early, after))
    applied_rim = apply_rim(
        basis, late, own_ops, share, rest, neighbours, mask, next_own, next_other, next_neighbours,
        next_mask, ids
    )
    if height % 128 == 0:
        far_a = chunk(away, 1 - pair, 1 - side, BF16, "rim", early[0])
        near_a = chunk([0], 1 - pair, 1 - side, BF16, "rim", early[1])
    else:
        far_a = chunk(away, 1 - pair, 1 - side, BF16)
        near_a = chunk([0], 1 - pair, 1 - side, BF16)
    near_a, applied_rim = lax.optimization_barrier((near_a, applied_rim))
    far_a = lax.ppermute(far_a, "row", swap_side)
    near_a = lax.ppermute(near_a, "row", swap_pair)
    far_a, far_b = lax.optimization_barrier((far_a, chunk(away, pair, 1 - side, BF16)))
    far_b = lax.ppermute(far_b, "row", swap_side)
    far_c = add(chunk(away, 1 - pair, side, F32), far_a).astype(BF16)
    far_c = lax.ppermute(far_c, "row", swap_pair)
    near_b = lax.ppermute(chunk([0], 1 - pair, side, BF16), "row", swap_pair)
    near_c = add(chunk([0], pair, 1 - side, F32), near_a).astype(BF16)
    near_c = lax.ppermute(near_c, "row", swap_side)
    far_d = add(chunk(away, pair, side, F32), far_b, far_c).astype(BF16)
    parts = []
    for i, step in enumerate(away):
        route = [(g, (g + 4 * step) % count) for g in range(count)]
        parts.append(lax.ppermute(far_d[i * height : (i + 1) * height], "row", route))
    total = add(chunk([0], pair, side, F32), near_b, near_c, *parts)
    return total * (1.0 / math.sqrt(rows * count))


def solution(mesh):
    return jax.shard_map(
        per_device,
        mesh=mesh,
        in_specs=(P("row", "col"), P("row", None, "sec", None), P("row", None), P("row", None)),
        out_specs=P(("sec", "row"), "col"),
        check_vma=False,
    )
```

time: 555 us -> 204 us (0.37)
  the two profiles are of different devices: /device:TPU:0 before, /device:TPU:6 now
where the time goes in v3:
time: 204 us; the launch traced here: 203 us
  waiting for transfers between devices  92.4 us (45%)
  Pallas kernels  70.9 us (35%)
  starting transfers between devices  20.3 us (10%)
  other arithmetic  11.2 us (5%)
  local copies, waits for them, and re-layouts  8.22 us (4%)
    pallas_call x12, Pallas kernels, call(): pl.pallas_call(kernel, grid_spec=pltpu.PrefetchScalarGridSpec(num_scalar_...  70.9 us
    ppermute x1, waiting for transfers between devices, per_device(): near_b = lax.ppermute(chunk([0], 1 - pair, side, BF16), 'row', swap_pair)  27.6 us
    ppermute x1, waiting for transfers between devices, per_device(): next_neighbours = lax.ppermute(neighbours, 'row', down)  24.8 us
    ppermute x1, waiting for transfers between devices, per_device(): parts.append(lax.ppermute(far_d[i * height:(i + 1) * height], 'row', route))  14.8 us
    ppermute x1, waiting for transfers between devices, per_device(): next_other = lax.ppermute(next_own, 'sec', swap)  7.88 us
    ppermute x1, waiting for transfers between devices, per_device(): far_a = lax.ppermute(far_a, 'row', swap_side)  7.86 us
    ppermute x1, waiting for transfers between devices, per_device(): next_mask = lax.ppermute(mask, 'row', down)  4.52 us
  transfers between devices with their start and end apart: 16, of which 8 were waited for; matrix products, arithmetic and copies ran while one was open for 6% of the time, Pallas kernels for 32%

profile of v3, /device:TPU:6, one launch (start us, length us, event | category | flops | bytes accessed | tf_op | source)
XLA Modules:
  0.0 203.3 jit_solution(3488372152596091458)
XLA Ops:
  3.3 3.3 %collective-permute-start.2 = (bf16[5,7,64,128]{3,2,1,0:T(8,128)(2,1)}, bf16[5,7,64,128]{3,2,1,0:T(8,128)(2,1)S(1)}, u32[]{:S(2)}, u32[]{:S(2)}) collective-permute-start(bf16[5,7,64,128]{3,2,1,0:T(8,128)(2,1)} %constant_dynamic-slice_fusion), channel_id=1, source_target_pairs={{0,16},{16,0},{1,17},{17,1},{2,18},{18,2},{3,19},{19,3},{4,20},{20... | collective-permute-start | bytes 1720328 | tf_op jit(solution)/shard_map/ppermute | solution.py:188
  15.8 24.8 %collective-permute-done.4.nnb_ref = s32[10,7]{1,0:T(8,128)S(1)} collective-permute-done((s32[10,7]{1,0:T(8,128)S(1)}, s32[10,7]{1,0:T(8,128)S(1)}, u32[]{:S(2)}, u32[]{:S(2)}) %collective-permute-start.4) | collective-permute-done | bytes 312 | tf_op jit(solution)/shard_map/ppermute | solution.py:189
  42.6 4.5 %collective-permute-done.5.nmask_ref = s32[10,7]{1,0:T(8,128)S(1)} collective-permute-done((s32[10,7]{1,0:T(8,128)S(1)}, s32[10,7]{1,0:T(8,128)S(1)}, u32[]{:S(2)}, u32[]{:S(2)}) %collective-permute-start.5) | collective-permute-done | bytes 312 | tf_op jit(solution)/shard_map/ppermute | solution.py:190
  47.4 7.9 %collective-permute-done.7.next_other_ref = bf16[2,7,64,128]{3,2,1,0:T(8,128)(2,1)S(1)} collective-permute-done((bf16[2,7,64,128]{3,2,1,0:T(8,128)(2,1)S(1)}, bf16[2,7,64,128]{3,2,1,0:T(8,128)(2,1)S(1)}, u32[]{:S(2)}, u32[]{:S(2)}) %collective-permute-start.7) | collective-permute-done | bytes 229408 | tf_op jit(solution)/shard_map/ppermute | solution.py:196
  55.2 13.5 %apply_inner.1.refs_2_ = bf16[1024,2048]{1,0:T(8,128)(2,1)} custom-call(s32[10,7]{1,0:T(8,128)S(1)} %copy.7.nb_ref, s32[10,7]{1,0:T(8,128)S(1)} %copy.8.mask_ref, s32[1]{0:T(128)} %bitcast.2.sec_ref, s32[1]{0:T(128)} %bitcast.3.col_ref, s32[1]{0:T(128)} %bitcast.4.row_ref, bf16[1280,2048]{1,0:T(8,128)(2,1)} %refs_3_.11, ...), custom_call_target="tpu_custom_call" | custom-call | flops 3758096384 | bytes 7536640 | tf_op jit(solution)/shard_map/apply_inner/pallas_call | solution.py:18
  70.2 4.4 %tile_chunk.10.refs_6_ = f32[256,2048]{1,0:T(8,128)S(1)} custom-call(s32[1]{0:T(128)} %bitcast.6.chunk_ref, s32[1]{0:T(128)} %bitcast.1.mine_ref, bf16[1280,2048]{1,0:T(8,128)(2,1)} %refs_3_.11, bf16[1280,2048]{1,0:T(8,128)(2,1)} %collective-permute-done.refs_1_.refs_4_, bf16[1024,2048]{1,0:T(8,128)(2,1)} %apply_inner.1.refs_2_), custom_call_target="tpu_custom_call" | custom-call | flops 1073741824 | bytes 14680064 | tf_op jit(solution)/shard_map/tile_chunk/pallas_call | solution.py:18
  76.1 4.6 %tile_chunk.11.refs_6_ = f32[256,2048]{1,0:T(8,128)S(1)} custom-call(s32[1]{0:T(128)} %bitcast.5.chunk_ref, s32[1]{0:T(128)} %bitcast.1.mine_ref, bf16[1280,2048]{1,0:T(8,128)(2,1)} %refs_3_.11, bf16[1280,2048]{1,0:T(8,128)(2,1)} %collective-permute-done.refs_1_.refs_4_, bf16[1024,2048]{1,0:T(8,128)(2,1)} %apply_inner.1.refs_2_), custom_call_target="tpu_custom_call" | custom-call | flops 1073741824 | bytes 14680064 | tf_op jit(solution)/shard_map/tile_chunk/pallas_call | solution.py:18
  82.0 5.5 %apply_rim.1.refs_2_.refs_5_.refs_8_ = bf16[512,2048]{1,0:T(8,128)(2,1)S(1)} custom-call(s32[10,7]{1,0:T(8,128)S(1)} %copy.7.nb_ref, s32[10,7]{1,0:T(8,128)S(1)} %copy.8.mask_ref, s32[10,7]{1,0:T(8,128)S(1)} %collective-permute-done.4.nnb_ref, s32[10,7]{1,0:T(8,128)S(1)} %collective-permute-done.5.nmask_ref, s32[1]{0:T(128)} %bitcast.2.sec_ref, ...), custom_call_target="tpu_custom_call" | custom-call | flops 1476395008 | bytes 14286848 | tf_op jit(solution)/shard_map/apply_rim/pallas_call | solution.py:18
  87.5 5.2 %tile_chunk.17 = bf16[256,2048]{1,0:T(8,128)(2,1)} custom-call(s32[1]{0:T(128)} %bitcast.6.chunk_ref, s32[1]{0:T(128)} %bitcast.1.mine_ref, bf16[1280,2048]{1,0:T(8,128)(2,1)} %refs_3_.11, bf16[1280,2048]{1,0:T(8,128)(2,1)} %collective-permute-done.refs_1_.refs_4_, bf16[512,2048]{1,0:T(8,128)(2,1)S(1)} %apply_rim.1.refs_2_.refs_5_.refs_8_, ...), custom_call_target="tpu_custom_call" | custom-call | flops 536870912 | bytes 18874368 | tf_op jit(solution)/shard_map/tile_chunk/pallas_call | solution.py:18
  92.7 4.5 %tile_chunk.12 = bf16[256,2048]{1,0:T(8,128)(2,1)} custom-call(s32[1]{0:T(128)} %bitcast.5.chunk_ref, s32[1]{0:T(128)} %bitcast.1.mine_ref, bf16[1280,2048]{1,0:T(8,128)(2,1)} %refs_3_.11, bf16[1280,2048]{1,0:T(8,128)(2,1)} %collective-permute-done.refs_1_.refs_4_, bf16[512,2048]{1,0:T(8,128)(2,1)S(1)} %apply_rim.1.refs_2_.refs_5_.refs_8_, ...), custom_call_target="tpu_custom_call" | custom-call | flops 536870912 | bytes 18874368 | tf_op jit(solution)/shard_map/tile_chunk/pallas_call | solution.py:18
  98.8 5.5 %tile_chunk.19 = f32[256,2048]{1,0:T(8,128)S(1)} custom-call(s32[1]{0:T(128)} %bitcast.11.chunk_ref, s32[1]{0:T(128)} %bitcast.1.mine_ref, bf16[1280,2048]{1,0:T(8,128)(2,1)} %refs_3_.11, bf16[1280,2048]{1,0:T(8,128)(2,1)} %collective-permute-done.refs_1_.refs_4_, bf16[1024,2048]{1,0:T(8,128)(2,1)} %apply_inner.1.refs_2_, bf16[1280,2048]{1,0:T(8,128)(2,1)} %refs_3_.11, ...), custom_call_target="tpu_custom_call" | custom-call | flops 1610612736 | bytes 31457280 | tf_op jit(solution)/shard_map/tile_chunk/pallas_call | solution.py:18
  104.3 5.9 %tile_chunk.18 = bf16[256,2048]{1,0:T(8,128)(2,1)} custom-call(s32[1]{0:T(128)} %bitcast.10.chunk_ref, s32[1]{0:T(128)} %bitcast.1.mine_ref, bf16[1280,2048]{1,0:T(8,128)(2,1)} %refs_3_.11, bf16[1280,2048]{1,0:T(8,128)(2,1)} %collective-permute-done.refs_1_.refs_4_, bf16[1024,2048]{1,0:T(8,128)(2,1)} %apply_inner.1.refs_2_, bf16[1280,2048]{1,0:T(8,128)(2,1)} %refs_3_.11, ...), custom_call_target="tpu_custom_call" | custom-call | flops 1610612736 | bytes 31457280 | tf_op jit(solution)/shard_map/tile_chunk/pallas_call | solution.py:18
  110.2 7.9 %collective-permute-done.12 = bf16[256,2048]{1,0:T(8,128)(2,1)} collective-permute-done((bf16[256,2048]{1,0:T(8,128)(2,1)}, bf16[256,2048]{1,0:T(8,128)(2,1)}, u32[]{:S(2)}, u32[]{:S(2)}) %collective-permute-start.12) | collective-permute-done | bytes 1048608 | tf_op jit(solution)/shard_map/ppermute | solution.py:255
  118.0 2.5 %add_convert_fusion.1 = bf16[256,2048]{1,0:T(8,128)(2,1)} fusion(f32[256,2048]{1,0:T(8,128)S(1)} %tile_chunk.19, bf16[256,2048]{1,0:T(8,128)(2,1)} %collective-permute-done.12), kind=kLoop, calls=%fused_computation.2 | loop fusion | flops 1572864 | bytes 4194304 | tf_op jit(solution)/shard_map/convert_element_type | solution.py:259
  122.2 5.7 %tile_chunk.14 = bf16[256,2048]{1,0:T(8,128)(2,1)} custom-call(s32[1]{0:T(128)} %bitcast.7.chunk_ref, s32[1]{0:T(128)} %bitcast.1.mine_ref, bf16[1280,2048]{1,0:T(8,128)(2,1)} %refs_3_.11, bf16[1280,2048]{1,0:T(8,128)(2,1)} %collective-permute-done.refs_1_.refs_4_, bf16[1024,2048]{1,0:T(8,128)(2,1)} %apply_inner.1.refs_2_, bf16[1280,2048]{1,0:T(8,128)(2,1)} %refs_3_.11, ...), custom_call_target="tpu_custom_call" | custom-call | flops 1610612736 | bytes 31457280 | tf_op jit(solution)/shard_map/tile_chunk/pallas_call | solution.py:18
  128.3 5.3 %tile_chunk.16 = f32[256,2048]{1,0:T(8,128)S(1)} custom-call(s32[1]{0:T(128)} %bitcast.9.chunk_ref, s32[1]{0:T(128)} %bitcast.1.mine_ref, bf16[1280,2048]{1,0:T(8,128)(2,1)} %refs_3_.11, bf16[1280,2048]{1,0:T(8,128)(2,1)} %collective-permute-done.refs_1_.refs_4_, bf16[1024,2048]{1,0:T(8,128)(2,1)} %apply_inner.1.refs_2_, bf16[1280,2048]{1,0:T(8,128)(2,1)} %refs_3_.11, ...), custom_call_target="tpu_custom_call" | custom-call | flops 1610612736 | bytes 31457280 | tf_op jit(solution)/shard_map/tile_chunk/pallas_call | solution.py:18
  133.7 5.4 %tile_chunk.15 = f32[256,2048]{1,0:T(8,128)S(1)} custom-call(s32[1]{0:T(128)} %bitcast.8.chunk_ref, s32[1]{0:T(128)} %bitcast.1.mine_ref, bf16[1280,2048]{1,0:T(8,128)(2,1)} %refs_3_.11, bf16[1280,2048]{1,0:T(8,128)(2,1)} %collective-permute-done.refs_1_.refs_4_, bf16[1024,2048]{1,0:T(8,128)(2,1)} %apply_inner.1.refs_2_, bf16[1280,2048]{1,0:T(8,128)(2,1)} %refs_3_.11, ...), custom_call_target="tpu_custom_call" | custom-call | flops 1610612736 | bytes 31457280 | tf_op jit(solution)/shard_map/tile_chunk/pallas_call | solution.py:18
  139.1 2.5 %add_convert_fusion.2 = bf16[256,2048]{1,0:T(8,128)(2,1)} fusion(f32[256,2048]{1,0:T(8,128)S(1)} %tile_chunk.15, bf16[256,2048]{1,0:T(8,128)(2,1)} %collective-permute-done.10), kind=kLoop, calls=%fused_computation.3 | loop fusion | flops 1572864 | bytes 4194304 | tf_op jit(solution)/shard_map/convert_element_type | solution.py:262
  143.6 3.1 %collective-permute-done.14 = bf16[256,2048]{1,0:T(8,128)(2,1)} collective-permute-done((bf16[256,2048]{1,0:T(8,128)(2,1)}, bf16[256,2048]{1,0:T(8,128)(2,1)}, u32[]{:S(2)}, u32[]{:S(2)}) %collective-permute-start.14) | collective-permute-done | bytes 1048608 | tf_op jit(solution)/shard_map/ppermute | solution.py:260
  148.5 3.0 %add_convert_fusion = bf16[256,2048]{1,0:T(8,128)(2,1)} fusion(bf16[256,2048]{1,0:T(8,128)(2,1)} %collective-permute-done.14, f32[256,2048]{1,0:T(8,128)S(1)} %tile_chunk.16, bf16[256,2048]{1,0:T(8,128)(2,1)} %collective-permute-done.13), kind=kLoop, calls=%fused_computation.1 | loop fusion | flops 2621440 | bytes 5242880 | tf_op jit(solution)/shard_map/convert_element_type | solution.py:264
  152.4 5.4 %tile_chunk.13 = f32[256,2048]{1,0:T(8,128)S(1)} custom-call(s32[1]{0:T(128)} %bitcast.chunk_ref, s32[1]{0:T(128)} %bitcast.1.mine_ref, bf16[1280,2048]{1,0:T(8,128)(2,1)} %refs_3_.11, bf16[1280,2048]{1,0:T(8,128)(2,1)} %collective-permute-done.refs_1_.refs_4_, bf16[1024,2048]{1,0:T(8,128)(2,1)} %apply_inner.1.refs_2_, bf16[1280,2048]{1,0:T(8,128)(2,1)} %refs_3_.11, ...), custom_call_target="tpu_custom_call" | custom-call | flops 1610612736 | bytes 31457280 | tf_op jit(solution)/shard_map/tile_chunk/pallas_call | solution.py:18
  157.7 27.6 %collective-permute-done.9 = bf16[256,2048]{1,0:T(8,128)(2,1)S(1)} collective-permute-done((bf16[256,2048]{1,0:T(8,128)(2,1)}, bf16[256,2048]{1,0:T(8,128)(2,1)S(1)}, u32[]{:S(2)}, u32[]{:S(2)}) %collective-permute-start.9) | collective-permute-done | bytes 1048608 | tf_op jit(solution)/shard_map/ppermute | solution.py:261
  185.4 14.8 %collective-permute-done.15 = bf16[256,2048]{1,0:T(8,128)(2,1)} collective-permute-done((bf16[256,2048]{1,0:T(8,128)(2,1)}, bf16[256,2048]{1,0:T(8,128)(2,1)}, u32[]{:S(2)}, u32[]{:S(2)}) %collective-permute-start.15) | collective-permute-done | bytes 1048608 | tf_op jit(solution)/shard_map/ppermute | solution.py:268
  200.2 3.1 %add_multiply_fusion = f32[256,2048]{1,0:T(8,128)} fusion(bf16[256,2048]{1,0:T(8,128)(2,1)} %collective-permute-done.15, bf16[256,2048]{1,0:T(8,128)(2,1)S(1)} %collective-permute-done.11, f32[256,2048]{1,0:T(8,128)S(1)} %tile_chunk.13, bf16[256,2048]{1,0:T(8,128)(2,1)S(1)} %collective-permute-done.9), kind=kLoop, calls=%fused_computation | loop fusion | flops 3670016 | bytes 7340032 | tf_op jit(solution)/shard_map/mul | solution.py:270
  (53 shorter events, 27.0 us)
Async XLA Ops:
  0.0 55.2 %copy-start.4 = (bf16[10,7,64,128]{3,2,1,0:T(8,128)(2,1)S(1)}, bf16[10,7,64,128]{3,2,1,0:T(8,128)(2,1)}, u32[]{:S(2)}) copy-start(bf16[10,7,64,128]{3,2,1,0:T(8,128)(2,1)} %own_ref.3) | copy-start | bytes 3440644
  0.0 13.7 %copy-start.10 = (s32[10,7]{0,1:T(8,128)S(1)}, s32[10,7]{0,1:T(8,128)}, u32[]{:S(2)}) copy-start(s32[10,7]{0,1:T(8,128)} %param.6) | copy-start | bytes 844
  0.0 15.7 %copy-start.11 = (s32[10,7]{0,1:T(8,128)S(1)}, s32[10,7]{0,1:T(8,128)}, u32[]{:S(2)}) copy-start(s32[10,7]{0,1:T(8,128)} %param.7) | copy-start | bytes 844
  2.0 68.1 %collective-permute-start = (bf16[1280,2048]{1,0:T(8,128)(2,1)}, bf16[1280,2048]{1,0:T(8,128)(2,1)}, u32[]{:S(2)}, u32[]{:S(2)}) collective-permute-start(bf16[1280,2048]{1,0:T(8,128)(2,1)} %refs_3_.11), channel_id=1, source_target_pairs={{0,1},{17,16},{2,3},{19,18},{4,5},{21,20},{6,7},{23,22},{8,9},{25,... | collective-permute-start | bytes 15728648 | tf_op jit(solution)/shard_map/ppermute | solution.py:191
  3.3 43.8 %collective-permute-start.2 = (bf16[5,7,64,128]{3,2,1,0:T(8,128)(2,1)}, bf16[5,7,64,128]{3,2,1,0:T(8,128)(2,1)S(1)}, u32[]{:S(2)}, u32[]{:S(2)}) collective-permute-start(bf16[5,7,64,128]{3,2,1,0:T(8,128)(2,1)} %constant_dynamic-slice_fusion), channel_id=1, source_target_pairs={{0,16},{16,0},{1,17},{17,1},{2,18},{18,2},{3,19},{19,3},{4,20},{20... | collective-permute-start | bytes 1720328 | tf_op jit(solution)/shard_map/ppermute | solution.py:188
  7.6 39.6 %collective-permute-start.3 = (bf16[2,7,64,128]{3,2,1,0:T(8,128)(2,1)S(1)}, bf16[2,7,64,128]{3,2,1,0:T(8,128)(2,1)S(1)}, u32[]{:S(2)}, u32[]{:S(2)}) collective-permute-start(bf16[2,7,64,128]{3,2,1,0:T(8,128)(2,1)S(1)} %slice.7), channel_id=1, source_target_pairs={{2,0},{4,2},{6,4},{8,6},{10,8},{12,10},{14,12},{3,1},{5,3},{7,5},{... | collective-permute-start | bytes 688136 | tf_op jit(solution)/shard_map/ppermute | solution.py:186
  11.8 57.0 %collective-permute-start.1 = (bf16[256,2048]{1,0:T(8,128)(2,1)}, bf16[256,2048]{1,0:T(8,128)(2,1)S(1)}, u32[]{:S(2)}, u32[]{:S(2)}) collective-permute-start(bf16[256,2048]{1,0:T(8,128)(2,1)} %slice.6), channel_id=1, source_target_pairs={{2,0},{4,2},{6,4},{8,6},{10,8},{12,10},{14,12},{3,1},{5,3},{7,5},{... | collective-permute-start | bytes 3145736 | tf_op jit(solution)/shard_map/ppermute | solution.py:187
  13.8 26.9 %collective-permute-start.4 = (s32[10,7]{1,0:T(8,128)S(1)}, s32[10,7]{1,0:T(8,128)S(1)}, u32[]{:S(2)}, u32[]{:S(2)}) collective-permute-start(s32[10,7]{1,0:T(8,128)S(1)} %copy.7.nb_ref), channel_id=1, source_target_pairs={{2,0},{4,2},{6,4},{8,6},{10,8},{12,10},{14,12},{3,1},{5,3},{7,5},{... | collective-permute-start | bytes 848 | tf_op jit(solution)/shard_map/ppermute | solution.py:189
  40.7 6.4 %collective-permute-start.5 = (s32[10,7]{1,0:T(8,128)S(1)}, s32[10,7]{1,0:T(8,128)S(1)}, u32[]{:S(2)}, u32[]{:S(2)}) collective-permute-start(s32[10,7]{1,0:T(8,128)S(1)} %copy.8.mask_ref), channel_id=1, source_target_pairs={{2,0},{4,2},{6,4},{8,6},{10,8},{12,10},{14,12},{3,1},{5,3},{7,5},{... | collective-permute-start | bytes 848 | tf_op jit(solution)/shard_map/ppermute | solution.py:190
  47.1 21.6 %copy-start.6 = (bf16[5,7,64,128]{3,2,1,0:T(8,128)(2,1)}, bf16[5,7,64,128]{3,2,1,0:T(8,128)(2,1)S(1)}, u32[]{:S(2)}) copy-start(bf16[5,7,64,128]{3,2,1,0:T(8,128)(2,1)S(1)} %collective-permute-done.2.share_ref) | copy-start | bytes 1720324
  47.1 8.1 %collective-permute-start.6 = (bf16[5,7,64,128]{3,2,1,0:T(8,128)(2,1)S(1)}, bf16[5,7,64,128]{3,2,1,0:T(8,128)(2,1)}, u32[]{:S(2)}, u32[]{:S(2)}) collective-permute-start(bf16[5,7,64,128]{3,2,1,0:T(8,128)(2,1)S(1)} %collective-permute-done.2.share_ref), channel_id=1, source_target_pairs={{0,1},{1,0},{2,3},{3,2},{4,5},{5,4},{6,7},{7,6},{8,9},{9,8},{10,11... | collective-permute-start | bytes 1720328 | tf_op jit(solution)/shard_map/ppermute | solution.py:195
  47.2 8.0 %collective-permute-start.7 = (bf16[2,7,64,128]{3,2,1,0:T(8,128)(2,1)S(1)}, bf16[2,7,64,128]{3,2,1,0:T(8,128)(2,1)S(1)}, u32[]{:S(2)}, u32[]{:S(2)}) collective-permute-start(bf16[2,7,64,128]{3,2,1,0:T(8,128)(2,1)S(1)} %collective-permute-done.3.next_ref), channel_id=1, source_target_pairs={{0,16},{16,0},{1,17},{17,1},{2,18},{18,2},{3,19},{19,3},{4,20},{20... | collective-permute-start | bytes 688136 | tf_op jit(solution)/shard_map/ppermute | solution.py:196
  55.2 13.5 %copy-start.8 = (bf16[2,7,64,128]{3,2,1,0:T(8,128)(2,1)}, bf16[2,7,64,128]{3,2,1,0:T(8,128)(2,1)S(1)}, u32[]{:S(2)}) copy-start(bf16[2,7,64,128]{3,2,1,0:T(8,128)(2,1)S(1)} %collective-permute-done.7.next_other_ref) | copy-start | bytes 688132
  68.8 18.7 %collective-permute-start.8 = (bf16[256,2048]{1,0:T(8,128)(2,1)S(1)}, bf16[256,2048]{1,0:T(8,128)(2,1)}, u32[]{:S(2)}, u32[]{:S(2)}) collective-permute-start(bf16[256,2048]{1,0:T(8,128)(2,1)S(1)} %collective-permute-done.1.c_ref.refs_3_.refs_6_), channel_id=1, source_target_pairs={{0,1},{17,16},{2,3},{19,18},{4,5},{21,20},{6,7},{23,22},{8,9},{25,... | collective-permute-start | bytes 3145736 | tf_op jit(solution)/shard_map/ppermute | solution.py:202
  76.1 5.9 %copy-start.5 = (bf16[10,7,64,128]{3,2,1,0:T(8,128)(2,1)S(1)}, bf16[10,7,64,128]{3,2,1,0:T(8,128)(2,1)}, u32[]{:S(2)}) copy-start(bf16[10,7,64,128]{3,2,1,0:T(8,128)(2,1)} %own_ref.3) | copy-start | bytes 3440644
  76.1 5.9 %copy-start.7 = (bf16[5,7,64,128]{3,2,1,0:T(8,128)(2,1)S(1)}, bf16[5,7,64,128]{3,2,1,0:T(8,128)(2,1)}, u32[]{:S(2)}) copy-start(bf16[5,7,64,128]{3,2,1,0:T(8,128)(2,1)} %copy-done.6) | copy-start | bytes 1720324
  76.1 5.9 %copy-start.9 = (bf16[2,7,64,128]{3,2,1,0:T(8,128)(2,1)S(1)}, bf16[2,7,64,128]{3,2,1,0:T(8,128)(2,1)}, u32[]{:S(2)}) copy-start(bf16[2,7,64,128]{3,2,1,0:T(8,128)(2,1)} %copy-done.8) | copy-start | bytes 688132
  92.7 25.4 %collective-permute-start.12 = (bf16[256,2048]{1,0:T(8,128)(2,1)}, bf16[256,2048]{1,0:T(8,128)(2,1)}, u32[]{:S(2)}, u32[]{:S(2)}) collective-permute-start(bf16[256,2048]{1,0:T(8,128)(2,1)} %tile_chunk.17), channel_id=1, source_target_pairs={{0,2},{2,0},{4,6},{6,4},{8,10},{10,8},{12,14},{14,12},{1,3},{3,1},... | collective-permute-start | bytes 3145736 | tf_op jit(solution)/shard_map/ppermute | solution.py:255
  97.2 41.9 %collective-permute-start.10 = (bf16[256,2048]{1,0:T(8,128)(2,1)}, bf16[256,2048]{1,0:T(8,128)(2,1)}, u32[]{:S(2)}, u32[]{:S(2)}) collective-permute-start(bf16[256,2048]{1,0:T(8,128)(2,1)} %tile_chunk.12), channel_id=1, source_target_pairs={{0,4},{2,6},{4,0},{6,2},{8,12},{10,14},{12,8},{14,10},{1,5},{3,7},... | collective-permute-start | bytes 3145736 | tf_op jit(solution)/shard_map/ppermute | solution.py:256
  120.5 26.2 %collective-permute-start.14 = (bf16[256,2048]{1,0:T(8,128)(2,1)}, bf16[256,2048]{1,0:T(8,128)(2,1)}, u32[]{:S(2)}, u32[]{:S(2)}) collective-permute-start(bf16[256,2048]{1,0:T(8,128)(2,1)} %add_convert_fusion.1), channel_id=1, source_target_pairs={{0,4},{2,6},{4,0},{6,2},{8,12},{10,14},{12,8},{14,10},{1,5},{3,7},... | collective-permute-start | bytes 3145736 | tf_op jit(solution)/shard_map/ppermute | solution.py:260
  122.2 26.3 %collective-permute-start.13 = (bf16[256,2048]{1,0:T(8,128)(2,1)}, bf16[256,2048]{1,0:T(8,128)(2,1)}, u32[]{:S(2)}, u32[]{:S(2)}) collective-permute-start(bf16[256,2048]{1,0:T(8,128)(2,1)} %tile_chunk.18), channel_id=1, source_target_pairs={{0,2},{2,0},{4,6},{6,4},{8,10},{10,8},{12,14},{14,12},{1,3},{3,1},... | collective-permute-start | bytes 3145736 | tf_op jit(solution)/shard_map/ppermute | solution.py:258
  127.9 57.5 %collective-permute-start.9 = (bf16[256,2048]{1,0:T(8,128)(2,1)}, bf16[256,2048]{1,0:T(8,128)(2,1)S(1)}, u32[]{:S(2)}, u32[]{:S(2)}) collective-permute-start(bf16[256,2048]{1,0:T(8,128)(2,1)} %tile_chunk.14), channel_id=1, source_target_pairs={{0,4},{2,6},{4,0},{6,2},{8,12},{10,14},{12,8},{14,10},{1,5},{3,7},... | collective-permute-start | bytes 3145736 | tf_op jit(solution)/shard_map/ppermute | solution.py:261
  141.6 43.8 %collective-permute-start.11 = (bf16[256,2048]{1,0:T(8,128)(2,1)}, bf16[256,2048]{1,0:T(8,128)(2,1)S(1)}, u32[]{:S(2)}, u32[]{:S(2)}) collective-permute-start(bf16[256,2048]{1,0:T(8,128)(2,1)} %add_convert_fusion.2), channel_id=1, source_target_pairs={{0,2},{2,0},{4,6},{6,4},{8,10},{10,8},{12,14},{14,12},{1,3},{3,1},... | collective-permute-start | bytes 3145736 | tf_op jit(solution)/shard_map/ppermute | solution.py:263
  151.6 48.6 %collective-permute-start.15 = (bf16[256,2048]{1,0:T(8,128)(2,1)}, bf16[256,2048]{1,0:T(8,128)(2,1)}, u32[]{:S(2)}, u32[]{:S(2)}) collective-permute-start(bf16[256,2048]{1,0:T(8,128)(2,1)} %add_convert_fusion), channel_id=1, source_target_pairs={{0,8},{2,10},{4,12},{6,14},{8,0},{10,2},{12,4},{14,6},{1,9},{3,11}... | collective-permute-start | bytes 3145736 | tf_op jit(solution)/shard_map/ppermute | solution.py:268
  (4 other events, 13.4 us)

commit v4 on v0

v4 whole, which is shorter than its diff:
```python
import math

import jax
import jax.numpy as jnp
from jax import lax
from jax.experimental import pallas as pl
from jax.experimental.pallas import tpu as pltpu
from jax.sharding import PartitionSpec as P

REACH = 2
VMEM_LIMIT = 56 * 1024 * 1024
F32, BF16 = jnp.float32, jnp.bfloat16


def call(kernel, scalars, grid, in_specs, operands, out_specs, out_shape, scratch, flops, name):
    moved = sum(x.size * x.dtype.itemsize for x in operands)
    return pl.pallas_call(
        kernel,
        grid_spec=pltpu.PrefetchScalarGridSpec(
            num_scalar_prefetch=len(scalars), grid=grid, in_specs=in_specs,
            out_specs=out_specs, scratch_shapes=scratch,
        ),
        out_shape=out_shape,
        compiler_params=pltpu.CompilerParams(vmem_limit_bytes=VMEM_LIMIT),
        cost_estimate=pl.CostEstimate(flops=flops, bytes_accessed=moved, transcendentals=0),
        name=name,
    )(*scalars, *operands)


def fixed(array):
    return pl.BlockSpec(array.shape, lambda j, *_: (0,) * array.ndim)


def transposed_dot(left, right):
    return lax.dot_general(left, right, (((0,), (0,)), ((), ())), preferred_element_type=F32)


def apply_block(b, shift, nb_ref, mask_ref, sec, first, halves, rows_ref, out_ref, base):
    slots = nb_ref.shape[1]
    rhs, lhs = [], []
    for s in range(slots):
        own, other = halves(s)
        half, block = own.shape
        place = nb_ref[b, s] - first + shift
        rhs.append(rows_ref[pl.ds(pl.multiple_of(place * block, block), block), :])
        weight = mask_ref[b, s].astype(F32).astype(BF16)
        lhs.append(jnp.concatenate([own, other], axis=0) * weight)
    total = jnp.dot(
        jnp.concatenate(lhs, axis=1), jnp.concatenate(rhs, axis=0), preferred_element_type=F32
    ).astype(BF16)
    for i, half_of in enumerate((sec, 1 - sec)):
        start = pl.multiple_of(base + half_of * half, half)
        out_ref[pl.ds(start, half), :] = total[i * half : (i + 1) * half]


def inner_rows(basis, own_ops, share, rest, tables, ids, lefts, index, size):
    rows, width = basis.shape
    blocks, slots, half, block = own_ops.shape
    part, rim = blocks // 2, REACH * block
    tile = min(1024, width)

    def kernel(nb_ref, mask_ref, sec_ref, col_ref, row_ref, index_ref, rows_ref, own_ref, share_ref, rest_ref,
               m0, o0, m1, o1, out_ref, unit_ref):
        mine = sec_ref[0] == col_ref[0]
        for b in range(REACH, blocks - REACH):
            def halves(s, b=b):
                other = jnp.where(col_ref[0] == b // part, share_ref[b % part, s], rest_ref[b % part, s])
                return own_ref[b, s], other

            apply_block(b, 0, nb_ref, mask_ref, sec_ref[0], row_ref[0] * blocks, halves, rows_ref,
                        out_ref, (b - REACH) * block)
        for u, (here, there) in enumerate(((m0, o0), (m1, o1))):
            left = jnp.where(mine, here[rim : rows - rim, :], there[rim : rows - rim, :])
            unit_ref[u] = transposed_dot(left, out_ref[...])

    unit = [pl.BlockSpec((rows, size), lambda j, *s, u=u: (0, s[5][u])) for u in (0, 0, 1, 1)]
    return call(
        kernel, (*tables, *ids, index), (width // tile,),
        [pl.BlockSpec((rows, tile), lambda j, *_: (0, j)), fixed(own_ops), fixed(share), fixed(rest)] + unit,
        (basis, own_ops, share, rest, *lefts, *lefts),
        [pl.BlockSpec((rows - 2 * rim, tile), lambda j, *_: (0, j)),
         pl.BlockSpec((2, size, tile), lambda j, *_: (0, 0, j))],
        [jax.ShapeDtypeStruct((rows - 2 * rim, width), BF16), jax.ShapeDtypeStruct((2, size, width), F32)],
        [], 2 * (rows - 2 * rim) * width * (slots * block + 2 * size), "inner_rows",
    )


def rim_rows(basis, halos, own_ops, share, rest, tables, ids, lefts, index, size, begun):
    rows, width = basis.shape
    blocks, slots, half, block = own_ops.shape
    part, rim = blocks // 2, REACH * block
    tile = min(1024, width)

    def kernel(nb_ref, mask_ref, sec_ref, col_ref, row_ref, index_ref, up_ref, down_ref, split_ref, swapped_ref,
               head_ref, tail0_ref, tail1_ref, own_ref, share_ref, rest_ref, m0, o0, m1, o1, begun_ref,
               out_ref, unit0_ref, unit1_ref, ext):
        mine, lower = sec_ref[0] == col_ref[0], sec_ref[0] == 0
        split, swapped = split_ref[...], swapped_ref[...]
        pieces = (jnp.where(lower, swapped, split), up_ref[...], head_ref[...], tail0_ref[...],
                  tail1_ref[...], down_ref[...], jnp.where(lower, split, swapped))
        start = 0
        for piece in pieces:
            ext[start : start + piece.shape[0], :] = piece
            start += piece.shape[0]
        for i, b in enumerate((0, 1, blocks - 2, blocks - 1)):
            def halves(s, b=b):
                other = jnp.where(col_ref[0] == b // part, share_ref[b % part, s], rest_ref[b % part, s])
                return own_ref[b, s], other

            shift = REACH if b < REACH else 5 * REACH - blocks
            apply_block(b, shift, nb_ref, mask_ref, sec_ref[0], row_ref[0] * blocks, halves, ext,
                        out_ref, i * block)
        for u, (here, there, unit_ref) in enumerate(((m0, o0, unit0_ref), (m1, o1, unit1_ref))):
            total = begun_ref[u]
            for i, at in enumerate((0, rows - rim)):
                left = jnp.where(mine, here[at : at + rim, :], there[at : at + rim, :])
                total = total + transposed_dot(left, out_ref[i * rim : (i + 1) * rim, :])
            unit_ref[...] = total.astype(BF16)

    unit = [pl.BlockSpec((rows, size), lambda j, *s, u=u: (0, s[5][u])) for u in (0, 0, 1, 1)]
    last = rows // rim - 1
    halo_spec = pl.BlockSpec((block, tile), lambda j, *_: (0, j))
    unit_out = pl.BlockSpec((size, tile), lambda j, *_: (0, j))
    return call(
        kernel, (*tables, *ids, index), (width // tile,),
        [halo_spec] * 4
        + [pl.BlockSpec((2 * rim, tile), lambda j, *_: (0, j)),
           pl.BlockSpec((rim, tile), lambda j, *_: (last - 1, j)),
           pl.BlockSpec((rim, tile), lambda j, *_: (last, j)),
           fixed(own_ops), fixed(share), fixed(rest)]
        + unit + [pl.BlockSpec((2, size, tile), lambda j, *_: (0, 0, j))],
        (*halos, basis, basis, basis, own_ops, share, rest, *lefts, *lefts, begun),
        [pl.BlockSpec((2 * rim, tile), lambda j, *_: (0, j)), unit_out, unit_out],
        [jax.ShapeDtypeStruct((2 * rim, width), BF16)] + [jax.ShapeDtypeStruct((size, width), BF16)] * 2,
        [pltpu.VMEM((6 * rim, tile), BF16)],
        4 * rim * width * (slots * block + 2 * size), "rim_rows",
    )


def units(lefts, inner, rim_part, ids, index, first, count, size, dtype):
    rows = lefts[0].shape[0]
    width = inner.shape[1]
    rim = rim_part.shape[0] // 2

    def kernel(sec_ref, col_ref, row_ref, index_ref, here, there, inner_ref, rim_ref, *out_refs):
        left = jnp.where(sec_ref[0] == col_ref[0], here[...], there[...])
        total = (
            transposed_dot(left[rim : rows - rim], inner_ref[...])
            + transposed_dot(left[:rim], rim_ref[:rim, :])
            + transposed_dot(left[rows - rim :], rim_ref[rim:, :])
        ).astype(dtype)
        for u, out_ref in enumerate(out_refs):
            @pl.when(pl.program_id(0) == u)
            def _(out_ref=out_ref):
                out_ref[...] = total

    unit = pl.BlockSpec((rows, size), lambda u, *s: (0, s[3][first + u]))
    return call(
        kernel, (*ids, index), (count,), [unit, unit, fixed(inner), fixed(rim_part)],
        (*lefts, inner, rim_part),
        [pl.BlockSpec((size, width), lambda u, *_: (0, 0))] * count,
        [jax.ShapeDtypeStruct((size, width), dtype)] * count, [],
        2 * count * rows * size * width, "units",
    )


def per_device(basis, own_ops, neighbours, mask):
    rows, width = basis.shape
    blocks, slots, half, block = own_ops.shape
    sec, row, col = (lax.axis_index(name) for name in ("sec", "row", "col"))
    count = lax.axis_size("row")
    rim = REACH * block
    swap = [(0, 1), (1, 0)]
    up = [(i, i + 1) for i in range(count - 1)]
    down = [(i + 1, i) for i in range(count - 1)]

    part = blocks // 2
    split = lax.dynamic_slice_in_dim(basis, block + sec * (rows - 3 * block), block, 0)
    share = lax.dynamic_slice_in_dim(own_ops, col * part, part, 0)
    split, share, behind = lax.optimization_barrier((split, share, basis))
    split = lax.ppermute(
        split, ("sec", "row"), down + [(count + i, count + j) for i, j in up]
    )
    share = lax.ppermute(share, "sec", swap)
    from_before = lax.ppermute(basis[rows - block :], "row", up)
    from_after = lax.ppermute(basis[:block], "row", down)
    moved = lax.ppermute(behind, ("sec", "col"), [(0, 1), (3, 2)])
    share, split = lax.optimization_barrier((share, split))
    rest = lax.ppermute(share, "col", swap)
    swapped = lax.ppermute(split, "sec", swap)

    height = width * lax.axis_size("col") // lax.axis_size("sec") // count
    fars = count // 4
    far, pair, side = row // 4, row // 2 % 2, row % 2
    away = list(range(1, fars))
    plan = [
        (away, 1 - pair, 1 - side), ([0], 1 - pair, 1 - side), (away, pair, 1 - side), ([0], 1 - pair, side),
        (away, 1 - pair, side), ([0], pair, 1 - side), (away, pair, side), ([0], pair, side),
    ]
    where = [[((far + step) % fars * 2 + p) * 2 + s for step in steps] for steps, p, s in plan]
    lefts = (basis, moved)
    if fars == 2 and height % 128 == 0:
        size = height
        index = jnp.stack([w[0] for w in where]).astype(jnp.int32)
    else:
        size = -(-len(away) * height // 128) * 128
        index = jnp.arange(len(plan), dtype=jnp.int32)

        def gathered(left):
            columns = []
            for w in where:
                columns += [lax.dynamic_slice_in_dim(left, i * height, height, 1) for i in w]
                columns.append(jnp.zeros((rows, size - len(w) * height), left.dtype))
            return jnp.concatenate(columns, 1)

        lefts = tuple(gathered(left) for left in lefts)

    ids = tuple(x.astype(jnp.int32)[None] for x in (sec, col, row))
    tables = (neighbours, mask)
    inner, begun = inner_rows(basis, own_ops, share, rest, tables, ids, lefts, index, size)
    from_before, from_after, swapped, begun = lax.optimization_barrier((from_before, from_after, swapped, begun))
    rim_part, far_a, near_a = rim_rows(
        basis, (from_before, from_after, split, swapped), own_ops, share, rest, tables, ids, lefts, index,
        size, begun,
    )
    swap_side = [(i, i ^ 1) for i in range(count)]
    swap_pair = [(i, i ^ 2) for i in range(count)]

    def take(unit, i):
        return unit[: len(plan[i][0]) * height]

    def add(first, *others):
        for other in others:
            first = first + other.astype(F32)
        return first

    def after(value, *earlier):
        return lax.optimization_barrier((value, *earlier))[0]

    far_a = lax.ppermute(take(far_a, 0), "row", swap_side)
    near_a = lax.ppermute(take(near_a, 1), "row", swap_pair)
    far_b, near_b = units(lefts, inner, rim_part, ids, index, 2, 2, size, BF16)
    third = units(lefts, inner, after(rim_part, far_b), ids, index, 4, 4, size, F32)
    far_b = lax.ppermute(take(far_b, 2), "row", swap_side)
    far_c = add(take(third[0], 4), far_a).astype(BF16)
    near_c = add(take(third[1], 5), after(near_a, far_c)).astype(BF16)
    near_b = lax.ppermute(after(take(near_b, 3), near_c), "row", swap_pair)
    far_c = lax.ppermute(far_c, "row", swap_pair)
    near_c = lax.ppermute(near_c, "row", swap_side)
    far_d = add(take(third[2], 6), far_b, far_c).astype(BF16)
    parts = []
    for i, step in enumerate(away):
        route = [(g, (g + 4 * step) % count) for g in range(count)]
        parts.append(lax.ppermute(far_d[i * height : (i + 1) * height], "row", route))
    total = add(take(third[3], 7), near_b, near_c, *parts)
    return total * (1.0 / math.sqrt(rows * count))


def solution(mesh):
    return jax.shard_map(
        per_device,
        mesh=mesh,
        in_specs=(P("row", "col"), P("row", None, "sec", None), P("row", None), P("row", None)),
        out_specs=P(("sec", "row"), "col"),
        check_vma=False,
    )
```

time: 555 us -> 174 us (0.31)
  waiting for transfers between devices: 421 us -> 90.4 us
  matrix products: 55.2 us -> 0 us
  Pallas kernels: 0 us -> 43.9 us
  local copies, waits for them, and re-layouts: 51.4 us -> 7.58 us
  starting transfers between devices: 6.27 us -> 26.7 us
  between operations: 13.2 us -> 0.11 us
    reduce_scatter x1 -> x0, waiting for transfers between devices: 284 us -> none  [per_device(): lax.psum_scatter(partial_tile, 'row', scatter_dimension=0, tiled=True)]
    all_gather x2 -> x0, waiting for transfers between devices: 94.5 us -> none  [the longest x1 70 us: per_device(): lax.all_gather(applied_half, 'sec', axis=1, tiled=True)]
    dot_general x8 -> x0, matrix products: 55.2 us -> none  [the longest x7 37.3 us: slot_product(): jnp.einsum('hol,hla->hoa', sparse_block_list, reduced_basis_tiles, prefer...]
    gather x7 -> x0, local copies, waits for them, and re-layouts: 48.6 us -> none  [per_device(): selected_entries = jnp.take(rim_tiles, offset_index[:, neighbour], axis=0)]
    ppermute x2 -> x14, waiting for transfers between devices: 42.3 us -> 90.4 us  [the longest x1 39.6 us: per_device(): near_b = lax.ppermute(after(take(near_b, 3), near_c), 'row', swap_pair)]
    pallas_call x0 -> x4, Pallas kernels: none -> 43.9 us  [call(): pl.pallas_call(kernel, grid_spec=pltpu.PrefetchScalarGridSpec(num_scalar_...]
    ppermute x2 -> x14, starting transfers between devices: 6.19 us -> 26.7 us  [the longest x1 5.48 us: per_device(): from_before = lax.ppermute(basis[rows - block:], 'row', up)]
    concatenate x1 -> x0, other arithmetic: 6.04 us -> none  [padded(): shard = jnp.concatenate([before, shard, after], axis=dim)]
  transfers between devices with their start and end apart: 5 -> 14, of which waited for: 4 -> 9; matrix products, arithmetic and copies ran while one was open for 0% -> 3% of each run, Pallas kernels for 0% -> 19%
where the time goes in v4:
time: 174 us
  waiting for transfers between devices  90.4 us (52%)
  Pallas kernels  43.9 us (25%)
  starting transfers between devices  26.7 us (15%)
  local copies, waits for them, and re-layouts  7.58 us (4%)
  other arithmetic  4.84 us (3%)
    pallas_call x4, Pallas kernels, call(): pl.pallas_call(kernel, grid_spec=pltpu.PrefetchScalarGridSpec(num_scalar_...  43.9 us
    ppermute x1, waiting for transfers between devices, per_device(): near_b = lax.ppermute(after(take(near_b, 3), near_c), 'row', swap_pair)  39.6 us
    ppermute x1, waiting for transfers between devices, per_device(): lax.ppermute(split, ('sec', 'row'), down + [(count + i, count + j) for i,...  14.2 us
    ppermute x1, waiting for transfers between devices, per_device(): far_c = lax.ppermute(far_c, 'row', swap_pair)  10.4 us
    ppermute x1, waiting for transfers between devices, per_device(): far_b = lax.ppermute(take(far_b, 2), 'row', swap_side)  8.05 us
    ppermute x1, waiting for transfers between devices, per_device(): from_before = lax.ppermute(basis[rows - block:], 'row', up)  7.22 us
    ppermute x1, waiting for transfers between devices, per_device(): near_a = lax.ppermute(take(near_a, 1), 'row', swap_pair)  6.74 us
    ppermute x1, starting transfers between devices, per_device(): from_before = lax.ppermute(basis[rows - block:], 'row', up)  5.48 us
  transfers between devices with their start and end apart: 14, of which 9 were waited for; matrix products, arithmetic and copies ran while one was open for 3% of the time, Pallas kernels for 19%

profile of v4, /device:TPU:0, one launch (start us, length us, event | category | flops | bytes accessed | tf_op | source)
XLA Modules:
  0.0 173.5 jit_solution(1911584531184249557)
XLA Ops:
  1.1 2.6 %fusion = (bf16[128,2048]{1,0:T(8,128)(2,1)}, bf16[128,2048]{1,0:T(8,128)(2,1)}, bf16[128,2048]{1,0:T(8,128)(2,1)S(1)}) fusion(bf16[1280,2048]{1,0:T(8,128)(2,1)} %here.3, s32[]{:T(128)S(6)} %select_n.50), kind=kLoop, calls=%fused_computation.6 | loop fusion | bytes 3145732 | tf_op jit(solution)/shard_map/slice | solution.py:186
  3.7 4.7 %collective-permute-start = (bf16[1280,2048]{1,0:T(8,128)(2,1)}, bf16[1280,2048]{1,0:T(8,128)(2,1)}, u32[]{:S(2)}, u32[]{:S(2)}) collective-permute-start(bf16[1280,2048]{1,0:T(8,128)(2,1)} %here.3), channel_id=1, source_target_pairs={{0,1},{17,16},{2,3},{19,18},{4,5},{21,20},{6,7},{23,22},{8,9},{25,... | collective-permute-start | bytes 15728648 | tf_op jit(solution)/shard_map/ppermute | solution.py:187
  8.4 1.3 collective-permute-start.2
  9.7 14.2 %collective-permute-done.2.split_ref = bf16[128,2048]{1,0:T(8,128)(2,1)S(1)} collective-permute-done((bf16[128,2048]{1,0:T(8,128)(2,1)S(1)}, bf16[128,2048]{1,0:T(8,128)(2,1)S(1)}, u32[]{:S(2)}, u32[]{:S(2)}) %collective-permute-start.2) | collective-permute-done | bytes 524320 | tf_op jit(solution)/shard_map/ppermute | solution.py:181
  23.9 1.3 collective-permute-start.3
  26.5 5.5 %collective-permute-start.4 = (bf16[128,2048]{1,0:T(8,128)(2,1)}, bf16[128,2048]{1,0:T(8,128)(2,1)S(1)}, u32[]{:S(2)}, u32[]{:S(2)}) collective-permute-start(bf16[128,2048]{1,0:T(8,128)(2,1)} %get-tuple-element.52), channel_id=1, source_target_pairs={{0,2},{2,4},{4,6},{6,8},{8,10},{10,12},{12,14},{1,3},{3,5},{5,7},{... | collective-permute-start | bytes 1572872 | tf_op jit(solution)/shard_map/ppermute | solution.py:185
  35.5 11.1 %inner_rows.1 = (bf16[768,2048]{1,0:T(8,128)(2,1)}, f32[2,256,2048]{2,1,0:T(8,128)}) custom-call(s32[10,7]{1,0:T(8,128)} %copy.5.nb_ref, s32[10,7]{1,0:T(8,128)} %copy.6.mask_ref, s32[1]{0:T(128)} %bitcast.sec_ref, s32[1]{0:T(128)} %bitcast.1.col_ref, s32[1]{0:T(128)} %bitcast.2.row_ref, s32[8]{0:T(128)} %stack.35.index_ref, bf16[1280,2048]{1,0:T(8,128)(2,1)} %here.3, ...), custom_call_target="tpu_custom_call" | custom-call | flops 4429185024 | bytes 28508160 | tf_op jit(solution)/shard_map/inner_rows/pallas_call | solution.py:17
  46.6 7.2 %collective-permute-done.4.up_ref = bf16[128,2048]{1,0:T(8,128)(2,1)S(1)} collective-permute-done((bf16[128,2048]{1,0:T(8,128)(2,1)}, bf16[128,2048]{1,0:T(8,128)(2,1)S(1)}, u32[]{:S(2)}, u32[]{:S(2)}) %collective-permute-start.4) | collective-permute-done | bytes 524320 | tf_op jit(solution)/shard_map/ppermute | solution.py:185
  54.9 10.5 %rim_rows.1 = (bf16[512,2048]{1,0:T(8,128)(2,1)}, bf16[256,2048]{1,0:T(8,128)(2,1)}, bf16[256,2048]{1,0:T(8,128)(2,1)}) custom-call(s32[10,7]{1,0:T(8,128)} %copy.5.nb_ref, s32[10,7]{1,0:T(8,128)} %copy.6.mask_ref, s32[1]{0:T(128)} %bitcast.sec_ref, s32[1]{0:T(128)} %bitcast.1.col_ref, s32[1]{0:T(128)} %bitcast.2.row_ref, s32[8]{0:T(128)} %stack.35.index_ref, ...), custom_call_target="tpu_custom_call" | custom-call | flops 2952790016 | bytes 45285376 | tf_op jit(solution)/shard_map/rim_rows/pallas_call | solution.py:17
  65.4 2.5 %collective-permute-start.8 = (bf16[256,2048]{1,0:T(8,128)(2,1)}, bf16[256,2048]{1,0:T(8,128)(2,1)S(1)}, u32[]{:S(2)}, u32[]{:S(2)}) collective-permute-start(bf16[256,2048]{1,0:T(8,128)(2,1)} %get-tuple-element.47), channel_id=1, source_target_pairs={{0,2},{2,0},{4,6},{6,4},{8,10},{10,8},{12,14},{14,12},{1,3},{3,1},... | collective-permute-start | bytes 3145736 | tf_op jit(solution)/shard_map/ppermute | solution.py:240
  67.9 8.4 %units.2 = (bf16[256,2048]{1,0:T(8,128)(2,1)}, bf16[256,2048]{1,0:T(8,128)(2,1)}) custom-call(s32[1]{0:T(128)} %bitcast.sec_ref, s32[1]{0:T(128)} %bitcast.1.col_ref, s32[1]{0:T(128)} %bitcast.2.row_ref, s32[8]{0:T(128)} %stack.35.index_ref, bf16[1280,2048]{1,0:T(8,128)(2,1)} %here.3, bf16[1280,2048]{1,0:T(8,128)(2,1)} %collective-permute-done.o0.o1.there, ...), custom_call_target="tpu_custom_call" | custom-call | flops 2684354560 | bytes 15728640 | tf_op jit(solution)/shard_map/units/pallas_call | solution.py:17
  76.4 1.6 collective-permute-start.7
  78.0 13.8 %units.3 = (f32[256,2048]{1,0:T(8,128)}, f32[256,2048]{1,0:T(8,128)}, f32[256,2048]{1,0:T(8,128)}, f32[256,2048]{1,0:T(8,128)}) custom-call(s32[1]{0:T(128)} %bitcast.sec_ref, s32[1]{0:T(128)} %bitcast.1.col_ref, s32[1]{0:T(128)} %bitcast.2.row_ref, s32[8]{0:T(128)} %stack.35.index_ref, bf16[1280,2048]{1,0:T(8,128)(2,1)} %here.3, ...), custom_call_target="tpu_custom_call" | custom-call | flops 5368709120 | bytes 15728640 | tf_op jit(solution)/shard_map/units/pallas_call | solution.py:17
  92.1 2.0 %add_convert_fusion.2 = bf16[256,2048]{1,0:T(8,128)(2,1)S(1)} fusion(f32[256,2048]{1,0:T(8,128)} %get-tuple-element.46, bf16[256,2048]{1,0:T(8,128)(2,1)S(1)} %collective-permute-done.8), kind=kLoop, calls=%fused_computation.3 | loop fusion | flops 1572864 | bytes 4194304 | tf_op jit(solution)/shard_map/convert_element_type | solution.py:245
  94.1 1.6 collective-permute-start.12
  95.7 6.7 %collective-permute-done.7 = bf16[256,2048]{1,0:T(8,128)(2,1)S(1)} collective-permute-done((bf16[256,2048]{1,0:T(8,128)(2,1)S(1)}, bf16[256,2048]{1,0:T(8,128)(2,1)S(1)}, u32[]{:S(2)}, u32[]{:S(2)}) %collective-permute-start.7) | collective-permute-done | bytes 1048608 | tf_op jit(solution)/shard_map/ppermute | solution.py:241
  102.8 2.1 %collective-permute-start.10 = (bf16[256,2048]{1,0:T(8,128)(2,1)S(1)}, bf16[256,2048]{1,0:T(8,128)(2,1)S(1)}, u32[]{:S(2)}, u32[]{:S(2)}) collective-permute-start(bf16[256,2048]{1,0:T(8,128)(2,1)S(1)} %add_convert_fusion.1), channel_id=1, source_target_pairs={{0,2},{2,0},{4,6},{6,4},{8,10},{10,8},{12,14},{14,12},{1,3},{3,1},... | collective-permute-start | bytes 3145736 | tf_op jit(solution)/shard_map/ppermute | solution.py:249
  104.9 1.6 collective-permute-start.9
  106.5 8.1 %collective-permute-done.11 = bf16[256,2048]{1,0:T(8,128)(2,1)S(1)} collective-permute-done((bf16[256,2048]{1,0:T(8,128)(2,1)}, bf16[256,2048]{1,0:T(8,128)(2,1)S(1)}, u32[]{:S(2)}, u32[]{:S(2)}) %collective-permute-start.11) | collective-permute-done | bytes 1048608 | tf_op jit(solution)/shard_map/ppermute | solution.py:244
  114.5 10.4 %collective-permute-done.12 = bf16[256,2048]{1,0:T(8,128)(2,1)S(1)} collective-permute-done((bf16[256,2048]{1,0:T(8,128)(2,1)S(1)}, bf16[256,2048]{1,0:T(8,128)(2,1)S(1)}, u32[]{:S(2)}, u32[]{:S(2)}) %collective-permute-start.12) | collective-permute-done | bytes 1048608 | tf_op jit(solution)/shard_map/ppermute | solution.py:248
  125.5 2.6 %collective-permute-start.13 = (bf16[256,2048]{1,0:T(8,128)(2,1)S(1)}, bf16[256,2048]{1,0:T(8,128)(2,1)S(1)}, u32[]{:S(2)}, u32[]{:S(2)}) collective-permute-start(bf16[256,2048]{1,0:T(8,128)(2,1)S(1)} %add_convert_fusion), channel_id=1, source_target_pairs={{0,8},{2,10},{4,12},{6,14},{8,0},{10,2},{12,4},{14,6},{1,9},{3,11}... | collective-permute-start | bytes 3145736 | tf_op jit(solution)/shard_map/ppermute | solution.py:254
  128.1 39.6 %collective-permute-done.9 = bf16[256,2048]{1,0:T(8,128)(2,1)S(1)} collective-permute-done((bf16[256,2048]{1,0:T(8,128)(2,1)S(1)}, bf16[256,2048]{1,0:T(8,128)(2,1)S(1)}, u32[]{:S(2)}, u32[]{:S(2)}) %collective-permute-start.9) | collective-permute-done | bytes 1048608 | tf_op jit(solution)/shard_map/ppermute | solution.py:247
  167.7 3.8 %collective-permute-done.13 = bf16[256,2048]{1,0:T(8,128)(2,1)S(1)} collective-permute-done((bf16[256,2048]{1,0:T(8,128)(2,1)S(1)}, bf16[256,2048]{1,0:T(8,128)(2,1)S(1)}, u32[]{:S(2)}, u32[]{:S(2)}) %collective-permute-start.13) | collective-permute-done | bytes 1048608 | tf_op jit(solution)/shard_map/ppermute | solution.py:254
  171.6 1.9 %add_multiply_fusion = f32[256,2048]{1,0:T(8,128)} fusion(bf16[256,2048]{1,0:T(8,128)(2,1)S(1)} %collective-permute-done.13, bf16[256,2048]{1,0:T(8,128)(2,1)S(1)} %collective-permute-done.10, f32[256,2048]{1,0:T(8,128)S(1)} %copy-done.2, bf16[256,2048]{1,0:T(8,128)(2,1)S(1)} %collective-permute-done.9), kind=kLoop, calls=%fused_computation | loop fusion | flops 3670016 | bytes 7340032 | tf_op jit(solution)/shard_map/mul | solution.py:256
  (43 shorter events, 8.2 us)
Async XLA Ops:
  0.0 32.6 %copy-start.9 = (s32[10,7]{0,1:T(8,128)S(1)}, s32[10,7]{0,1:T(8,128)}, u32[]{:S(2)}) copy-start(s32[10,7]{0,1:T(8,128)} %param.6) | copy-start | bytes 844
  0.0 33.3 %copy-start.10 = (s32[10,7]{0,1:T(8,128)S(1)}, s32[10,7]{0,1:T(8,128)}, u32[]{:S(2)}) copy-start(s32[10,7]{0,1:T(8,128)} %param.7) | copy-start | bytes 844
  3.7 31.0 %collective-permute-start = (bf16[1280,2048]{1,0:T(8,128)(2,1)}, bf16[1280,2048]{1,0:T(8,128)(2,1)}, u32[]{:S(2)}, u32[]{:S(2)}) collective-permute-start(bf16[1280,2048]{1,0:T(8,128)(2,1)} %here.3), channel_id=1, source_target_pairs={{0,1},{17,16},{2,3},{19,18},{4,5},{21,20},{6,7},{23,22},{8,9},{25,... | collective-permute-start | bytes 15728648 | tf_op jit(solution)/shard_map/ppermute | solution.py:187
  8.4 15.5 %collective-permute-start.1 = (bf16[5,7,64,128]{3,2,1,0:T(8,128)(2,1)S(1)}, bf16[5,7,64,128]{3,2,1,0:T(8,128)(2,1)S(1)}, u32[]{:S(2)}, u32[]{:S(2)}) collective-permute-start(bf16[5,7,64,128]{3,2,1,0:T(8,128)(2,1)S(1)} %constant_dynamic-slice_fusion), channel_id=1, source_target_pairs={{0,16},{16,0},{1,17},{17,1},{2,18},{18,2},{3,19},{19,3},{4,20},{20... | collective-permute-start | bytes 1720328 | tf_op jit(solution)/shard_map/ppermute | solution.py:184
  8.4 15.5 %collective-permute-start.2 = (bf16[128,2048]{1,0:T(8,128)(2,1)S(1)}, bf16[128,2048]{1,0:T(8,128)(2,1)S(1)}, u32[]{:S(2)}, u32[]{:S(2)}) collective-permute-start(bf16[128,2048]{1,0:T(8,128)(2,1)S(1)} %get-tuple-element.30), channel_id=1, source_target_pairs={{2,0},{4,2},{6,4},{8,6},{10,8},{12,10},{14,12},{16,18},{18,20},{20... | collective-permute-start | bytes 1572872 | tf_op jit(solution)/shard_map/ppermute | solution.py:181
  23.8 22.8 %copy-start.5 = (bf16[128,2048]{1,0:T(8,128)(2,1)}, bf16[128,2048]{1,0:T(8,128)(2,1)S(1)}, u32[]{:S(2)}) copy-start(bf16[128,2048]{1,0:T(8,128)(2,1)S(1)} %collective-permute-done.2.split_ref) | copy-start | bytes 1572868
  23.9 10.8 %copy-start = (bf16[5,7,64,128]{3,2,1,0:T(8,128)(2,1)}, bf16[5,7,64,128]{3,2,1,0:T(8,128)(2,1)S(1)}, u32[]{:S(2)}) copy-start(bf16[5,7,64,128]{3,2,1,0:T(8,128)(2,1)S(1)} %collective-permute-done.1.share_ref) | copy-start | bytes 1720324
  23.9 10.7 %collective-permute-start.3 = (bf16[5,7,64,128]{3,2,1,0:T(8,128)(2,1)S(1)}, bf16[5,7,64,128]{3,2,1,0:T(8,128)(2,1)S(1)}, u32[]{:S(2)}, u32[]{:S(2)}) collective-permute-start(bf16[5,7,64,128]{3,2,1,0:T(8,128)(2,1)S(1)} %collective-permute-done.1.share_ref), channel_id=1, source_target_pairs={{0,1},{1,0},{2,3},{3,2},{4,5},{5,4},{6,7},{7,6},{8,9},{9,8},{10,11... | collective-permute-start | bytes 1720328 | tf_op jit(solution)/shard_map/ppermute | solution.py:189
  25.3 21.4 %collective-permute-start.5 = (bf16[128,2048]{1,0:T(8,128)(2,1)}, bf16[128,2048]{1,0:T(8,128)(2,1)S(1)}, u32[]{:S(2)}, u32[]{:S(2)}) collective-permute-start(bf16[128,2048]{1,0:T(8,128)(2,1)} %get-tuple-element.51), channel_id=1, source_target_pairs={{2,0},{4,2},{6,4},{8,6},{10,8},{12,10},{14,12},{3,1},{5,3},{7,5},{... | collective-permute-start | bytes 1572872 | tf_op jit(solution)/shard_map/ppermute | solution.py:186
  26.5 27.3 %collective-permute-start.4 = (bf16[128,2048]{1,0:T(8,128)(2,1)}, bf16[128,2048]{1,0:T(8,128)(2,1)S(1)}, u32[]{:S(2)}, u32[]{:S(2)}) collective-permute-start(bf16[128,2048]{1,0:T(8,128)(2,1)} %get-tuple-element.52), channel_id=1, source_target_pairs={{0,2},{2,4},{4,6},{6,8},{8,10},{10,12},{12,14},{1,3},{3,5},{5,7},{... | collective-permute-start | bytes 1572872 | tf_op jit(solution)/shard_map/ppermute | solution.py:185
  32.0 21.8 %collective-permute-start.6 = (bf16[128,2048]{1,0:T(8,128)(2,1)S(1)}, bf16[128,2048]{1,0:T(8,128)(2,1)S(1)}, u32[]{:S(2)}, u32[]{:S(2)}) collective-permute-start(bf16[128,2048]{1,0:T(8,128)(2,1)S(1)} %collective-permute-done.2.split_ref), channel_id=1, source_target_pairs={{0,16},{16,0},{1,17},{17,1},{2,18},{18,2},{3,19},{19,3},{4,20},{20... | collective-permute-start | bytes 1572872 | tf_op jit(solution)/shard_map/ppermute | solution.py:190
  46.6 7.2 %copy-start.6 = (bf16[128,2048]{1,0:T(8,128)(2,1)}, bf16[128,2048]{1,0:T(8,128)(2,1)S(1)}, u32[]{:S(2)}) copy-start(bf16[128,2048]{1,0:T(8,128)(2,1)S(1)} %collective-permute-done.5.down_ref) | copy-start | bytes 1572868
  65.4 26.6 %collective-permute-start.8 = (bf16[256,2048]{1,0:T(8,128)(2,1)}, bf16[256,2048]{1,0:T(8,128)(2,1)S(1)}, u32[]{:S(2)}, u32[]{:S(2)}) collective-permute-start(bf16[256,2048]{1,0:T(8,128)(2,1)} %get-tuple-element.47), channel_id=1, source_target_pairs={{0,2},{2,0},{4,6},{6,4},{8,10},{10,8},{12,14},{14,12},{1,3},{3,1},... | collective-permute-start | bytes 3145736 | tf_op jit(solution)/shard_map/ppermute | solution.py:240
  67.9 8.5 %copy-start.12 = (bf16[256,2048]{1,0:T(8,128)(2,1)S(1)}, bf16[256,2048]{1,0:T(8,128)(2,1)}, u32[]{:S(2)}) copy-start(bf16[256,2048]{1,0:T(8,128)(2,1)} %get-tuple-element.45) | copy-start | bytes 3145732
  76.3 38.2 %collective-permute-start.11 = (bf16[256,2048]{1,0:T(8,128)(2,1)}, bf16[256,2048]{1,0:T(8,128)(2,1)S(1)}, u32[]{:S(2)}, u32[]{:S(2)}) collective-permute-start(bf16[256,2048]{1,0:T(8,128)(2,1)} %get-tuple-element.40), channel_id=1, source_target_pairs={{0,2},{2,0},{4,6},{6,4},{8,10},{10,8},{12,14},{14,12},{1,3},{3,1},... | collective-permute-start | bytes 3145736 | tf_op jit(solution)/shard_map/ppermute | solution.py:244
  76.4 26.1 %collective-permute-start.7 = (bf16[256,2048]{1,0:T(8,128)(2,1)S(1)}, bf16[256,2048]{1,0:T(8,128)(2,1)S(1)}, u32[]{:S(2)}, u32[]{:S(2)}) collective-permute-start(bf16[256,2048]{1,0:T(8,128)(2,1)S(1)} %copy-done.12), channel_id=1, source_target_pairs={{0,4},{2,6},{4,0},{6,2},{8,12},{10,14},{12,8},{14,10},{1,5},{3,7},... | collective-permute-start | bytes 3145736 | tf_op jit(solution)/shard_map/ppermute | solution.py:241
  92.0 10.4 %copy-start.4 = (f32[256,2048]{1,0:T(8,128)S(1)}, f32[256,2048]{1,0:T(8,128)}, u32[]{:S(2)}) copy-start(f32[256,2048]{1,0:T(8,128)} %get-tuple-element.44) | copy-start | bytes 6291460
  94.1 30.9 %collective-permute-start.12 = (bf16[256,2048]{1,0:T(8,128)(2,1)S(1)}, bf16[256,2048]{1,0:T(8,128)(2,1)S(1)}, u32[]{:S(2)}, u32[]{:S(2)}) collective-permute-start(bf16[256,2048]{1,0:T(8,128)(2,1)S(1)} %add_convert_fusion.2), channel_id=1, source_target_pairs={{0,4},{2,6},{4,0},{6,2},{8,12},{10,14},{12,8},{14,10},{1,5},{3,7},... | collective-permute-start | bytes 3145736 | tf_op jit(solution)/shard_map/ppermute | solution.py:248
  102.5 2.4 %copy-start.11 = (bf16[256,2048]{1,0:T(8,128)(2,1)S(1)}, bf16[256,2048]{1,0:T(8,128)(2,1)}, u32[]{:S(2)}) copy-start(bf16[256,2048]{1,0:T(8,128)(2,1)} %get-tuple-element.49) | copy-start | bytes 3145732
  102.5 22.5 %copy-start.3 = (f32[256,2048]{1,0:T(8,128)S(1)}, f32[256,2048]{1,0:T(8,128)}, u32[]{:S(2)}) copy-start(f32[256,2048]{1,0:T(8,128)} %get-tuple-element.50) | copy-start | bytes 6291460
  102.8 64.9 %collective-permute-start.10 = (bf16[256,2048]{1,0:T(8,128)(2,1)S(1)}, bf16[256,2048]{1,0:T(8,128)(2,1)S(1)}, u32[]{:S(2)}, u32[]{:S(2)}) collective-permute-start(bf16[256,2048]{1,0:T(8,128)(2,1)S(1)} %add_convert_fusion.1), channel_id=1, source_target_pairs={{0,2},{2,0},{4,6},{6,4},{8,10},{10,8},{12,14},{14,12},{1,3},{3,1},... | collective-permute-start | bytes 3145736 | tf_op jit(solution)/shard_map/ppermute | solution.py:249
  104.9 62.9 %collective-permute-start.9 = (bf16[256,2048]{1,0:T(8,128)(2,1)S(1)}, bf16[256,2048]{1,0:T(8,128)(2,1)S(1)}, u32[]{:S(2)}, u32[]{:S(2)}) collective-permute-start(bf16[256,2048]{1,0:T(8,128)(2,1)S(1)} %copy-done.11), channel_id=1, source_target_pairs={{0,4},{2,6},{4,0},{6,2},{8,12},{10,14},{12,8},{14,10},{1,5},{3,7},... | collective-permute-start | bytes 3145736 | tf_op jit(solution)/shard_map/ppermute | solution.py:247
  124.9 46.7 %copy-start.2 = (f32[256,2048]{1,0:T(8,128)S(1)}, f32[256,2048]{1,0:T(8,128)}, u32[]{:S(2)}) copy-start(f32[256,2048]{1,0:T(8,128)} %get-tuple-element.42) | copy-start | bytes 6291460
  125.5 46.1 %collective-permute-start.13 = (bf16[256,2048]{1,0:T(8,128)(2,1)S(1)}, bf16[256,2048]{1,0:T(8,128)(2,1)S(1)}, u32[]{:S(2)}, u32[]{:S(2)}) collective-permute-start(bf16[256,2048]{1,0:T(8,128)(2,1)S(1)} %add_convert_fusion), channel_id=1, source_target_pairs={{0,8},{2,10},{4,12},{6,14},{8,0},{10,2},{12,4},{14,6},{1,9},{3,11}... | collective-permute-start | bytes 3145736 | tf_op jit(solution)/shard_map/ppermute | solution.py:254
  (3 other events, 2.7 us)

commit v5 on v4

v5 whole, which is shorter than its diff:
```python
import math

import jax
import jax.numpy as jnp
from jax import lax
from jax.experimental import pallas as pl
from jax.experimental.pallas import tpu as pltpu
from jax.sharding import PartitionSpec as P

REACH = 2
VMEM_LIMIT = 32 * 1024 * 1024
F32, BF16 = jnp.float32, jnp.bfloat16


def call(kernel, scalars, grid, in_specs, operands, out_specs, out_shape, scratch, name):
    return pl.pallas_call(
        kernel,
        grid_spec=pltpu.PrefetchScalarGridSpec(
            num_scalar_prefetch=len(scalars), grid=grid, in_specs=in_specs,
            out_specs=out_specs, scratch_shapes=scratch,
        ),
        out_shape=out_shape,
        compiler_params=pltpu.CompilerParams(vmem_limit_bytes=VMEM_LIMIT),
        cost_estimate=pl.CostEstimate(flops=1, bytes_accessed=1, transcendentals=0),
        name=name,
    )(*scalars, *operands)


def fixed(array):
    return pl.BlockSpec(array.shape, lambda j, *_: (0,) * array.ndim)


def transposed_dot(left, right):
    return lax.dot_general(left, right, (((0,), (0,)), ((), ())), preferred_element_type=F32)


def masked(b, mask_ref, halves, slots):
    rows = []
    for i in range(2):
        parts = [halves(s)[i] * mask_ref[b, s].astype(F32).astype(BF16) for s in range(slots)]
        rows.append(jnp.concatenate(parts, axis=1))
    return rows


def gathered_rows(b, shift, nb_ref, first, rows_ref, block):
    return jnp.concatenate(
        [
            rows_ref[pl.ds(pl.multiple_of((nb_ref[b, s] - first + shift) * block, block), block), :]
            for s in range(nb_ref.shape[1])
        ],
        axis=0,
    )


def inner_rows(basis, own_ops, share, rest, tables, ids, lefts, index, size):
    rows, width = basis.shape
    blocks, slots, half, block = own_ops.shape
    part, rim, tile = blocks // 2, REACH * block, width // 2

    def kernel(nb_ref, mask_ref, sec_ref, col_ref, row_ref, index_ref, rows_ref, own_ref, *refs):
        shares, rests, (m0, o0, m1, o1, out_ref, unit_ref, ops_ref) = refs[:2], refs[2:4], refs[4:]
        split = shares[0].shape[0]
        mine, sec = sec_ref[0] == col_ref[0], sec_ref[0]

        def operator(b):
            def halves(s):
                piece, at = (0, b % part) if b % part < split else (1, b % part - split)
                other = jnp.where(col_ref[0] == b // part, shares[piece][at, s], rests[piece][at, s])
                return own_ref[b, s], other

            return masked(b, mask_ref, halves, slots)

        @pl.when(pl.program_id(0) == 0)
        def _():
            for i, b in enumerate((0, 1, blocks - 2, blocks - 1)):
                own, other = operator(b)
                ops_ref[i, pl.ds(pl.multiple_of(sec * half, half), half), :] = own
                ops_ref[i, pl.ds(pl.multiple_of((1 - sec) * half, half), half), :] = other

        for b in range(REACH, blocks - REACH):
            total = jnp.dot(
                jnp.concatenate(operator(b), axis=0),
                gathered_rows(b, 0, nb_ref, row_ref[0] * blocks, rows_ref, block),
                preferred_element_type=F32,
            ).astype(BF16)
            for i, place in enumerate((sec, 1 - sec)):
                start = pl.multiple_of((b - REACH) * block + place * half, half)
                out_ref[0, pl.ds(start, half), :] = total[i * half : (i + 1) * half]
        for u, (here, there) in enumerate(((m0, o0), (m1, o1))):
            left = jnp.where(mine, here[rim : rows - rim, :], there[rim : rows - rim, :])
            unit_ref[0, u] = transposed_dot(left, out_ref[0])

    unit = [pl.BlockSpec((rows, size), lambda j, *s, u=u: (0, s[5][u])) for u in (0, 0, 1, 1)]
    ops = jax.ShapeDtypeStruct((2 * REACH, block, slots * block), BF16)
    inner = rows - 2 * rim
    return call(
        kernel, (*tables, *ids, index), (2,),
        [pl.BlockSpec((rows, tile), lambda j, *_: (0, j)), fixed(own_ops), *map(fixed, (*share, *rest))] + unit,
        (basis, own_ops, *share, *rest, *lefts, *lefts),
        [pl.BlockSpec((1, inner, tile), lambda j, *_: (j, 0, 0)),
         pl.BlockSpec((1, 2, size, tile), lambda j, *_: (j, 0, 0, 0)), fixed(ops)],
        [jax.ShapeDtypeStruct((2, inner, tile), BF16), jax.ShapeDtypeStruct((2, 2, size, tile), F32), ops],
        [], "inner_rows",
    )


def rim_rows(part, basis, halos, ops, tables, ids, lefts, index, size, begun):
    rows, width = basis.shape
    block = halos[0].shape[0]
    rim = REACH * block
    blocks = rows // block
    steps = 2
    tile = width // 2 // steps

    def kernel(nb_ref, mask_ref, sec_ref, col_ref, row_ref, index_ref, up_ref, down_ref, split_ref, swapped_ref,
               head_ref, tail0_ref, tail1_ref, ops_ref, *refs):
        left_refs, (begun_ref, out_ref, *unit_refs, ext) = refs[:8], refs[8:]
        mine, lower = sec_ref[0] == col_ref[0], sec_ref[0] == 0
        split, swapped = split_ref[...], swapped_ref[...]
        ext[:block, :] = jnp.where(lower, swapped, split)
        ext[block:rim, :] = up_ref[...]
        ext[rim : 3 * rim, :] = head_ref[...]
        ext[3 * rim : 4 * rim, :] = tail0_ref[...]
        ext[4 * rim : 5 * rim, :] = tail1_ref[...]
        ext[5 * rim : 5 * rim + block, :] = down_ref[...]
        ext[5 * rim + block :, :] = jnp.where(lower, split, swapped)
        for i, b in enumerate((0, 1, blocks - 2, blocks - 1)):
            shift = REACH if b < REACH else 5 * REACH - blocks
            out_ref[i * block : (i + 1) * block, :] = jnp.dot(
                ops_ref[i],
                gathered_rows(b, shift, nb_ref, row_ref[0] * blocks, ext, block),
                preferred_element_type=F32,
            ).astype(BF16)
        for u, unit_ref in enumerate(unit_refs):
            total = begun_ref[0, u]
            for i in range(2):
                here, there = left_refs[4 * u + 2 * i : 4 * u + 2 * i + 2]
                left = jnp.where(mine, here[...], there[...])
                total = total + transposed_dot(left, out_ref[i * rim : (i + 1) * rim, :])
            unit_ref[...] = total.astype(BF16)

    last = rows // rim - 1
    unit = [
        pl.BlockSpec((rim, size), lambda j, *s, u=u, at=at: (at, s[5][u]))
        for u in range(2) for at in (0, last) for _ in range(2)
    ]

    def across(height, at=0):
        return pl.BlockSpec((height, tile), lambda j, *_: (at, part * steps + j))

    def out(height):
        return pl.BlockSpec((height, tile), lambda j, *_: (0, j))

    return call(
        kernel, (*tables, *ids, index), (steps,),
        [across(block)] * 4 + [across(2 * rim), across(rim, last - 1), across(rim, last), fixed(ops)]
        + unit + [pl.BlockSpec((1, 2, size, tile), lambda j, *_: (part, 0, 0, j))],
        (*halos, basis, basis, basis, ops, *(lefts * 4), begun),
        [out(2 * rim), out(size), out(size)],
        [jax.ShapeDtypeStruct((2 * rim, width // 2), BF16)]
        + [jax.ShapeDtypeStruct((size, width // 2), BF16)] * 2,
        [pltpu.VMEM((6 * rim, tile), BF16)], "rim_rows",
    )


def units(part, which, lefts, inner, rim_part, ids, index, size, dtype):
    rows = lefts[0].shape[0]
    width = inner.shape[2]
    rim = rim_part.shape[0] // 2
    first, count = which[0], len(which)
    assert list(which) == list(range(first, first + count))

    def kernel(sec_ref, col_ref, row_ref, index_ref, here, there, inner_ref, rim_ref, *out_refs):
        left = jnp.where(sec_ref[0] == col_ref[0], here[...], there[...])
        total = (
            transposed_dot(left[rim : rows - rim], inner_ref[0])
            + transposed_dot(left[:rim], rim_ref[:rim, :])
            + transposed_dot(left[rows - rim :], rim_ref[rim:, :])
        ).astype(dtype)
        for u, out_ref in enumerate(out_refs):
            @pl.when(pl.program_id(0) == u)
            def _(out_ref=out_ref):
                out_ref[...] = total

    unit = pl.BlockSpec((rows, size), lambda u, *s: (0, s[3][first + u]))
    return call(
        kernel, (*ids, index), (count,),
        [unit, unit, pl.BlockSpec((1, *inner.shape[1:]), lambda u, *_: (part, 0, 0)), fixed(rim_part)],
        (*lefts, inner, rim_part),
        [pl.BlockSpec((size, width), lambda u, *_: (0, 0))] * count,
        [jax.ShapeDtypeStruct((size, width), dtype)] * count, [], "units",
    )


def finish(halves, scale):
    height, width = halves[0][0].shape
    count = len(halves[0])

    def kernel(*refs):
        for part, chosen in enumerate((refs[:count], refs[count:-1])):
            @pl.when(pl.program_id(0) == part)
            def _(chosen=chosen):
                total = chosen[0][...]
                for ref in chosen[1:]:
                    total = total + ref[...].astype(F32)
                refs[-1][...] = total * scale

    operands = [x for half in halves for x in half]
    return call(
        kernel, (), (2,), [fixed(x) for x in operands], operands,
        pl.BlockSpec((height, width), lambda j: (0, j)),
        jax.ShapeDtypeStruct((height, 2 * width), F32), [], "finish",
    )


def per_device(basis, own_ops, neighbours, mask):
    rows, width = basis.shape
    blocks, slots, half, block = own_ops.shape
    sec, row, col = (lax.axis_index(name) for name in ("sec", "row", "col"))
    count = lax.axis_size("row")
    rim = REACH * block
    swap = [(0, 1), (1, 0)]
    up = [(i, (i + 1) % count) for i in range(count)]
    down = [(j, i) for i, j in up]

    def after(value, *earlier):
        return lax.optimization_barrier((value, earlier))[0]

    split = lax.dynamic_slice_in_dim(basis, block + sec * (rows - 3 * block), block, 0)
    behind = after(basis, split)
    split = lax.ppermute(split, ("sec", "row"), down + [(count + i, count + j) for i, j in up])
    part = blocks // 2
    cuts = (0, part // 2, part)
    share = [
        lax.dynamic_slice_in_dim(own_ops, col * part + i, j - i, 0) for i, j in zip(cuts, cuts[1:])
    ]
    behind = after(behind, share)
    share = [lax.ppermute(x, "sec", swap) for x in share]
    from_before = lax.ppermute(behind[rows - block :], "row", up)
    from_after = lax.ppermute(behind[:block], "row", down)
    moved = lax.ppermute(behind, "col", swap)
    rest = [lax.ppermute(x, "col", swap) for x in share]
    swapped = lax.ppermute(split, "sec", swap)

    height = width * lax.axis_size("col") // lax.axis_size("sec") // count
    fars = count // 4
    far, pair, side = row // 4, row // 2 % 2, row % 2
    away = list(range(1, fars))
    plan = [
        (away, 1 - pair, 1 - side), ([0], 1 - pair, 1 - side), (away, pair, 1 - side), ([0], 1 - pair, side),
        (away, 1 - pair, side), ([0], pair, 1 - side), (away, pair, side), ([0], pair, side),
    ]
    where = [[((far + step) % fars * 2 + p) * 2 + s for step in steps] for steps, p, s in plan]
    lefts = (basis, moved)
    if fars == 2 and height % 128 == 0:
        size = height
        index = jnp.stack([w[0] for w in where]).astype(jnp.int32)
    else:
        size = -(-len(away) * height // 128) * 128
        index = jnp.arange(len(plan), dtype=jnp.int32)

        def gathered(left):
            columns = []
            for w in where:
                columns += [lax.dynamic_slice_in_dim(left, i * height, height, 1) for i in w]
                columns.append(jnp.zeros((rows, size - len(w) * height), left.dtype))
            return jnp.concatenate(columns, 1)

        lefts = tuple(gathered(left) for left in lefts)

    ids = tuple(x.astype(jnp.int32)[None] for x in (sec, col, row))
    tables = (neighbours, mask)
    inner, begun, ops = inner_rows(basis, own_ops, share, rest, tables, ids, lefts, index, size)
    halos = (from_before, from_after, split, swapped)
    swap_side = [(i, i ^ 1) for i in range(count)]
    swap_pair = [(i, i ^ 2) for i in range(count)]

    def rim_half(part, halos):
        rim_part, a, b = rim_rows(part, basis, halos, ops, tables, ids, lefts, index, size, begun)
        return rim_part, a[: len(away) * height], b[:height]

    def unit_half(part, which, rim_part, dtype):
        made = units(part, which, lefts, inner, rim_part, ids, index, size, dtype)
        return [x[: len(plan[i][0]) * height] for i, x in zip(which, made)]

    def to_side(x):
        return lax.ppermute(x, "row", swap_side)

    def to_pair(x):
        return lax.ppermute(x, "row", swap_pair)

    def to_far(x):
        parts = []
        for i, step in enumerate(away):
            route = [(g, (g + 4 * step) % count) for g in range(count)]
            parts.append(lax.ppermute(x[i * height : (i + 1) * height], "row", route))
        return parts

    def add32(first, *others):
        for other in others:
            first = first + other.astype(F32)
        return first

    def add(first, *others):
        return add32(first, *others).astype(BF16)

    rim0, far_a0, near_a0 = rim_half(0, halos)
    far_a0, near_a0 = to_side(far_a0), to_pair(near_a0)
    far_b0, near_b0 = unit_half(0, (2, 3), rim0, BF16)
    far_b0 = to_side(far_b0)
    rim1, far_a1, near_a1 = rim_half(1, (after(halos[0], near_b0), *halos[1:]))
    far_a1 = to_side(far_a1)
    far_c0, near_c0, far_d0, own0 = unit_half(0, (4, 5, 6, 7), after(rim0, rim1), F32)
    far_c0 = add(far_c0, far_a0)
    near_c0 = add(near_c0, after(near_a0, far_c0))
    far_c0 = to_pair(far_c0)
    near_b0 = to_pair(after(near_b0, near_c0))
    late1 = after(rim1, near_c0)
    (far_b1,) = unit_half(1, (2,), late1, BF16)
    near_b1, far_c1, near_c1, far_d1, own1 = unit_half(1, (3, 4, 5, 6, 7), after(late1, far_b1), F32)
    far_b1 = to_side(far_b1)
    near_a1 = to_side(after(near_a1, far_c1))
    far_d0 = add(far_d0, after(far_b0, far_c1), far_c0)
    far_c1 = add(far_c1, after(far_a1, far_d0))
    far_d0 = to_far(far_d0)
    own0 = add32(own0, after(near_b0, far_c1), *far_d0)
    near_c0, near_c1 = after((near_c0, near_c1), far_c1)
    far_c1 = to_pair(far_c1)
    far_d1 = add(far_d1, after(far_b1, own0), far_c1)
    near_b1 = add(near_b1, after(near_a1, far_d1))
    far_d1 = to_far(far_d1)
    own1 = add32(own1, *after(far_d1, near_b1))
    near_b1 = to_pair(near_b1)
    near_c0 = to_side(near_c0)
    near_c1 = to_side(near_c1.astype(BF16))
    near_b1, near_c0, near_c1 = after((near_b1, near_c0, near_c1), own1)
    return finish(
        ((own0, near_c0), (own1, near_b1, near_c1)), 1.0 / math.sqrt(rows * count)
    )


def solution(mesh):
    return jax.shard_map(
        per_device,
        mesh=mesh,
        in_specs=(P("row", "col"), P("row", None, "sec", None), P("row", None), P("row", None)),
        out_specs=P(("sec", "row"), "col"),
        check_vma=False,
    )
```

time: 174 us -> 144 us (0.83)
  waiting for transfers between devices: 90.4 us -> 54 us
  starting transfers between devices: 26.7 us -> 39.1 us
  Pallas kernels: 43.9 us -> 38.6 us
  other arithmetic: 4.84 us -> 1.54 us
  local copies, waits for them, and re-layouts: 7.58 us -> 9.8 us
    ppermute x12 -> x21, waiting for transfers between devices: 76.3 us -> 52.6 us  [the longest x5 23.9 us: to_pair(): return lax.ppermute(x, 'row', swap_pair)]
    ppermute x1, waiting for transfers between devices: 14.2 us -> 1.42 us  [per_device(): lax.ppermute(split, ('sec', 'row'), down + [(count + i, count + j) for i,...]
    ppermute x12 -> x21, starting transfers between devices: 24.8 us -> 34 us  [the longest x7 10.4 us: to_side(): return lax.ppermute(x, 'row', swap_side)]
    pallas_call x4 -> x8, Pallas kernels: 43.9 us -> 38.6 us  [call(): pl.pallas_call(kernel, grid_spec=pltpu.PrefetchScalarGridSpec(num_scalar_...]
    ppermute x1, starting transfers between devices: 1.28 us -> 4.53 us  [per_device(): lax.ppermute(split, ('sec', 'row'), down + [(count + i, count + j) for i,...]
    dynamic_slice x1 -> x3, local copies, waits for them, and re-layouts: 1.12 us -> 3.14 us  [the longest x2 2.05 us: per_device(): lax.dynamic_slice_in_dim(own_ops, col * part + i, j - i, 0)]
    mul x1 -> x0, other arithmetic: 1.94 us -> none  [per_device(): return total * (1.0 / math.sqrt(rows * count))]
    convert_element_type x3 -> x7, other arithmetic: 2.9 us -> 1.12 us  [the longest x6 1.05 us: add(): return add32(first, *others).astype(BF16)]
  transfers between devices with their start and end apart: 14 -> 23, of which waited for: 9 -> 10; matrix products, arithmetic and copies ran while one was open for 3% -> 3% of each run, Pallas kernels for 19% -> 23%
where the time goes in v5:
time: 144 us; the launch traced here: 143 us
  waiting for transfers between devices  54 us (38%)
  starting transfers between devices  39.1 us (27%)
  Pallas kernels  38.6 us (27%)
  local copies, waits for them, and re-layouts  9.8 us (7%)
  other arithmetic  1.54 us (1%)
    pallas_call x8, Pallas kernels, call(): pl.pallas_call(kernel, grid_spec=pltpu.PrefetchScalarGridSpec(num_scalar_...  38.6 us
    ppermute x5, waiting for transfers between devices, to_pair(): return lax.ppermute(x, 'row', swap_pair)  23.9 us
    ppermute x2, waiting for transfers between devices, to_far(): parts.append(lax.ppermute(x[i * height:(i + 1) * height], 'row', route))  18 us
    ppermute x7, starting transfers between devices, to_side(): return lax.ppermute(x, 'row', swap_side)  10.4 us
    ppermute x2, starting transfers between devices, to_far(): parts.append(lax.ppermute(x[i * height:(i + 1) * height], 'row', route))  8.88 us
    ppermute x5, starting transfers between devices, to_pair(): return lax.ppermute(x, 'row', swap_pair)  5.48 us
    ppermute x1, starting transfers between devices, per_device(): from_after = lax.ppermute(behind[:block], 'row', down)  5.23 us
    ppermute x1, starting transfers between devices, per_device(): lax.ppermute(split, ('sec', 'row'), down + [(count + i, count + j) for i,...  4.53 us
  transfers between devices with their start and end apart: 23, of which 10 were waited for; matrix products, arithmetic and copies ran while one was open for 3% of the time, Pallas kernels for 23%

profile of v5, /device:TPU:0, one launch (start us, length us, event | category | flops | bytes accessed | tf_op | source)
XLA Modules:
  0.0 143.3 jit_solution(9973963406656879011)
XLA Ops:
  3.7 2.6 %collective-permute-start.1 = (bf16[2,7,64,128]{3,2,1,0:T(8,128)(2,1)S(1)}, bf16[2,7,64,128]{3,2,1,0:T(8,128)(2,1)S(1)}, u32[]{:S(2)}, u32[]{:S(2)}) collective-permute-start(bf16[2,7,64,128]{3,2,1,0:T(8,128)(2,1)S(1)} %constant_dynamic-slice_fusion.1), channel_id=1, source_target_pairs={{0,16},{16,0},{1,17},{17,1},{2,18},{18,2},{3,19},{19,3},{4,20},{20... | collective-permute-start | bytes 688136 | tf_op jit(solution)/shard_map/ppermute | solution.py:238
  6.3 4.5 %collective-permute-start.7 = (bf16[128,2048]{1,0:T(8,128)(2,1)S(1)}, bf16[128,2048]{1,0:T(8,128)(2,1)S(1)}, u32[]{:S(2)}, u32[]{:S(2)}) collective-permute-start(bf16[128,2048]{1,0:T(8,128)(2,1)S(1)} %constant_dynamic-slice_fusion.2), channel_id=1, source_target_pairs={{2,0},{4,2},{6,4},{8,6},{10,8},{12,10},{14,12},{0,14},{16,18},{18,... | collective-permute-start | bytes 1572872 | tf_op jit(solution)/shard_map/ppermute | solution.py:231
  12.5 2.3 %fusion = (bf16[128,2048]{1,0:T(8,128)(2,1)}, bf16[128,2048]{1,0:T(8,128)(2,1)}) fusion(bf16[1280,2048]{1,0:T(8,128)(2,1)} %here.7), kind=kLoop, calls=%fused_computation.11 | loop fusion | bytes 2097152 | tf_op jit(solution)/shard_map/slice | solution.py:240
  14.7 5.2 %collective-permute-start.6 = (bf16[128,2048]{1,0:T(8,128)(2,1)}, bf16[128,2048]{1,0:T(8,128)(2,1)S(1)}, u32[]{:S(2)}, u32[]{:S(2)}) collective-permute-start(bf16[128,2048]{1,0:T(8,128)(2,1)} %get-tuple-element.85), channel_id=1, source_target_pairs={{2,0},{4,2},{6,4},{8,6},{10,8},{12,10},{14,12},{0,14},{3,1},{5,3},... | collective-permute-start | bytes 1572872 | tf_op jit(solution)/shard_map/ppermute | solution.py:240
  24.6 1.7 %collective-permute-done.4.refs_3_ = bf16[3,7,64,128]{3,2,1,0:T(8,128)(2,1)} collective-permute-done((bf16[3,7,64,128]{3,2,1,0:T(8,128)(2,1)}, bf16[3,7,64,128]{3,2,1,0:T(8,128)(2,1)}, u32[]{:S(2)}, u32[]{:S(2)}) %collective-permute-start.4) | collective-permute-done | bytes 344096 | tf_op jit(solution)/shard_map/ppermute | solution.py:242
  26.4 2.5 %copy-done = bf16[1280,2048]{1,0:T(8,128)(2,1)S(1)} copy-done((bf16[1280,2048]{1,0:T(8,128)(2,1)S(1)}, bf16[1280,2048]{1,0:T(8,128)(2,1)}, u32[]{:S(2)}) %copy-start) | copy-done | bytes 5242904
  29.8 8.4 %inner_rows.1 = (bf16[2,768,1024]{2,1,0:T(8,128)(2,1)S(1)}, f32[2,2,256,1024]{3,2,1,0:T(8,128)S(1)}, bf16[4,128,896]{2,1,0:T(8,128)(2,1)S(1)}) custom-call(s32[10,7]{1,0:T(8,128)S(1)} %copy.5.nb_ref, s32[10,7]{1,0:T(8,128)S(1)} %copy.6.mask_ref, s32[1]{0:T(128)} %bitcast.sec_ref, s32[1]{0:T(128)} %bitcast.1.col_ref, s32[1]{0:T(128)} %bitcast.2.row_ref, ...), custom_call_target="tpu_custom_call" | custom-call | flops 1 | bytes 1 | tf_op jit(solution)/shard_map/inner_rows/pallas_call | solution.py:16
  38.2 4.5 %collective-permute-done.6.down_ref = bf16[128,2048]{1,0:T(8,128)(2,1)S(1)} collective-permute-done((bf16[128,2048]{1,0:T(8,128)(2,1)}, bf16[128,2048]{1,0:T(8,128)(2,1)S(1)}, u32[]{:S(2)}, u32[]{:S(2)}) %collective-permute-start.6) | collective-permute-done | bytes 524320 | tf_op jit(solution)/shard_map/ppermute | solution.py:240
  42.8 4.8 %rim_rows.2 = (bf16[512,1024]{1,0:T(8,128)(2,1)S(1)}, bf16[256,1024]{1,0:T(8,128)(2,1)S(1)}, bf16[256,1024]{1,0:T(8,128)(2,1)S(1)}) custom-call(s32[10,7]{1,0:T(8,128)S(1)} %copy.5.nb_ref, s32[10,7]{1,0:T(8,128)S(1)} %copy.6.mask_ref, s32[1]{0:T(128)} %bitcast.sec_ref, s32[1]{0:T(128)} %bitcast.1.col_ref, s32[1]{0:T(128)} %bitcast.2.row_ref, ...), custom_call_target="tpu_custom_call" | custom-call | flops 1 | bytes 1 | tf_op jit(solution)/shard_map/rim_rows/pallas_call | solution.py:16
  47.6 2.4 %collective-permute-start.10 = (bf16[256,1024]{1,0:T(8,128)(2,1)S(1)}, bf16[256,1024]{1,0:T(8,128)(2,1)S(1)}, u32[]{:S(2)}, u32[]{:S(2)}) collective-permute-start(bf16[256,1024]{1,0:T(8,128)(2,1)S(1)} %get-tuple-element.59), channel_id=1, source_target_pairs={{0,2},{2,0},{4,6},{6,4},{8,10},{10,8},{12,14},{14,12},{1,3},{3,1},... | collective-permute-start | bytes 1572872 | tf_op jit(solution)/shard_map/ppermute | solution.py:287
  51.6 3.6 %units.4 = (bf16[256,1024]{1,0:T(8,128)(2,1)S(1)}, bf16[256,1024]{1,0:T(8,128)(2,1)S(1)}) custom-call(s32[1]{0:T(128)} %bitcast.sec_ref, s32[1]{0:T(128)} %bitcast.1.col_ref, s32[1]{0:T(128)} %bitcast.2.row_ref, s32[8]{0:T(128)S(1)} %stack.35.index_ref, bf16[1280,2048]{1,0:T(8,128)(2,1)S(1)} %copy-done, ...), custom_call_target="tpu_custom_call" | custom-call | flops 1 | bytes 1 | tf_op jit(solution)/shard_map/units/pallas_call | solution.py:16
  55.2 4.8 %rim_rows.3 = (bf16[512,1024]{1,0:T(8,128)(2,1)S(1)}, bf16[256,1024]{1,0:T(8,128)(2,1)S(1)}, bf16[256,1024]{1,0:T(8,128)(2,1)S(1)}) custom-call(s32[10,7]{1,0:T(8,128)S(1)} %copy.5.nb_ref, s32[10,7]{1,0:T(8,128)S(1)} %copy.6.mask_ref, s32[1]{0:T(128)} %bitcast.sec_ref, s32[1]{0:T(128)} %bitcast.1.col_ref, s32[1]{0:T(128)} %bitcast.2.row_ref, ...), custom_call_target="tpu_custom_call" | custom-call | flops 1 | bytes 1 | tf_op jit(solution)/shard_map/rim_rows/pallas_call | solution.py:16
  60.2 5.9 %units.5 = (f32[256,1024]{1,0:T(8,128)S(1)}, f32[256,1024]{1,0:T(8,128)S(1)}, f32[256,1024]{1,0:T(8,128)S(1)}, f32[256,1024]{1,0:T(8,128)S(1)}) custom-call(s32[1]{0:T(128)} %bitcast.sec_ref, s32[1]{0:T(128)} %bitcast.1.col_ref, s32[1]{0:T(128)} %bitcast.2.row_ref, s32[8]{0:T(128)S(1)} %stack.35.index_ref, bf16[1280,2048]{1,0:T(8,128)(2,1)S(1)} %copy-done, ...), custom_call_target="tpu_custom_call" | custom-call | flops 1 | bytes 1 | tf_op jit(solution)/shard_map/units/pallas_call | solution.py:16
  66.8 1.9 %collective-permute-start.12 = (bf16[256,1024]{1,0:T(8,128)(2,1)S(1)}, bf16[256,1024]{1,0:T(8,128)(2,1)S(1)}, u32[]{:S(2)}, u32[]{:S(2)}) collective-permute-start(bf16[256,1024]{1,0:T(8,128)(2,1)S(1)} %get-tuple-element.65), channel_id=1, source_target_pairs={{0,2},{2,0},{4,6},{6,4},{8,10},{10,8},{12,14},{14,12},{1,3},{3,1},... | collective-permute-start | bytes 1572872 | tf_op jit(solution)/shard_map/ppermute | solution.py:287
  68.9 2.6 %units.6 = bf16[256,1024]{1,0:T(8,128)(2,1)S(1)} custom-call(s32[1]{0:T(128)} %bitcast.sec_ref, s32[1]{0:T(128)} %bitcast.1.col_ref, s32[1]{0:T(128)} %bitcast.2.row_ref, s32[8]{0:T(128)S(1)} %stack.35.index_ref, bf16[1280,2048]{1,0:T(8,128)(2,1)S(1)} %copy-done, bf16[1280,2048]{1,0:T(8,128)(2,1)} %collective-permute-done.refs_5_.refs_7_.refs_1_.refs_3_.there, ...), custom_call_target="tpu_custom_call" | custom-call | flops 1 | bytes 1 | tf_op jit(solution)/shard_map/units/pallas_call | solution.py:16
  71.5 7.0 %units.7 = (f32[256,1024]{1,0:T(8,128)S(1)}, f32[256,1024]{1,0:T(8,128)S(1)}, f32[256,1024]{1,0:T(8,128)S(1)}, f32[256,1024]{1,0:T(8,128)S(1)}, f32[256,1024]{1,0:T(8,128)S(1)}) custom-call(s32[1]{0:T(128)} %bitcast.sec_ref, s32[1]{0:T(128)} %bitcast.1.col_ref, s32[1]{0:T(128)} %bitcast.2.row_ref, s32[8]{0:T(128)S(1)} %stack.35.index_ref, ...), custom_call_target="tpu_custom_call" | custom-call | flops 1 | bytes 1 | tf_op jit(solution)/shard_map/units/pallas_call | solution.py:16
  80.4 4.5 %collective-permute-start.15 = (bf16[256,1024]{1,0:T(8,128)(2,1)S(1)}, bf16[256,1024]{1,0:T(8,128)(2,1)S(1)}, u32[]{:S(2)}, u32[]{:S(2)}) collective-permute-start(bf16[256,1024]{1,0:T(8,128)(2,1)S(1)} %add_convert_fusion.3), channel_id=1, source_target_pairs={{0,8},{2,10},{4,12},{6,14},{8,0},{10,2},{12,4},{14,6},{1,9},{3,11}... | collective-permute-start | bytes 1572872 | tf_op jit(solution)/shard_map/ppermute | solution.py:296
  84.9 2.3 %collective-permute-start.17 = (bf16[256,1024]{1,0:T(8,128)(2,1)S(1)}, bf16[256,1024]{1,0:T(8,128)(2,1)S(1)}, u32[]{:S(2)}, u32[]{:S(2)}) collective-permute-start(bf16[256,1024]{1,0:T(8,128)(2,1)S(1)} %units.6), channel_id=1, source_target_pairs={{0,2},{2,0},{4,6},{6,4},{8,10},{10,8},{12,14},{14,12},{1,3},{3,1},... | collective-permute-start | bytes 1572872 | tf_op jit(solution)/shard_map/ppermute | solution.py:287
  88.8 15.6 %collective-permute-done.11 = bf16[256,1024]{1,0:T(8,128)(2,1)S(1)} collective-permute-done((bf16[256,1024]{1,0:T(8,128)(2,1)S(1)}, bf16[256,1024]{1,0:T(8,128)(2,1)S(1)}, u32[]{:S(2)}, u32[]{:S(2)}) %collective-permute-start.11) | collective-permute-done | bytes 524320 | tf_op jit(solution)/shard_map/ppermute | solution.py:290
  105.2 8.3 %collective-permute-done.18 = bf16[256,1024]{1,0:T(8,128)(2,1)S(1)} collective-permute-done((bf16[256,1024]{1,0:T(8,128)(2,1)S(1)}, bf16[256,1024]{1,0:T(8,128)(2,1)S(1)}, u32[]{:S(2)}, u32[]{:S(2)}) %collective-permute-start.18) | collective-permute-done | bytes 524320 | tf_op jit(solution)/shard_map/ppermute | solution.py:290
  113.7 4.4 %collective-permute-start.22 = (bf16[256,1024]{1,0:T(8,128)(2,1)S(1)}, bf16[256,1024]{1,0:T(8,128)(2,1)S(1)}, u32[]{:S(2)}, u32[]{:S(2)}) collective-permute-start(bf16[256,1024]{1,0:T(8,128)(2,1)S(1)} %add_convert_fusion.1), channel_id=1, source_target_pairs={{0,8},{2,10},{4,12},{6,14},{8,0},{10,2},{12,4},{14,6},{1,9},{3,11}... | collective-permute-start | bytes 1572872 | tf_op jit(solution)/shard_map/ppermute | solution.py:296
  118.2 1.9 %collective-permute-start.21 = (bf16[256,1024]{1,0:T(8,128)(2,1)S(1)}, bf16[256,1024]{1,0:T(8,128)(2,1)S(1)}, u32[]{:S(2)}, u32[]{:S(2)}) collective-permute-start(bf16[256,1024]{1,0:T(8,128)(2,1)S(1)} %convert_element_type.70), channel_id=1, source_target_pairs={{0,2},{2,0},{4,6},{6,4},{8,10},{10,8},{12,14},{14,12},{1,3},{3,1},... | collective-permute-start | bytes 1572872 | tf_op jit(solution)/shard_map/ppermute | solution.py:287
  122.2 17.4 %collective-permute-done.22 = bf16[256,1024]{1,0:T(8,128)(2,1)S(1)} collective-permute-done((bf16[256,1024]{1,0:T(8,128)(2,1)S(1)}, bf16[256,1024]{1,0:T(8,128)(2,1)S(1)}, u32[]{:S(2)}, u32[]{:S(2)}) %collective-permute-start.22) | collective-permute-done | bytes 524320 | tf_op jit(solution)/shard_map/ppermute | solution.py:296
  139.8 2.1 %collective-permute-done.20.refs_1_ = bf16[256,1024]{1,0:T(8,128)(2,1)S(1)} collective-permute-done((bf16[256,1024]{1,0:T(8,128)(2,1)S(1)}, bf16[256,1024]{1,0:T(8,128)(2,1)S(1)}, u32[]{:S(2)}, u32[]{:S(2)}) %collective-permute-start.20) | collective-permute-done | bytes 524320 | tf_op jit(solution)/shard_map/ppermute | solution.py:287
  (58 shorter events, 21.8 us)
Async XLA Ops:
  0.0 26.4 %copy-start.1 = (bf16[10,7,64,128]{3,2,1,0:T(8,128)(2,1)S(1)}, bf16[10,7,64,128]{3,2,1,0:T(8,128)(2,1)}, u32[]{:S(2)}) copy-start(bf16[10,7,64,128]{3,2,1,0:T(8,128)(2,1)} %own_ref.1) | copy-start | bytes 3440644
  3.2 23.2 %collective-permute-start = (bf16[1280,2048]{1,0:T(8,128)(2,1)}, bf16[1280,2048]{1,0:T(8,128)(2,1)}, u32[]{:S(2)}, u32[]{:S(2)}) collective-permute-start(bf16[1280,2048]{1,0:T(8,128)(2,1)} %here.7), channel_id=1, source_target_pairs={{0,1},{1,0},{2,3},{3,2},{4,5},{5,4},{6,7},{7,6},{8,9},{9,8},{10,11... | collective-permute-start | bytes 15728648 | tf_op jit(solution)/shard_map/ppermute | solution.py:241
  3.7 8.8 %collective-permute-start.1 = (bf16[2,7,64,128]{3,2,1,0:T(8,128)(2,1)S(1)}, bf16[2,7,64,128]{3,2,1,0:T(8,128)(2,1)S(1)}, u32[]{:S(2)}, u32[]{:S(2)}) collective-permute-start(bf16[2,7,64,128]{3,2,1,0:T(8,128)(2,1)S(1)} %constant_dynamic-slice_fusion.1), channel_id=1, source_target_pairs={{0,16},{16,0},{1,17},{17,1},{2,18},{18,2},{3,19},{19,3},{4,20},{20... | collective-permute-start | bytes 688136 | tf_op jit(solution)/shard_map/ppermute | solution.py:238
  6.3 16.8 %collective-permute-start.7 = (bf16[128,2048]{1,0:T(8,128)(2,1)S(1)}, bf16[128,2048]{1,0:T(8,128)(2,1)S(1)}, u32[]{:S(2)}, u32[]{:S(2)}) collective-permute-start(bf16[128,2048]{1,0:T(8,128)(2,1)S(1)} %constant_dynamic-slice_fusion.2), channel_id=1, source_target_pairs={{2,0},{4,2},{6,4},{8,6},{10,8},{12,10},{14,12},{0,14},{16,18},{18,... | collective-permute-start | bytes 1572872 | tf_op jit(solution)/shard_map/ppermute | solution.py:231
  10.8 10.0 %collective-permute-start.2 = (bf16[3,7,64,128]{3,2,1,0:T(8,128)(2,1)S(1)}, bf16[3,7,64,128]{3,2,1,0:T(8,128)(2,1)}, u32[]{:S(2)}, u32[]{:S(2)}) collective-permute-start(bf16[3,7,64,128]{3,2,1,0:T(8,128)(2,1)S(1)} %constant_dynamic-slice_fusion), channel_id=1, source_target_pairs={{0,16},{16,0},{1,17},{17,1},{2,18},{18,2},{3,19},{19,3},{4,20},{20... | collective-permute-start | bytes 1032200 | tf_op jit(solution)/shard_map/ppermute | solution.py:238
  12.5 11.2 %collective-permute-start.3 = (bf16[2,7,64,128]{3,2,1,0:T(8,128)(2,1)S(1)}, bf16[2,7,64,128]{3,2,1,0:T(8,128)(2,1)S(1)}, u32[]{:S(2)}, u32[]{:S(2)}) collective-permute-start(bf16[2,7,64,128]{3,2,1,0:T(8,128)(2,1)S(1)} %collective-permute-done.1.refs_0_), channel_id=1, source_target_pairs={{0,1},{1,0},{2,3},{3,2},{4,5},{5,4},{6,7},{7,6},{8,9},{9,8},{10,11... | collective-permute-start | bytes 688136 | tf_op jit(solution)/shard_map/ppermute | solution.py:242
  14.7 28.0 %collective-permute-start.6 = (bf16[128,2048]{1,0:T(8,128)(2,1)}, bf16[128,2048]{1,0:T(8,128)(2,1)S(1)}, u32[]{:S(2)}, u32[]{:S(2)}) collective-permute-start(bf16[128,2048]{1,0:T(8,128)(2,1)} %get-tuple-element.85), channel_id=1, source_target_pairs={{2,0},{4,2},{6,4},{8,6},{10,8},{12,10},{14,12},{0,14},{3,1},{5,3},... | collective-permute-start | bytes 1572872 | tf_op jit(solution)/shard_map/ppermute | solution.py:240
  20.8 22.0 %collective-permute-start.5 = (bf16[128,2048]{1,0:T(8,128)(2,1)}, bf16[128,2048]{1,0:T(8,128)(2,1)S(1)}, u32[]{:S(2)}, u32[]{:S(2)}) collective-permute-start(bf16[128,2048]{1,0:T(8,128)(2,1)} %get-tuple-element.86), channel_id=1, source_target_pairs={{0,2},{2,4},{4,6},{6,8},{8,10},{10,12},{12,14},{14,0},{1,3},{3,5},... | collective-permute-start | bytes 1572872 | tf_op jit(solution)/shard_map/ppermute | solution.py:239
  23.1 19.7 %collective-permute-start.8 = (bf16[128,2048]{1,0:T(8,128)(2,1)S(1)}, bf16[128,2048]{1,0:T(8,128)(2,1)S(1)}, u32[]{:S(2)}, u32[]{:S(2)}) collective-permute-start(bf16[128,2048]{1,0:T(8,128)(2,1)S(1)} %collective-permute-done.7.split_ref), channel_id=1, source_target_pairs={{0,16},{16,0},{1,17},{17,1},{2,18},{18,2},{3,19},{19,3},{4,20},{20... | collective-permute-start | bytes 1572872 | tf_op jit(solution)/shard_map/ppermute | solution.py:243
  24.4 2.0 %collective-permute-start.4 = (bf16[3,7,64,128]{3,2,1,0:T(8,128)(2,1)}, bf16[3,7,64,128]{3,2,1,0:T(8,128)(2,1)}, u32[]{:S(2)}, u32[]{:S(2)}) collective-permute-start(bf16[3,7,64,128]{3,2,1,0:T(8,128)(2,1)} %collective-permute-done.2.refs_1_), channel_id=1, source_target_pairs={{0,1},{1,0},{2,3},{3,2},{4,5},{5,4},{6,7},{7,6},{8,9},{9,8},{10,11... | collective-permute-start | bytes 1032200 | tf_op jit(solution)/shard_map/ppermute | solution.py:242
  47.6 18.5 %collective-permute-start.10 = (bf16[256,1024]{1,0:T(8,128)(2,1)S(1)}, bf16[256,1024]{1,0:T(8,128)(2,1)S(1)}, u32[]{:S(2)}, u32[]{:S(2)}) collective-permute-start(bf16[256,1024]{1,0:T(8,128)(2,1)S(1)} %get-tuple-element.59), channel_id=1, source_target_pairs={{0,2},{2,0},{4,6},{6,4},{8,10},{10,8},{12,14},{14,12},{1,3},{3,1},... | collective-permute-start | bytes 1572872 | tf_op jit(solution)/shard_map/ppermute | solution.py:287
  50.0 18.7 %collective-permute-start.9 = (bf16[256,1024]{1,0:T(8,128)(2,1)S(1)}, bf16[256,1024]{1,0:T(8,128)(2,1)S(1)}, u32[]{:S(2)}, u32[]{:S(2)}) collective-permute-start(bf16[256,1024]{1,0:T(8,128)(2,1)S(1)} %get-tuple-element.57), channel_id=1, source_target_pairs={{0,4},{2,6},{4,0},{6,2},{8,12},{10,14},{12,8},{14,10},{1,5},{3,7},... | collective-permute-start | bytes 1572872 | tf_op jit(solution)/shard_map/ppermute | solution.py:290
  60.1 18.4 %collective-permute-start.13 = (bf16[256,1024]{1,0:T(8,128)(2,1)S(1)}, bf16[256,1024]{1,0:T(8,128)(2,1)S(1)}, u32[]{:S(2)}, u32[]{:S(2)}) collective-permute-start(bf16[256,1024]{1,0:T(8,128)(2,1)S(1)} %get-tuple-element.67), channel_id=1, source_target_pairs={{0,2},{2,0},{4,6},{6,4},{8,10},{10,8},{12,14},{14,12},{1,3},{3,1},... | collective-permute-start | bytes 1572872 | tf_op jit(solution)/shard_map/ppermute | solution.py:287
  66.3 13.9 %collective-permute-start.14 = (bf16[256,1024]{1,0:T(8,128)(2,1)S(1)}, bf16[256,1024]{1,0:T(8,128)(2,1)S(1)}, u32[]{:S(2)}, u32[]{:S(2)}) collective-permute-start(bf16[256,1024]{1,0:T(8,128)(2,1)S(1)} %add_convert_fusion.5), channel_id=1, source_target_pairs={{0,4},{2,6},{4,0},{6,2},{8,12},{10,14},{12,8},{14,10},{1,5},{3,7},... | collective-permute-start | bytes 1572872 | tf_op jit(solution)/shard_map/ppermute | solution.py:290
  66.8 20.4 %collective-permute-start.12 = (bf16[256,1024]{1,0:T(8,128)(2,1)S(1)}, bf16[256,1024]{1,0:T(8,128)(2,1)S(1)}, u32[]{:S(2)}, u32[]{:S(2)}) collective-permute-start(bf16[256,1024]{1,0:T(8,128)(2,1)S(1)} %get-tuple-element.65), channel_id=1, source_target_pairs={{0,2},{2,0},{4,6},{6,4},{8,10},{10,8},{12,14},{14,12},{1,3},{3,1},... | collective-permute-start | bytes 1572872 | tf_op jit(solution)/shard_map/ppermute | solution.py:287
  78.5 25.9 %collective-permute-start.11 = (bf16[256,1024]{1,0:T(8,128)(2,1)S(1)}, bf16[256,1024]{1,0:T(8,128)(2,1)S(1)}, u32[]{:S(2)}, u32[]{:S(2)}) collective-permute-start(bf16[256,1024]{1,0:T(8,128)(2,1)S(1)} %get-tuple-element.61), channel_id=1, source_target_pairs={{0,4},{2,6},{4,0},{6,2},{8,12},{10,14},{12,8},{14,10},{1,5},{3,7},... | collective-permute-start | bytes 1572872 | tf_op jit(solution)/shard_map/ppermute | solution.py:290
  80.4 24.6 %collective-permute-start.15 = (bf16[256,1024]{1,0:T(8,128)(2,1)S(1)}, bf16[256,1024]{1,0:T(8,128)(2,1)S(1)}, u32[]{:S(2)}, u32[]{:S(2)}) collective-permute-start(bf16[256,1024]{1,0:T(8,128)(2,1)S(1)} %add_convert_fusion.3), channel_id=1, source_target_pairs={{0,8},{2,10},{4,12},{6,14},{8,0},{10,2},{12,4},{14,6},{1,9},{3,11}... | collective-permute-start | bytes 1572872 | tf_op jit(solution)/shard_map/ppermute | solution.py:296
  84.9 20.3 %collective-permute-start.17 = (bf16[256,1024]{1,0:T(8,128)(2,1)S(1)}, bf16[256,1024]{1,0:T(8,128)(2,1)S(1)}, u32[]{:S(2)}, u32[]{:S(2)}) collective-permute-start(bf16[256,1024]{1,0:T(8,128)(2,1)S(1)} %units.6), channel_id=1, source_target_pairs={{0,2},{2,0},{4,6},{6,4},{8,10},{10,8},{12,14},{14,12},{1,3},{3,1},... | collective-permute-start | bytes 1572872 | tf_op jit(solution)/shard_map/ppermute | solution.py:287
  87.3 26.2 %collective-permute-start.18 = (bf16[256,1024]{1,0:T(8,128)(2,1)S(1)}, bf16[256,1024]{1,0:T(8,128)(2,1)S(1)}, u32[]{:S(2)}, u32[]{:S(2)}) collective-permute-start(bf16[256,1024]{1,0:T(8,128)(2,1)S(1)} %add_convert_fusion.2), channel_id=1, source_target_pairs={{0,4},{2,6},{4,0},{6,2},{8,12},{10,14},{12,8},{14,10},{1,5},{3,7},... | collective-permute-start | bytes 1572872 | tf_op jit(solution)/shard_map/ppermute | solution.py:290
  87.4 32.9 %collective-permute-start.16 = (bf16[256,1024]{1,0:T(8,128)(2,1)S(1)}, bf16[256,1024]{1,0:T(8,128)(2,1)S(1)}, u32[]{:S(2)}, u32[]{:S(2)}) collective-permute-start(bf16[256,1024]{1,0:T(8,128)(2,1)S(1)} %get-tuple-element.73), channel_id=1, source_target_pairs={{0,2},{2,0},{4,6},{6,4},{8,10},{10,8},{12,14},{14,12},{1,3},{3,1},... | collective-permute-start | bytes 1572872 | tf_op jit(solution)/shard_map/ppermute | solution.py:287
  113.7 25.8 %collective-permute-start.22 = (bf16[256,1024]{1,0:T(8,128)(2,1)S(1)}, bf16[256,1024]{1,0:T(8,128)(2,1)S(1)}, u32[]{:S(2)}, u32[]{:S(2)}) collective-permute-start(bf16[256,1024]{1,0:T(8,128)(2,1)S(1)} %add_convert_fusion.1), channel_id=1, source_target_pairs={{0,8},{2,10},{4,12},{6,14},{8,0},{10,2},{12,4},{14,6},{1,9},{3,11}... | collective-permute-start | bytes 1572872 | tf_op jit(solution)/shard_map/ppermute | solution.py:296
  118.2 21.5 %collective-permute-start.21 = (bf16[256,1024]{1,0:T(8,128)(2,1)S(1)}, bf16[256,1024]{1,0:T(8,128)(2,1)S(1)}, u32[]{:S(2)}, u32[]{:S(2)}) collective-permute-start(bf16[256,1024]{1,0:T(8,128)(2,1)S(1)} %convert_element_type.70), channel_id=1, source_target_pairs={{0,2},{2,0},{4,6},{6,4},{8,10},{10,8},{12,14},{14,12},{1,3},{3,1},... | collective-permute-start | bytes 1572872 | tf_op jit(solution)/shard_map/ppermute | solution.py:287
  120.1 21.7 %collective-permute-start.20 = (bf16[256,1024]{1,0:T(8,128)(2,1)S(1)}, bf16[256,1024]{1,0:T(8,128)(2,1)S(1)}, u32[]{:S(2)}, u32[]{:S(2)}) collective-permute-start(bf16[256,1024]{1,0:T(8,128)(2,1)S(1)} %add_convert_fusion.4), channel_id=1, source_target_pairs={{0,2},{2,0},{4,6},{6,4},{8,10},{10,8},{12,14},{14,12},{1,3},{3,1},... | collective-permute-start | bytes 1572872 | tf_op jit(solution)/shard_map/ppermute | solution.py:287
  120.5 21.4 %collective-permute-start.19 = (bf16[256,1024]{1,0:T(8,128)(2,1)S(1)}, bf16[256,1024]{1,0:T(8,128)(2,1)S(1)}, u32[]{:S(2)}, u32[]{:S(2)}) collective-permute-start(bf16[256,1024]{1,0:T(8,128)(2,1)S(1)} %add_convert_fusion), channel_id=1, source_target_pairs={{0,4},{2,6},{4,0},{6,2},{8,12},{10,14},{12,8},{14,10},{1,5},{3,7},... | collective-permute-start | bytes 1572872 | tf_op jit(solution)/shard_map/ppermute | solution.py:290
  (5 other events, 52.9 us)

commit v6 on v5

--- a/solution.py
+++ b/solution.py
@@ -163,7 +163,7 @@
     )
 
 
-def units(part, which, lefts, inner, rim_part, ids, index, size, dtype):
+def units(part, which, lefts, inner, rim_part, ids, index, size, dtypes):
     rows = lefts[0].shape[0]
     width = inner.shape[2]
     rim = rim_part.shape[0] // 2
@@ -176,11 +176,11 @@
             transposed_dot(left[rim : rows - rim], inner_ref[0])
             + transposed_dot(left[:rim], rim_ref[:rim, :])
             + transposed_dot(left[rows - rim :], rim_ref[rim:, :])
-        ).astype(dtype)
+        )
         for u, out_ref in enumerate(out_refs):
             @pl.when(pl.program_id(0) == u)
             def _(out_ref=out_ref):
-                out_ref[...] = total
+                out_ref[...] = total.astype(out_ref.dtype)
 
     unit = pl.BlockSpec((rows, size), lambda u, *s: (0, s[3][first + u]))
     return call(
@@ -188,7 +188,7 @@
         [unit, unit, pl.BlockSpec((1, *inner.shape[1:]), lambda u, *_: (part, 0, 0)), fixed(rim_part)],
         (*lefts, inner, rim_part),
         [pl.BlockSpec((size, width), lambda u, *_: (0, 0))] * count,
-        [jax.ShapeDtypeStruct((size, width), dtype)] * count, [], "units",
+        [jax.ShapeDtypeStruct((size, width), dtype) for dtype in dtypes], [], "units",
     )
 
 
@@ -279,8 +279,8 @@
         rim_part, a, b = rim_rows(part, basis, halos, ops, tables, ids, lefts, index, size, begun)
         return rim_part, a[: len(away) * height], b[:height]
 
-    def unit_half(part, which, rim_part, dtype):
-        made = units(part, which, lefts, inner, rim_part, ids, index, size, dtype)
+    def unit_half(part, which, rim_part, *dtypes):
+        made = units(part, which, lefts, inner, rim_part, ids, index, size, dtypes)
         return [x[: len(plan[i][0]) * height] for i, x in zip(which, made)]
 
     def to_side(x):
@@ -306,37 +306,37 @@
 
     rim0, far_a0, near_a0 = rim_half(0, halos)
     far_a0, near_a0 = to_side(far_a0), to_pair(near_a0)
-    far_b0, near_b0 = unit_half(0, (2, 3), rim0, BF16)
+    far_b0, near_b0, far_c0 = unit_half(0, (2, 3, 4), rim0, BF16, BF16, F32)
+    rim1, far_a1, near_a1 = rim_half(1, (after(halos[0], far_c0), *halos[1:]))
     far_b0 = to_side(far_b0)
-    rim1, far_a1, near_a1 = rim_half(1, (after(halos[0], near_b0), *halos[1:]))
+    far_c0 = add(far_c0, after(far_a0, rim1))
+    near_c0, far_d0, own0 = unit_half(0, (5, 6, 7), after(rim0, far_c0), F32, F32, F32)
+    far_c0_sum = far_c0
+    far_c0 = to_pair(far_c0)
     far_a1 = to_side(far_a1)
-    far_c0, near_c0, far_d0, own0 = unit_half(0, (4, 5, 6, 7), after(rim0, rim1), F32)
-    far_c0 = add(far_c0, far_a0)
-    near_c0 = add(near_c0, after(near_a0, far_c0))
-    far_c0 = to_pair(far_c0)
-    near_b0 = to_pair(after(near_b0, near_c0))
-    late1 = after(rim1, near_c0)
-    (far_b1,) = unit_half(1, (2,), late1, BF16)
-    near_b1, far_c1, near_c1, far_d1, own1 = unit_half(1, (3, 4, 5, 6, 7), after(late1, far_b1), F32)
+    near_c0 = add(near_c0, after(near_a0, own0))
+    far_b1, near_b1, far_c1 = unit_half(1, (2, 3, 4), after(rim1, near_c0), BF16, F32, F32)
     far_b1 = to_side(far_b1)
-    near_a1 = to_side(after(near_a1, far_c1))
     far_d0 = add(far_d0, after(far_b0, far_c1), far_c0)
-    far_c1 = add(far_c1, after(far_a1, far_d0))
+    near_b0 = to_pair(after(near_b0, far_c0_sum))
+    near_a1 = to_side(after(near_a1, far_d0))
+    own0 = add32(own0, after(near_b0, far_d0))
+    far_c1 = add(far_c1, after(far_a1, own0))
     far_d0 = to_far(far_d0)
-    own0 = add32(own0, after(near_b0, far_c1), *far_d0)
-    near_c0, near_c1 = after((near_c0, near_c1), far_c1)
+    near_c1, far_d1, own1 = unit_half(1, (5, 6, 7), after(rim1, far_c1), BF16, F32, F32)
     far_c1 = to_pair(far_c1)
+    near_b1 = add(near_b1, after(near_a1, far_d1))
+    near_c0, near_c1 = after((near_c0, near_c1), near_b1)
+    own0 = add32(own0, *after(far_d0, near_b1))
+    near_b1 = to_pair(near_b1)
     far_d1 = add(far_d1, after(far_b1, own0), far_c1)
-    near_b1 = add(near_b1, after(near_a1, far_d1))
+    near_c0 = to_side(near_c0)
+    own0 = add32(own0, after(near_c0, far_d1))
     far_d1 = to_far(far_d1)
-    own1 = add32(own1, *after(far_d1, near_b1))
-    near_b1 = to_pair(near_b1)
-    near_c0 = to_side(near_c0)
-    near_c1 = to_side(near_c1.astype(BF16))
-    near_b1, near_c0, near_c1 = after((near_b1, near_c0, near_c1), own1)
-    return finish(
-        ((own0, near_c0), (own1, near_b1, near_c1)), 1.0 / math.sqrt(rows * count)
-    )
+    own1 = add32(own1, *after(far_d1, own0))
+    near_c1 = to_side(near_c1)
+    near_b1, near_c1 = after((near_b1, near_c1), own1)
+    return finish(((own0,), (own1, near_b1, near_c1)), 1.0 / math.sqrt(rows * count))
 
 
 def solution(mesh):

time: 144 us -> 139 us (0.965)
  waiting for transfers between devices: 54 us -> 50.9 us
  starting transfers between devices: 39.1 us -> 36.7 us
    ppermute x7, waiting for transfers between devices: 2.08 us -> 11.4 us  [to_side(): return lax.ppermute(x, 'row', swap_side)]
    ppermute x5, waiting for transfers between devices: 23.9 us -> 16.2 us  [to_pair(): return lax.ppermute(x, 'row', swap_pair)]
    ppermute x2, waiting for transfers between devices: 18 us -> 13.3 us  [to_far(): parts.append(lax.ppermute(x[i * height:(i + 1) * height], 'row', route))]
    ppermute x7, starting transfers between devices: 10.4 us -> 8.71 us  [to_side(): return lax.ppermute(x, 'row', swap_side)]
    ppermute x2, starting transfers between devices: 8.88 us -> 7.37 us  [to_far(): parts.append(lax.ppermute(x[i * height:(i + 1) * height], 'row', route))]
  transfers between devices with their start and end apart: 23 -> 23, of which waited for: 10 -> 11; matrix products, arithmetic and copies ran while one was open for 3% -> 3% of each run, Pallas kernels for 23% -> 24%
where the time goes in v6:
time: 139 us; the launch traced here: 138 us
  waiting for transfers between devices  50.9 us (37%)
  Pallas kernels  38.8 us (28%)
  starting transfers between devices  36.7 us (26%)
  local copies, waits for them, and re-layouts  9.83 us (7%)
  other arithmetic  1.71 us (1%)
    pallas_call x8, Pallas kernels, call(): pl.pallas_call(kernel, grid_spec=pltpu.PrefetchScalarGridSpec(num_scalar_...  38.8 us
    ppermute x5, waiting for transfers between devices, to_pair(): return lax.ppermute(x, 'row', swap_pair)  16.2 us
    ppermute x2, waiting for transfers between devices, to_far(): parts.append(lax.ppermute(x[i * height:(i + 1) * height], 'row', route))  13.3 us
    ppermute x7, waiting for transfers between devices, to_side(): return lax.ppermute(x, 'row', swap_side)  11.4 us
    ppermute x7, starting transfers between devices, to_side(): return lax.ppermute(x, 'row', swap_side)  8.71 us
    ppermute x2, starting transfers between devices, to_far(): parts.append(lax.ppermute(x[i * height:(i + 1) * height], 'row', route))  7.37 us
    ppermute x5, starting transfers between devices, to_pair(): return lax.ppermute(x, 'row', swap_pair)  6.21 us
    ppermute x1, starting transfers between devices, per_device(): from_after = lax.ppermute(behind[:block], 'row', down)  5.23 us
  transfers between devices with their start and end apart: 23, of which 11 were waited for; matrix products, arithmetic and copies ran while one was open for 3% of the time, Pallas kernels for 24%

profile of v6, /device:TPU:0, one launch (start us, length us, event | category | flops | bytes accessed | tf_op | source)
XLA Modules:
  0.0 138.2 jit_solution(5468679100533285470)
XLA Ops:
  3.7 2.6 %collective-permute-start.1 = (bf16[2,7,64,128]{3,2,1,0:T(8,128)(2,1)S(1)}, bf16[2,7,64,128]{3,2,1,0:T(8,128)(2,1)S(1)}, u32[]{:S(2)}, u32[]{:S(2)}) collective-permute-start(bf16[2,7,64,128]{3,2,1,0:T(8,128)(2,1)S(1)} %constant_dynamic-slice_fusion.1), channel_id=1, source_target_pairs={{0,16},{16,0},{1,17},{17,1},{2,18},{18,2},{3,19},{19,3},{4,20},{20... | collective-permute-start | bytes 688136 | tf_op jit(solution)/shard_map/ppermute | solution.py:238
  6.3 4.5 %collective-permute-start.7 = (bf16[128,2048]{1,0:T(8,128)(2,1)S(1)}, bf16[128,2048]{1,0:T(8,128)(2,1)S(1)}, u32[]{:S(2)}, u32[]{:S(2)}) collective-permute-start(bf16[128,2048]{1,0:T(8,128)(2,1)S(1)} %constant_dynamic-slice_fusion.2), channel_id=1, source_target_pairs={{2,0},{4,2},{6,4},{8,6},{10,8},{12,10},{14,12},{0,14},{16,18},{18,... | collective-permute-start | bytes 1572872 | tf_op jit(solution)/shard_map/ppermute | solution.py:231
  10.8 1.7 %collective-permute-done.1.refs_0_ = bf16[2,7,64,128]{3,2,1,0:T(8,128)(2,1)S(1)} collective-permute-done((bf16[2,7,64,128]{3,2,1,0:T(8,128)(2,1)S(1)}, bf16[2,7,64,128]{3,2,1,0:T(8,128)(2,1)S(1)}, u32[]{:S(2)}, u32[]{:S(2)}) %collective-permute-start.1) | collective-permute-done | bytes 229408 | tf_op jit(solution)/shard_map/ppermute | solution.py:238
  12.5 2.3 %fusion = (bf16[128,2048]{1,0:T(8,128)(2,1)}, bf16[128,2048]{1,0:T(8,128)(2,1)}) fusion(bf16[1280,2048]{1,0:T(8,128)(2,1)} %here.7), kind=kLoop, calls=%fused_computation.13 | loop fusion | bytes 2097152 | tf_op jit(solution)/shard_map/slice | solution.py:240
  14.8 5.2 %collective-permute-start.6 = (bf16[128,2048]{1,0:T(8,128)(2,1)}, bf16[128,2048]{1,0:T(8,128)(2,1)S(1)}, u32[]{:S(2)}, u32[]{:S(2)}) collective-permute-start(bf16[128,2048]{1,0:T(8,128)(2,1)} %get-tuple-element.91), channel_id=1, source_target_pairs={{2,0},{4,2},{6,4},{8,6},{10,8},{12,10},{14,12},{0,14},{3,1},{5,3},... | collective-permute-start | bytes 1572872 | tf_op jit(solution)/shard_map/ppermute | solution.py:240
  24.7 1.7 %collective-permute-done.4.refs_3_ = bf16[3,7,64,128]{3,2,1,0:T(8,128)(2,1)} collective-permute-done((bf16[3,7,64,128]{3,2,1,0:T(8,128)(2,1)}, bf16[3,7,64,128]{3,2,1,0:T(8,128)(2,1)}, u32[]{:S(2)}, u32[]{:S(2)}) %collective-permute-start.4) | collective-permute-done | bytes 344096 | tf_op jit(solution)/shard_map/ppermute | solution.py:242
  26.4 2.5 %copy-done = bf16[1280,2048]{1,0:T(8,128)(2,1)S(1)} copy-done((bf16[1280,2048]{1,0:T(8,128)(2,1)S(1)}, bf16[1280,2048]{1,0:T(8,128)(2,1)}, u32[]{:S(2)}) %copy-start) | copy-done | bytes 5242904
  29.8 8.4 %inner_rows.1 = (bf16[2,768,1024]{2,1,0:T(8,128)(2,1)S(1)}, f32[2,2,256,1024]{3,2,1,0:T(8,128)S(1)}, bf16[4,128,896]{2,1,0:T(8,128)(2,1)S(1)}) custom-call(s32[10,7]{1,0:T(8,128)S(1)} %copy.5.nb_ref, s32[10,7]{1,0:T(8,128)S(1)} %copy.6.mask_ref, s32[1]{0:T(128)} %bitcast.sec_ref, s32[1]{0:T(128)} %bitcast.1.col_ref, s32[1]{0:T(128)} %bitcast.2.row_ref, ...), custom_call_target="tpu_custom_call" | custom-call | flops 1 | bytes 1 | tf_op jit(solution)/shard_map/inner_rows/pallas_call | solution.py:16
  38.2 4.5 %collective-permute-done.6.down_ref = bf16[128,2048]{1,0:T(8,128)(2,1)S(1)} collective-permute-done((bf16[128,2048]{1,0:T(8,128)(2,1)}, bf16[128,2048]{1,0:T(8,128)(2,1)S(1)}, u32[]{:S(2)}, u32[]{:S(2)}) %collective-permute-start.6) | collective-permute-done | bytes 524320 | tf_op jit(solution)/shard_map/ppermute | solution.py:240
  42.8 4.8 %rim_rows.2 = (bf16[512,1024]{1,0:T(8,128)(2,1)S(1)}, bf16[256,1024]{1,0:T(8,128)(2,1)S(1)}, bf16[256,1024]{1,0:T(8,128)(2,1)S(1)}) custom-call(s32[10,7]{1,0:T(8,128)S(1)} %copy.5.nb_ref, s32[10,7]{1,0:T(8,128)S(1)} %copy.6.mask_ref, s32[1]{0:T(128)} %bitcast.sec_ref, s32[1]{0:T(128)} %bitcast.1.col_ref, s32[1]{0:T(128)} %bitcast.2.row_ref, ...), custom_call_target="tpu_custom_call" | custom-call | flops 1 | bytes 1 | tf_op jit(solution)/shard_map/rim_rows/pallas_call | solution.py:16
  47.6 2.4 %collective-permute-start.9 = (bf16[256,1024]{1,0:T(8,128)(2,1)S(1)}, bf16[256,1024]{1,0:T(8,128)(2,1)S(1)}, u32[]{:S(2)}, u32[]{:S(2)}) collective-permute-start(bf16[256,1024]{1,0:T(8,128)(2,1)S(1)} %get-tuple-element.55), channel_id=1, source_target_pairs={{0,2},{2,0},{4,6},{6,4},{8,10},{10,8},{12,14},{14,12},{1,3},{3,1},... | collective-permute-start | bytes 1572872 | tf_op jit(solution)/shard_map/ppermute | solution.py:287
  51.6 4.8 %units.4 = (bf16[256,1024]{1,0:T(8,128)(2,1)S(1)}, bf16[256,1024]{1,0:T(8,128)(2,1)S(1)}, f32[256,1024]{1,0:T(8,128)S(1)}) custom-call(s32[1]{0:T(128)} %bitcast.sec_ref, s32[1]{0:T(128)} %bitcast.1.col_ref, s32[1]{0:T(128)} %bitcast.2.row_ref, s32[8]{0:T(128)S(1)} %stack.35.index_ref, bf16[1280,2048]{1,0:T(8,128)(2,1)S(1)} %copy-done, ...), custom_call_target="tpu_custom_call" | custom-call | flops 1 | bytes 1 | tf_op jit(solution)/shard_map/units/pallas_call | solution.py:16
  56.6 4.8 %rim_rows.3 = (bf16[512,1024]{1,0:T(8,128)(2,1)S(1)}, bf16[256,1024]{1,0:T(8,128)(2,1)S(1)}, bf16[256,1024]{1,0:T(8,128)(2,1)S(1)}) custom-call(s32[10,7]{1,0:T(8,128)S(1)} %copy.5.nb_ref, s32[10,7]{1,0:T(8,128)S(1)} %copy.6.mask_ref, s32[1]{0:T(128)} %bitcast.sec_ref, s32[1]{0:T(128)} %bitcast.1.col_ref, s32[1]{0:T(128)} %bitcast.2.row_ref, ...), custom_call_target="tpu_custom_call" | custom-call | flops 1 | bytes 1 | tf_op jit(solution)/shard_map/rim_rows/pallas_call | solution.py:16
  64.5 2.1 %collective-permute-start.16 = (bf16[256,1024]{1,0:T(8,128)(2,1)S(1)}, bf16[256,1024]{1,0:T(8,128)(2,1)S(1)}, u32[]{:S(2)}, u32[]{:S(2)}) collective-permute-start(bf16[256,1024]{1,0:T(8,128)(2,1)S(1)} %get-tuple-element.75), channel_id=1, source_target_pairs={{0,2},{2,0},{4,6},{6,4},{8,10},{10,8},{12,14},{14,12},{1,3},{3,1},... | collective-permute-start | bytes 1572872 | tf_op jit(solution)/shard_map/ppermute | solution.py:287
  67.0 4.8 %units.5 = (f32[256,1024]{1,0:T(8,128)S(1)}, f32[256,1024]{1,0:T(8,128)S(1)}, f32[256,1024]{1,0:T(8,128)S(1)}) custom-call(s32[1]{0:T(128)} %bitcast.sec_ref, s32[1]{0:T(128)} %bitcast.1.col_ref, s32[1]{0:T(128)} %bitcast.2.row_ref, s32[8]{0:T(128)S(1)} %stack.35.index_ref, bf16[1280,2048]{1,0:T(8,128)(2,1)S(1)} %copy-done, ...), custom_call_target="tpu_custom_call" | custom-call | flops 1 | bytes 1 | tf_op jit(solution)/shard_map/units/pallas_call | solution.py:16
  72.0 4.8 %units.6 = (bf16[256,1024]{1,0:T(8,128)(2,1)S(1)}, f32[256,1024]{1,0:T(8,128)S(1)}, f32[256,1024]{1,0:T(8,128)S(1)}) custom-call(s32[1]{0:T(128)} %bitcast.sec_ref, s32[1]{0:T(128)} %bitcast.1.col_ref, s32[1]{0:T(128)} %bitcast.2.row_ref, s32[8]{0:T(128)S(1)} %stack.35.index_ref, bf16[1280,2048]{1,0:T(8,128)(2,1)S(1)} %copy-done, ...), custom_call_target="tpu_custom_call" | custom-call | flops 1 | bytes 1 | tf_op jit(solution)/shard_map/units/pallas_call | solution.py:16
  78.1 4.0 %collective-permute-start.14 = (bf16[256,1024]{1,0:T(8,128)(2,1)S(1)}, bf16[256,1024]{1,0:T(8,128)(2,1)S(1)}, u32[]{:S(2)}, u32[]{:S(2)}) collective-permute-start(bf16[256,1024]{1,0:T(8,128)(2,1)S(1)} %add_convert_fusion.3), channel_id=1, source_target_pairs={{0,8},{2,10},{4,12},{6,14},{8,0},{10,2},{12,4},{14,6},{1,9},{3,11}... | collective-permute-start | bytes 1572872 | tf_op jit(solution)/shard_map/ppermute | solution.py:296
  82.1 15.3 %collective-permute-done.10 = bf16[256,1024]{1,0:T(8,128)(2,1)S(1)} collective-permute-done((bf16[256,1024]{1,0:T(8,128)(2,1)S(1)}, bf16[256,1024]{1,0:T(8,128)(2,1)S(1)}, u32[]{:S(2)}, u32[]{:S(2)}) %collective-permute-start.10) | collective-permute-done | bytes 524320 | tf_op jit(solution)/shard_map/ppermute | solution.py:290
  99.2 4.8 %units.7 = (bf16[256,1024]{1,0:T(8,128)(2,1)S(1)}, f32[256,1024]{1,0:T(8,128)S(1)}, f32[256,1024]{1,0:T(8,128)S(1)}) custom-call(s32[1]{0:T(128)} %bitcast.sec_ref, s32[1]{0:T(128)} %bitcast.1.col_ref, s32[1]{0:T(128)} %bitcast.2.row_ref, s32[8]{0:T(128)S(1)} %stack.35.index_ref, bf16[1280,2048]{1,0:T(8,128)(2,1)S(1)} %copy-done, ...), custom_call_target="tpu_custom_call" | custom-call | flops 1 | bytes 1 | tf_op jit(solution)/shard_map/units/pallas_call | solution.py:16
  104.0 5.2 %collective-permute-done.15 = bf16[256,1024]{1,0:T(8,128)(2,1)S(1)} collective-permute-done((bf16[256,1024]{1,0:T(8,128)(2,1)S(1)}, bf16[256,1024]{1,0:T(8,128)(2,1)S(1)}, u32[]{:S(2)}, u32[]{:S(2)}) %collective-permute-start.15) | collective-permute-done | bytes 524320 | tf_op jit(solution)/shard_map/ppermute | solution.py:287
  111.2 3.4 %collective-permute-start.20 = (bf16[256,1024]{1,0:T(8,128)(2,1)S(1)}, bf16[256,1024]{1,0:T(8,128)(2,1)S(1)}, u32[]{:S(2)}, u32[]{:S(2)}) collective-permute-start(bf16[256,1024]{1,0:T(8,128)(2,1)S(1)} %add_convert_fusion), channel_id=1, source_target_pairs={{0,8},{2,10},{4,12},{6,14},{8,0},{10,2},{12,4},{14,6},{1,9},{3,11}... | collective-permute-start | bytes 1572872 | tf_op jit(solution)/shard_map/ppermute | solution.py:296
  114.6 2.5 %collective-permute-start.21 = (bf16[256,1024]{1,0:T(8,128)(2,1)S(1)}, bf16[256,1024]{1,0:T(8,128)(2,1)S(1)}, u32[]{:S(2)}, u32[]{:S(2)}) collective-permute-start(bf16[256,1024]{1,0:T(8,128)(2,1)S(1)} %add_convert_fusion.1), channel_id=1, source_target_pairs={{0,4},{2,6},{4,0},{6,2},{8,12},{10,14},{12,8},{14,10},{1,5},{3,7},... | collective-permute-start | bytes 1572872 | tf_op jit(solution)/shard_map/ppermute | solution.py:290
  118.3 4.8 %collective-permute-done.17 = bf16[256,1024]{1,0:T(8,128)(2,1)S(1)} collective-permute-done((bf16[256,1024]{1,0:T(8,128)(2,1)S(1)}, bf16[256,1024]{1,0:T(8,128)(2,1)S(1)}, u32[]{:S(2)}, u32[]{:S(2)}) %collective-permute-start.17) | collective-permute-done | bytes 524320 | tf_op jit(solution)/shard_map/ppermute | solution.py:287
  123.3 13.3 %collective-permute-done.20 = bf16[256,1024]{1,0:T(8,128)(2,1)S(1)} collective-permute-done((bf16[256,1024]{1,0:T(8,128)(2,1)S(1)}, bf16[256,1024]{1,0:T(8,128)(2,1)S(1)}, u32[]{:S(2)}, u32[]{:S(2)}) %collective-permute-start.20) | collective-permute-done | bytes 524320 | tf_op jit(solution)/shard_map/ppermute | solution.py:296
  (59 shorter events, 22.6 us)
Async XLA Ops:
  0.0 26.4 %copy-start.1 = (bf16[10,7,64,128]{3,2,1,0:T(8,128)(2,1)S(1)}, bf16[10,7,64,128]{3,2,1,0:T(8,128)(2,1)}, u32[]{:S(2)}) copy-start(bf16[10,7,64,128]{3,2,1,0:T(8,128)(2,1)} %own_ref.1) | copy-start | bytes 3440644
  3.2 23.2 %collective-permute-start = (bf16[1280,2048]{1,0:T(8,128)(2,1)}, bf16[1280,2048]{1,0:T(8,128)(2,1)}, u32[]{:S(2)}, u32[]{:S(2)}) collective-permute-start(bf16[1280,2048]{1,0:T(8,128)(2,1)} %here.7), channel_id=1, source_target_pairs={{0,1},{1,0},{2,3},{3,2},{4,5},{5,4},{6,7},{7,6},{8,9},{9,8},{10,11... | collective-permute-start | bytes 15728648 | tf_op jit(solution)/shard_map/ppermute | solution.py:241
  3.7 8.8 %collective-permute-start.1 = (bf16[2,7,64,128]{3,2,1,0:T(8,128)(2,1)S(1)}, bf16[2,7,64,128]{3,2,1,0:T(8,128)(2,1)S(1)}, u32[]{:S(2)}, u32[]{:S(2)}) collective-permute-start(bf16[2,7,64,128]{3,2,1,0:T(8,128)(2,1)S(1)} %constant_dynamic-slice_fusion.1), channel_id=1, source_target_pairs={{0,16},{16,0},{1,17},{17,1},{2,18},{18,2},{3,19},{19,3},{4,20},{20... | collective-permute-start | bytes 688136 | tf_op jit(solution)/shard_map/ppermute | solution.py:238
  6.3 16.8 %collective-permute-start.7 = (bf16[128,2048]{1,0:T(8,128)(2,1)S(1)}, bf16[128,2048]{1,0:T(8,128)(2,1)S(1)}, u32[]{:S(2)}, u32[]{:S(2)}) collective-permute-start(bf16[128,2048]{1,0:T(8,128)(2,1)S(1)} %constant_dynamic-slice_fusion.2), channel_id=1, source_target_pairs={{2,0},{4,2},{6,4},{8,6},{10,8},{12,10},{14,12},{0,14},{16,18},{18,... | collective-permute-start | bytes 1572872 | tf_op jit(solution)/shard_map/ppermute | solution.py:231
  10.8 10.0 %collective-permute-start.2 = (bf16[3,7,64,128]{3,2,1,0:T(8,128)(2,1)S(1)}, bf16[3,7,64,128]{3,2,1,0:T(8,128)(2,1)}, u32[]{:S(2)}, u32[]{:S(2)}) collective-permute-start(bf16[3,7,64,128]{3,2,1,0:T(8,128)(2,1)S(1)} %constant_dynamic-slice_fusion), channel_id=1, source_target_pairs={{0,16},{16,0},{1,17},{17,1},{2,18},{18,2},{3,19},{19,3},{4,20},{20... | collective-permute-start | bytes 1032200 | tf_op jit(solution)/shard_map/ppermute | solution.py:238
  12.5 11.2 %collective-permute-start.3 = (bf16[2,7,64,128]{3,2,1,0:T(8,128)(2,1)S(1)}, bf16[2,7,64,128]{3,2,1,0:T(8,128)(2,1)S(1)}, u32[]{:S(2)}, u32[]{:S(2)}) collective-permute-start(bf16[2,7,64,128]{3,2,1,0:T(8,128)(2,1)S(1)} %collective-permute-done.1.refs_0_), channel_id=1, source_target_pairs={{0,1},{1,0},{2,3},{3,2},{4,5},{5,4},{6,7},{7,6},{8,9},{9,8},{10,11... | collective-permute-start | bytes 688136 | tf_op jit(solution)/shard_map/ppermute | solution.py:242
  14.8 28.0 %collective-permute-start.6 = (bf16[128,2048]{1,0:T(8,128)(2,1)}, bf16[128,2048]{1,0:T(8,128)(2,1)S(1)}, u32[]{:S(2)}, u32[]{:S(2)}) collective-permute-start(bf16[128,2048]{1,0:T(8,128)(2,1)} %get-tuple-element.91), channel_id=1, source_target_pairs={{2,0},{4,2},{6,4},{8,6},{10,8},{12,10},{14,12},{0,14},{3,1},{5,3},... | collective-permute-start | bytes 1572872 | tf_op jit(solution)/shard_map/ppermute | solution.py:240
  20.8 22.0 %collective-permute-start.5 = (bf16[128,2048]{1,0:T(8,128)(2,1)}, bf16[128,2048]{1,0:T(8,128)(2,1)S(1)}, u32[]{:S(2)}, u32[]{:S(2)}) collective-permute-start(bf16[128,2048]{1,0:T(8,128)(2,1)} %get-tuple-element.92), channel_id=1, source_target_pairs={{0,2},{2,4},{4,6},{6,8},{8,10},{10,12},{12,14},{14,0},{1,3},{3,5},... | collective-permute-start | bytes 1572872 | tf_op jit(solution)/shard_map/ppermute | solution.py:239
  23.1 19.7 %collective-permute-start.8 = (bf16[128,2048]{1,0:T(8,128)(2,1)S(1)}, bf16[128,2048]{1,0:T(8,128)(2,1)S(1)}, u32[]{:S(2)}, u32[]{:S(2)}) collective-permute-start(bf16[128,2048]{1,0:T(8,128)(2,1)S(1)} %collective-permute-done.7.split_ref), channel_id=1, source_target_pairs={{0,16},{16,0},{1,17},{17,1},{2,18},{18,2},{3,19},{19,3},{4,20},{20... | collective-permute-start | bytes 1572872 | tf_op jit(solution)/shard_map/ppermute | solution.py:243
  24.4 2.0 %collective-permute-start.4 = (bf16[3,7,64,128]{3,2,1,0:T(8,128)(2,1)}, bf16[3,7,64,128]{3,2,1,0:T(8,128)(2,1)}, u32[]{:S(2)}, u32[]{:S(2)}) collective-permute-start(bf16[3,7,64,128]{3,2,1,0:T(8,128)(2,1)} %collective-permute-done.2.refs_1_), channel_id=1, source_target_pairs={{0,1},{1,0},{2,3},{3,2},{4,5},{5,4},{6,7},{7,6},{8,9},{9,8},{10,11... | collective-permute-start | bytes 1032200 | tf_op jit(solution)/shard_map/ppermute | solution.py:242
  47.6 15.2 %collective-permute-start.9 = (bf16[256,1024]{1,0:T(8,128)(2,1)S(1)}, bf16[256,1024]{1,0:T(8,128)(2,1)S(1)}, u32[]{:S(2)}, u32[]{:S(2)}) collective-permute-start(bf16[256,1024]{1,0:T(8,128)(2,1)S(1)} %get-tuple-element.55), channel_id=1, source_target_pairs={{0,2},{2,0},{4,6},{6,4},{8,10},{10,8},{12,14},{14,12},{1,3},{3,1},... | collective-permute-start | bytes 1572872 | tf_op jit(solution)/shard_map/ppermute | solution.py:287
  50.0 21.9 %collective-permute-start.12 = (bf16[256,1024]{1,0:T(8,128)(2,1)S(1)}, bf16[256,1024]{1,0:T(8,128)(2,1)S(1)}, u32[]{:S(2)}, u32[]{:S(2)}) collective-permute-start(bf16[256,1024]{1,0:T(8,128)(2,1)S(1)} %get-tuple-element.66), channel_id=1, source_target_pairs={{0,4},{2,6},{4,0},{6,2},{8,12},{10,14},{12,8},{14,10},{1,5},{3,7},... | collective-permute-start | bytes 1572872 | tf_op jit(solution)/shard_map/ppermute | solution.py:290
  56.4 20.5 %collective-permute-start.11 = (bf16[256,1024]{1,0:T(8,128)(2,1)S(1)}, bf16[256,1024]{1,0:T(8,128)(2,1)S(1)}, u32[]{:S(2)}, u32[]{:S(2)}) collective-permute-start(bf16[256,1024]{1,0:T(8,128)(2,1)S(1)} %get-tuple-element.64), channel_id=1, source_target_pairs={{0,2},{2,0},{4,6},{6,4},{8,10},{10,8},{12,14},{14,12},{1,3},{3,1},... | collective-permute-start | bytes 1572872 | tf_op jit(solution)/shard_map/ppermute | solution.py:287
  62.9 14.9 %collective-permute-start.13 = (bf16[256,1024]{1,0:T(8,128)(2,1)S(1)}, bf16[256,1024]{1,0:T(8,128)(2,1)S(1)}, u32[]{:S(2)}, u32[]{:S(2)}) collective-permute-start(bf16[256,1024]{1,0:T(8,128)(2,1)S(1)} %add_convert_fusion.5), channel_id=1, source_target_pairs={{0,4},{2,6},{4,0},{6,2},{8,12},{10,14},{12,8},{14,10},{1,5},{3,7},... | collective-permute-start | bytes 1572872 | tf_op jit(solution)/shard_map/ppermute | solution.py:290
  64.5 34.4 %collective-permute-start.16 = (bf16[256,1024]{1,0:T(8,128)(2,1)S(1)}, bf16[256,1024]{1,0:T(8,128)(2,1)S(1)}, u32[]{:S(2)}, u32[]{:S(2)}) collective-permute-start(bf16[256,1024]{1,0:T(8,128)(2,1)S(1)} %get-tuple-element.75), channel_id=1, source_target_pairs={{0,2},{2,0},{4,6},{6,4},{8,10},{10,8},{12,14},{14,12},{1,3},{3,1},... | collective-permute-start | bytes 1572872 | tf_op jit(solution)/shard_map/ppermute | solution.py:287
  66.6 30.8 %collective-permute-start.10 = (bf16[256,1024]{1,0:T(8,128)(2,1)S(1)}, bf16[256,1024]{1,0:T(8,128)(2,1)S(1)}, u32[]{:S(2)}, u32[]{:S(2)}) collective-permute-start(bf16[256,1024]{1,0:T(8,128)(2,1)S(1)} %get-tuple-element.62), channel_id=1, source_target_pairs={{0,4},{2,6},{4,0},{6,2},{8,12},{10,14},{12,8},{14,10},{1,5},{3,7},... | collective-permute-start | bytes 1572872 | tf_op jit(solution)/shard_map/ppermute | solution.py:290
  76.9 34.1 %collective-permute-start.18 = (bf16[256,1024]{1,0:T(8,128)(2,1)S(1)}, bf16[256,1024]{1,0:T(8,128)(2,1)S(1)}, u32[]{:S(2)}, u32[]{:S(2)}) collective-permute-start(bf16[256,1024]{1,0:T(8,128)(2,1)S(1)} %get-tuple-element.83), channel_id=1, source_target_pairs={{0,2},{2,0},{4,6},{6,4},{8,10},{10,8},{12,14},{14,12},{1,3},{3,1},... | collective-permute-start | bytes 1572872 | tf_op jit(solution)/shard_map/ppermute | solution.py:287
  78.1 32.7 %collective-permute-start.14 = (bf16[256,1024]{1,0:T(8,128)(2,1)S(1)}, bf16[256,1024]{1,0:T(8,128)(2,1)S(1)}, u32[]{:S(2)}, u32[]{:S(2)}) collective-permute-start(bf16[256,1024]{1,0:T(8,128)(2,1)S(1)} %add_convert_fusion.3), channel_id=1, source_target_pairs={{0,8},{2,10},{4,12},{6,14},{8,0},{10,2},{12,4},{14,6},{1,9},{3,11}... | collective-permute-start | bytes 1572872 | tf_op jit(solution)/shard_map/ppermute | solution.py:296
  97.4 11.9 %collective-permute-start.15 = (bf16[256,1024]{1,0:T(8,128)(2,1)S(1)}, bf16[256,1024]{1,0:T(8,128)(2,1)S(1)}, u32[]{:S(2)}, u32[]{:S(2)}) collective-permute-start(bf16[256,1024]{1,0:T(8,128)(2,1)S(1)} %get-tuple-element.74), channel_id=1, source_target_pairs={{0,2},{2,0},{4,6},{6,4},{8,10},{10,8},{12,14},{14,12},{1,3},{3,1},... | collective-permute-start | bytes 1572872 | tf_op jit(solution)/shard_map/ppermute | solution.py:287
  99.1 11.9 %collective-permute-start.19 = (bf16[256,1024]{1,0:T(8,128)(2,1)S(1)}, bf16[256,1024]{1,0:T(8,128)(2,1)S(1)}, u32[]{:S(2)}, u32[]{:S(2)}) collective-permute-start(bf16[256,1024]{1,0:T(8,128)(2,1)S(1)} %add_convert_fusion.2), channel_id=1, source_target_pairs={{0,4},{2,6},{4,0},{6,2},{8,12},{10,14},{12,8},{14,10},{1,5},{3,7},... | collective-permute-start | bytes 1572872 | tf_op jit(solution)/shard_map/ppermute | solution.py:290
  109.4 13.7 %collective-permute-start.17 = (bf16[256,1024]{1,0:T(8,128)(2,1)S(1)}, bf16[256,1024]{1,0:T(8,128)(2,1)S(1)}, u32[]{:S(2)}, u32[]{:S(2)}) collective-permute-start(bf16[256,1024]{1,0:T(8,128)(2,1)S(1)} %add_convert_fusion.4), channel_id=1, source_target_pairs={{0,2},{2,0},{4,6},{6,4},{8,10},{10,8},{12,14},{14,12},{1,3},{3,1},... | collective-permute-start | bytes 1572872 | tf_op jit(solution)/shard_map/ppermute | solution.py:287
  111.2 25.3 %collective-permute-start.20 = (bf16[256,1024]{1,0:T(8,128)(2,1)S(1)}, bf16[256,1024]{1,0:T(8,128)(2,1)S(1)}, u32[]{:S(2)}, u32[]{:S(2)}) collective-permute-start(bf16[256,1024]{1,0:T(8,128)(2,1)S(1)} %add_convert_fusion), channel_id=1, source_target_pairs={{0,8},{2,10},{4,12},{6,14},{8,0},{10,2},{12,4},{14,6},{1,9},{3,11}... | collective-permute-start | bytes 1572872 | tf_op jit(solution)/shard_map/ppermute | solution.py:296
  114.6 22.2 %collective-permute-start.21 = (bf16[256,1024]{1,0:T(8,128)(2,1)S(1)}, bf16[256,1024]{1,0:T(8,128)(2,1)S(1)}, u32[]{:S(2)}, u32[]{:S(2)}) collective-permute-start(bf16[256,1024]{1,0:T(8,128)(2,1)S(1)} %add_convert_fusion.1), channel_id=1, source_target_pairs={{0,4},{2,6},{4,0},{6,2},{8,12},{10,14},{12,8},{14,10},{1,5},{3,7},... | collective-permute-start | bytes 1572872 | tf_op jit(solution)/shard_map/ppermute | solution.py:290
  117.1 19.7 %collective-permute-start.22 = (bf16[256,1024]{1,0:T(8,128)(2,1)S(1)}, bf16[256,1024]{1,0:T(8,128)(2,1)S(1)}, u32[]{:S(2)}, u32[]{:S(2)}) collective-permute-start(bf16[256,1024]{1,0:T(8,128)(2,1)S(1)} %get-tuple-element.88), channel_id=1, source_target_pairs={{0,2},{2,0},{4,6},{6,4},{8,10},{10,8},{12,14},{14,12},{1,3},{3,1},... | collective-permute-start | bytes 1572872 | tf_op jit(solution)/shard_map/ppermute | solution.py:287
  (5 other events, 53.0 us)

commit v7 on v6

--- a/solution.py
+++ b/solution.py
@@ -314,16 +314,16 @@
     far_c0_sum = far_c0
     far_c0 = to_pair(far_c0)
     far_a1 = to_side(far_a1)
-    near_c0 = add(near_c0, after(near_a0, own0))
-    far_b1, near_b1, far_c1 = unit_half(1, (2, 3, 4), after(rim1, near_c0), BF16, F32, F32)
+    far_b1, near_b1, far_c1 = unit_half(1, (2, 3, 4), after(rim1, own0), BF16, F32, F32)
+    near_c0 = add(near_c0, after(near_a0, far_c1))
     far_b1 = to_side(far_b1)
     far_d0 = add(far_d0, after(far_b0, far_c1), far_c0)
     near_b0 = to_pair(after(near_b0, far_c0_sum))
     near_a1 = to_side(after(near_a1, far_d0))
-    own0 = add32(own0, after(near_b0, far_d0))
-    far_c1 = add(far_c1, after(far_a1, own0))
+    far_c1 = add(far_c1, after(far_a1, far_d0))
+    own0 = add32(own0, after(near_b0, far_c1))
     far_d0 = to_far(far_d0)
-    near_c1, far_d1, own1 = unit_half(1, (5, 6, 7), after(rim1, far_c1), BF16, F32, F32)
+    near_c1, far_d1, own1 = unit_half(1, (5, 6, 7), after(rim1, own0), BF16, F32, F32)
     far_c1 = to_pair(far_c1)
     near_b1 = add(near_b1, after(near_a1, far_d1))
     near_c0, near_c1 = after((near_c0, near_c1), near_b1)

time: 139 us -> 138 us (level)
  waiting for transfers between devices: 50.9 us -> 47 us
  starting transfers between devices: 36.7 us -> 39.7 us
    ppermute x5, waiting for transfers between devices: 16.2 us -> 11.5 us  [to_pair(): return lax.ppermute(x, 'row', swap_pair)]
  transfers between devices with their start and end apart: 23 -> 23, of which waited for: 11 -> 13; matrix products, arithmetic and copies ran while one was open for 3% -> 3% of each run, Pallas kernels for 24% -> 24%
where the time goes in v7:
time: 138 us; the launch traced here: 137 us
  waiting for transfers between devices  47 us (34%)
  starting transfers between devices  39.7 us (29%)
  Pallas kernels  38.8 us (28%)
  local copies, waits for them, and re-layouts  9.83 us (7%)
  other arithmetic  1.71 us (1%)
    pallas_call x8, Pallas kernels, call(): pl.pallas_call(kernel, grid_spec=pltpu.PrefetchScalarGridSpec(num_scalar_...  38.8 us
    ppermute x2, waiting for transfers between devices, to_far(): parts.append(lax.ppermute(x[i * height:(i + 1) * height], 'row', route))  13.3 us
    ppermute x7, waiting for transfers between devices, to_side(): return lax.ppermute(x, 'row', swap_side)  12.1 us
    ppermute x5, waiting for transfers between devices, to_pair(): return lax.ppermute(x, 'row', swap_pair)  11.5 us
    ppermute x7, starting transfers between devices, to_side(): return lax.ppermute(x, 'row', swap_side)  9.99 us
    ppermute x2, starting transfers between devices, to_far(): parts.append(lax.ppermute(x[i * height:(i + 1) * height], 'row', route))  8.34 us
    ppermute x5, starting transfers between devices, to_pair(): return lax.ppermute(x, 'row', swap_pair)  6.99 us
    ppermute x1, starting transfers between devices, per_device(): from_after = lax.ppermute(behind[:block], 'row', down)  5.23 us
  transfers between devices with their start and end apart: 23, of which 13 were waited for; matrix products, arithmetic and copies ran while one was open for 3% of the time, Pallas kernels for 24%

profile of v7, /device:TPU:0, one launch (start us, length us, event | category | flops | bytes accessed | tf_op | source)
XLA Modules:
  0.0 137.3 jit_solution(2996736950746048342)
XLA Ops:
  3.7 2.6 %collective-permute-start.1 = (bf16[2,7,64,128]{3,2,1,0:T(8,128)(2,1)S(1)}, bf16[2,7,64,128]{3,2,1,0:T(8,128)(2,1)S(1)}, u32[]{:S(2)}, u32[]{:S(2)}) collective-permute-start(bf16[2,7,64,128]{3,2,1,0:T(8,128)(2,1)S(1)} %constant_dynamic-slice_fusion.1), channel_id=1, source_target_pairs={{0,16},{16,0},{1,17},{17,1},{2,18},{18,2},{3,19},{19,3},{4,20},{20... | collective-permute-start | bytes 688136 | tf_op jit(solution)/shard_map/ppermute | solution.py:238
  6.3 4.5 %collective-permute-start.7 = (bf16[128,2048]{1,0:T(8,128)(2,1)S(1)}, bf16[128,2048]{1,0:T(8,128)(2,1)S(1)}, u32[]{:S(2)}, u32[]{:S(2)}) collective-permute-start(bf16[128,2048]{1,0:T(8,128)(2,1)S(1)} %constant_dynamic-slice_fusion.2), channel_id=1, source_target_pairs={{2,0},{4,2},{6,4},{8,6},{10,8},{12,10},{14,12},{0,14},{16,18},{18,... | collective-permute-start | bytes 1572872 | tf_op jit(solution)/shard_map/ppermute | solution.py:231
  12.5 2.3 %fusion = (bf16[128,2048]{1,0:T(8,128)(2,1)}, bf16[128,2048]{1,0:T(8,128)(2,1)}) fusion(bf16[1280,2048]{1,0:T(8,128)(2,1)} %here.7), kind=kLoop, calls=%fused_computation.13 | loop fusion | bytes 2097152 | tf_op jit(solution)/shard_map/slice | solution.py:240
  14.8 5.2 %collective-permute-start.6 = (bf16[128,2048]{1,0:T(8,128)(2,1)}, bf16[128,2048]{1,0:T(8,128)(2,1)S(1)}, u32[]{:S(2)}, u32[]{:S(2)}) collective-permute-start(bf16[128,2048]{1,0:T(8,128)(2,1)} %get-tuple-element.91), channel_id=1, source_target_pairs={{2,0},{4,2},{6,4},{8,6},{10,8},{12,10},{14,12},{0,14},{3,1},{5,3},... | collective-permute-start | bytes 1572872 | tf_op jit(solution)/shard_map/ppermute | solution.py:240
  26.4 2.5 %copy-done = bf16[1280,2048]{1,0:T(8,128)(2,1)S(1)} copy-done((bf16[1280,2048]{1,0:T(8,128)(2,1)S(1)}, bf16[1280,2048]{1,0:T(8,128)(2,1)}, u32[]{:S(2)}) %copy-start) | copy-done | bytes 5242904
  29.8 8.4 %inner_rows.1 = (bf16[2,768,1024]{2,1,0:T(8,128)(2,1)S(1)}, f32[2,2,256,1024]{3,2,1,0:T(8,128)S(1)}, bf16[4,128,896]{2,1,0:T(8,128)(2,1)S(1)}) custom-call(s32[10,7]{1,0:T(8,128)S(1)} %copy.5.nb_ref, s32[10,7]{1,0:T(8,128)S(1)} %copy.6.mask_ref, s32[1]{0:T(128)} %bitcast.sec_ref, s32[1]{0:T(128)} %bitcast.1.col_ref, s32[1]{0:T(128)} %bitcast.2.row_ref, ...), custom_call_target="tpu_custom_call" | custom-call | flops 1 | bytes 1 | tf_op jit(solution)/shard_map/inner_rows/pallas_call | solution.py:16
  38.2 4.5 %collective-permute-done.6.down_ref = bf16[128,2048]{1,0:T(8,128)(2,1)S(1)} collective-permute-done((bf16[128,2048]{1,0:T(8,128)(2,1)}, bf16[128,2048]{1,0:T(8,128)(2,1)S(1)}, u32[]{:S(2)}, u32[]{:S(2)}) %collective-permute-start.6) | collective-permute-done | bytes 524320 | tf_op jit(solution)/shard_map/ppermute | solution.py:240
  42.8 4.8 %rim_rows.2 = (bf16[512,1024]{1,0:T(8,128)(2,1)S(1)}, bf16[256,1024]{1,0:T(8,128)(2,1)S(1)}, bf16[256,1024]{1,0:T(8,128)(2,1)S(1)}) custom-call(s32[10,7]{1,0:T(8,128)S(1)} %copy.5.nb_ref, s32[10,7]{1,0:T(8,128)S(1)} %copy.6.mask_ref, s32[1]{0:T(128)} %bitcast.sec_ref, s32[1]{0:T(128)} %bitcast.1.col_ref, s32[1]{0:T(128)} %bitcast.2.row_ref, ...), custom_call_target="tpu_custom_call" | custom-call | flops 1 | bytes 1 | tf_op jit(solution)/shard_map/rim_rows/pallas_call | solution.py:16
  47.6 2.4 %collective-permute-start.9 = (bf16[256,1024]{1,0:T(8,128)(2,1)S(1)}, bf16[256,1024]{1,0:T(8,128)(2,1)S(1)}, u32[]{:S(2)}, u32[]{:S(2)}) collective-permute-start(bf16[256,1024]{1,0:T(8,128)(2,1)S(1)} %get-tuple-element.55), channel_id=1, source_target_pairs={{0,2},{2,0},{4,6},{6,4},{8,10},{10,8},{12,14},{14,12},{1,3},{3,1},... | collective-permute-start | bytes 1572872 | tf_op jit(solution)/shard_map/ppermute | solution.py:287
  51.6 4.8 %units.4 = (bf16[256,1024]{1,0:T(8,128)(2,1)S(1)}, bf16[256,1024]{1,0:T(8,128)(2,1)S(1)}, f32[256,1024]{1,0:T(8,128)S(1)}) custom-call(s32[1]{0:T(128)} %bitcast.sec_ref, s32[1]{0:T(128)} %bitcast.1.col_ref, s32[1]{0:T(128)} %bitcast.2.row_ref, s32[8]{0:T(128)S(1)} %stack.35.index_ref, bf16[1280,2048]{1,0:T(8,128)(2,1)S(1)} %copy-done, ...), custom_call_target="tpu_custom_call" | custom-call | flops 1 | bytes 1 | tf_op jit(solution)/shard_map/units/pallas_call | solution.py:16
  56.6 4.8 %rim_rows.3 = (bf16[512,1024]{1,0:T(8,128)(2,1)S(1)}, bf16[256,1024]{1,0:T(8,128)(2,1)S(1)}, bf16[256,1024]{1,0:T(8,128)(2,1)S(1)}) custom-call(s32[10,7]{1,0:T(8,128)S(1)} %copy.5.nb_ref, s32[10,7]{1,0:T(8,128)S(1)} %copy.6.mask_ref, s32[1]{0:T(128)} %bitcast.sec_ref, s32[1]{0:T(128)} %bitcast.1.col_ref, s32[1]{0:T(128)} %bitcast.2.row_ref, ...), custom_call_target="tpu_custom_call" | custom-call | flops 1 | bytes 1 | tf_op jit(solution)/shard_map/rim_rows/pallas_call | solution.py:16
  64.5 2.1 %collective-permute-start.11 = (bf16[256,1024]{1,0:T(8,128)(2,1)S(1)}, bf16[256,1024]{1,0:T(8,128)(2,1)S(1)}, u32[]{:S(2)}, u32[]{:S(2)}) collective-permute-start(bf16[256,1024]{1,0:T(8,128)(2,1)S(1)} %get-tuple-element.65), channel_id=1, source_target_pairs={{0,2},{2,0},{4,6},{6,4},{8,10},{10,8},{12,14},{14,12},{1,3},{3,1},... | collective-permute-start | bytes 1572872 | tf_op jit(solution)/shard_map/ppermute | solution.py:287
  67.0 4.8 %units.5 = (f32[256,1024]{1,0:T(8,128)S(1)}, f32[256,1024]{1,0:T(8,128)S(1)}, f32[256,1024]{1,0:T(8,128)S(1)}) custom-call(s32[1]{0:T(128)} %bitcast.sec_ref, s32[1]{0:T(128)} %bitcast.1.col_ref, s32[1]{0:T(128)} %bitcast.2.row_ref, s32[8]{0:T(128)S(1)} %stack.35.index_ref, bf16[1280,2048]{1,0:T(8,128)(2,1)S(1)} %copy-done, ...), custom_call_target="tpu_custom_call" | custom-call | flops 1 | bytes 1 | tf_op jit(solution)/shard_map/units/pallas_call | solution.py:16
  71.9 4.8 %units.6 = (bf16[256,1024]{1,0:T(8,128)(2,1)S(1)}, f32[256,1024]{1,0:T(8,128)S(1)}, f32[256,1024]{1,0:T(8,128)S(1)}) custom-call(s32[1]{0:T(128)} %bitcast.sec_ref, s32[1]{0:T(128)} %bitcast.1.col_ref, s32[1]{0:T(128)} %bitcast.2.row_ref, s32[8]{0:T(128)S(1)} %stack.35.index_ref, bf16[1280,2048]{1,0:T(8,128)(2,1)S(1)} %copy-done, ...), custom_call_target="tpu_custom_call" | custom-call | flops 1 | bytes 1 | tf_op jit(solution)/shard_map/units/pallas_call | solution.py:16
  78.1 4.0 %collective-permute-start.14 = (bf16[256,1024]{1,0:T(8,128)(2,1)S(1)}, bf16[256,1024]{1,0:T(8,128)(2,1)S(1)}, u32[]{:S(2)}, u32[]{:S(2)}) collective-permute-start(bf16[256,1024]{1,0:T(8,128)(2,1)S(1)} %add_convert_fusion.4), channel_id=1, source_target_pairs={{0,8},{2,10},{4,12},{6,14},{8,0},{10,2},{12,4},{14,6},{1,9},{3,11}... | collective-permute-start | bytes 1572872 | tf_op jit(solution)/shard_map/ppermute | solution.py:296
  82.1 3.2 %collective-permute-done.11 = bf16[256,1024]{1,0:T(8,128)(2,1)S(1)} collective-permute-done((bf16[256,1024]{1,0:T(8,128)(2,1)S(1)}, bf16[256,1024]{1,0:T(8,128)(2,1)S(1)}, u32[]{:S(2)}, u32[]{:S(2)}) %collective-permute-start.11) | collective-permute-done | bytes 524320 | tf_op jit(solution)/shard_map/ppermute | solution.py:287
  85.2 2.1 %collective-permute-start.15 = (bf16[256,1024]{1,0:T(8,128)(2,1)S(1)}, bf16[256,1024]{1,0:T(8,128)(2,1)S(1)}, u32[]{:S(2)}, u32[]{:S(2)}) collective-permute-start(bf16[256,1024]{1,0:T(8,128)(2,1)S(1)} %get-tuple-element.73), channel_id=1, source_target_pairs={{0,2},{2,0},{4,6},{6,4},{8,10},{10,8},{12,14},{14,12},{1,3},{3,1},... | collective-permute-start | bytes 1572872 | tf_op jit(solution)/shard_map/ppermute | solution.py:287
  89.1 10.5 %collective-permute-done.10 = bf16[256,1024]{1,0:T(8,128)(2,1)S(1)} collective-permute-done((bf16[256,1024]{1,0:T(8,128)(2,1)S(1)}, bf16[256,1024]{1,0:T(8,128)(2,1)S(1)}, u32[]{:S(2)}, u32[]{:S(2)}) %collective-permute-start.10) | collective-permute-done | bytes 524320 | tf_op jit(solution)/shard_map/ppermute | solution.py:290
  99.7 4.8 %units.7 = (bf16[256,1024]{1,0:T(8,128)(2,1)S(1)}, f32[256,1024]{1,0:T(8,128)S(1)}, f32[256,1024]{1,0:T(8,128)S(1)}) custom-call(s32[1]{0:T(128)} %bitcast.sec_ref, s32[1]{0:T(128)} %bitcast.1.col_ref, s32[1]{0:T(128)} %bitcast.2.row_ref, s32[8]{0:T(128)S(1)} %stack.35.index_ref, bf16[1280,2048]{1,0:T(8,128)(2,1)S(1)} %copy-done, ...), custom_call_target="tpu_custom_call" | custom-call | flops 1 | bytes 1 | tf_op jit(solution)/shard_map/units/pallas_call | solution.py:16
  104.5 2.5 %collective-permute-done.15 = bf16[256,1024]{1,0:T(8,128)(2,1)S(1)} collective-permute-done((bf16[256,1024]{1,0:T(8,128)(2,1)S(1)}, bf16[256,1024]{1,0:T(8,128)(2,1)S(1)}, u32[]{:S(2)}, u32[]{:S(2)}) %collective-permute-start.15) | collective-permute-done | bytes 524320 | tf_op jit(solution)/shard_map/ppermute | solution.py:287
  107.2 1.8 %collective-permute-start.17 = (bf16[256,1024]{1,0:T(8,128)(2,1)S(1)}, bf16[256,1024]{1,0:T(8,128)(2,1)S(1)}, u32[]{:S(2)}, u32[]{:S(2)}) collective-permute-start(bf16[256,1024]{1,0:T(8,128)(2,1)S(1)} %add_convert_fusion.1), channel_id=1, source_target_pairs={{0,2},{2,0},{4,6},{6,4},{8,10},{10,8},{12,14},{14,12},{1,3},{3,1},... | collective-permute-start | bytes 1572872 | tf_op jit(solution)/shard_map/ppermute | solution.py:287
  109.6 4.3 %collective-permute-start.20 = (bf16[256,1024]{1,0:T(8,128)(2,1)S(1)}, bf16[256,1024]{1,0:T(8,128)(2,1)S(1)}, u32[]{:S(2)}, u32[]{:S(2)}) collective-permute-start(bf16[256,1024]{1,0:T(8,128)(2,1)S(1)} %add_convert_fusion), channel_id=1, source_target_pairs={{0,8},{2,10},{4,12},{6,14},{8,0},{10,2},{12,4},{14,6},{1,9},{3,11}... | collective-permute-start | bytes 1572872 | tf_op jit(solution)/shard_map/ppermute | solution.py:296
  117.1 5.1 %collective-permute-done.17 = bf16[256,1024]{1,0:T(8,128)(2,1)S(1)} collective-permute-done((bf16[256,1024]{1,0:T(8,128)(2,1)S(1)}, bf16[256,1024]{1,0:T(8,128)(2,1)S(1)}, u32[]{:S(2)}, u32[]{:S(2)}) %collective-permute-start.17) | collective-permute-done | bytes 524320 | tf_op jit(solution)/shard_map/ppermute | solution.py:287
  122.3 13.3 %collective-permute-done.20 = bf16[256,1024]{1,0:T(8,128)(2,1)S(1)} collective-permute-done((bf16[256,1024]{1,0:T(8,128)(2,1)S(1)}, bf16[256,1024]{1,0:T(8,128)(2,1)S(1)}, u32[]{:S(2)}, u32[]{:S(2)}) %collective-permute-start.20) | collective-permute-done | bytes 524320 | tf_op jit(solution)/shard_map/ppermute | solution.py:296
  (59 shorter events, 26.8 us)
Async XLA Ops:
  0.0 26.4 %copy-start.1 = (bf16[10,7,64,128]{3,2,1,0:T(8,128)(2,1)S(1)}, bf16[10,7,64,128]{3,2,1,0:T(8,128)(2,1)}, u32[]{:S(2)}) copy-start(bf16[10,7,64,128]{3,2,1,0:T(8,128)(2,1)} %own_ref.1) | copy-start | bytes 3440644
  3.2 23.2 %collective-permute-start = (bf16[1280,2048]{1,0:T(8,128)(2,1)}, bf16[1280,2048]{1,0:T(8,128)(2,1)}, u32[]{:S(2)}, u32[]{:S(2)}) collective-permute-start(bf16[1280,2048]{1,0:T(8,128)(2,1)} %here.7), channel_id=1, source_target_pairs={{0,1},{1,0},{2,3},{3,2},{4,5},{5,4},{6,7},{7,6},{8,9},{9,8},{10,11... | collective-permute-start | bytes 15728648 | tf_op jit(solution)/shard_map/ppermute | solution.py:241
  3.7 8.8 %collective-permute-start.1 = (bf16[2,7,64,128]{3,2,1,0:T(8,128)(2,1)S(1)}, bf16[2,7,64,128]{3,2,1,0:T(8,128)(2,1)S(1)}, u32[]{:S(2)}, u32[]{:S(2)}) collective-permute-start(bf16[2,7,64,128]{3,2,1,0:T(8,128)(2,1)S(1)} %constant_dynamic-slice_fusion.1), channel_id=1, source_target_pairs={{0,16},{16,0},{1,17},{17,1},{2,18},{18,2},{3,19},{19,3},{4,20},{20... | collective-permute-start | bytes 688136 | tf_op jit(solution)/shard_map/ppermute | solution.py:238
  6.3 16.8 %collective-permute-start.7 = (bf16[128,2048]{1,0:T(8,128)(2,1)S(1)}, bf16[128,2048]{1,0:T(8,128)(2,1)S(1)}, u32[]{:S(2)}, u32[]{:S(2)}) collective-permute-start(bf16[128,2048]{1,0:T(8,128)(2,1)S(1)} %constant_dynamic-slice_fusion.2), channel_id=1, source_target_pairs={{2,0},{4,2},{6,4},{8,6},{10,8},{12,10},{14,12},{0,14},{16,18},{18,... | collective-permute-start | bytes 1572872 | tf_op jit(solution)/shard_map/ppermute | solution.py:231
  10.8 10.0 %collective-permute-start.2 = (bf16[3,7,64,128]{3,2,1,0:T(8,128)(2,1)S(1)}, bf16[3,7,64,128]{3,2,1,0:T(8,128)(2,1)}, u32[]{:S(2)}, u32[]{:S(2)}) collective-permute-start(bf16[3,7,64,128]{3,2,1,0:T(8,128)(2,1)S(1)} %constant_dynamic-slice_fusion), channel_id=1, source_target_pairs={{0,16},{16,0},{1,17},{17,1},{2,18},{18,2},{3,19},{19,3},{4,20},{20... | collective-permute-start | bytes 1032200 | tf_op jit(solution)/shard_map/ppermute | solution.py:238
  12.5 11.2 %collective-permute-start.3 = (bf16[2,7,64,128]{3,2,1,0:T(8,128)(2,1)S(1)}, bf16[2,7,64,128]{3,2,1,0:T(8,128)(2,1)S(1)}, u32[]{:S(2)}, u32[]{:S(2)}) collective-permute-start(bf16[2,7,64,128]{3,2,1,0:T(8,128)(2,1)S(1)} %collective-permute-done.1.refs_0_), channel_id=1, source_target_pairs={{0,1},{1,0},{2,3},{3,2},{4,5},{5,4},{6,7},{7,6},{8,9},{9,8},{10,11... | collective-permute-start | bytes 688136 | tf_op jit(solution)/shard_map/ppermute | solution.py:242
  14.8 28.0 %collective-permute-start.6 = (bf16[128,2048]{1,0:T(8,128)(2,1)}, bf16[128,2048]{1,0:T(8,128)(2,1)S(1)}, u32[]{:S(2)}, u32[]{:S(2)}) collective-permute-start(bf16[128,2048]{1,0:T(8,128)(2,1)} %get-tuple-element.91), channel_id=1, source_target_pairs={{2,0},{4,2},{6,4},{8,6},{10,8},{12,10},{14,12},{0,14},{3,1},{5,3},... | collective-permute-start | bytes 1572872 | tf_op jit(solution)/shard_map/ppermute | solution.py:240
  20.8 22.0 %collective-permute-start.5 = (bf16[128,2048]{1,0:T(8,128)(2,1)}, bf16[128,2048]{1,0:T(8,128)(2,1)S(1)}, u32[]{:S(2)}, u32[]{:S(2)}) collective-permute-start(bf16[128,2048]{1,0:T(8,128)(2,1)} %get-tuple-element.92), channel_id=1, source_target_pairs={{0,2},{2,4},{4,6},{6,8},{8,10},{10,12},{12,14},{14,0},{1,3},{3,5},... | collective-permute-start | bytes 1572872 | tf_op jit(solution)/shard_map/ppermute | solution.py:239
  23.1 19.7 %collective-permute-start.8 = (bf16[128,2048]{1,0:T(8,128)(2,1)S(1)}, bf16[128,2048]{1,0:T(8,128)(2,1)S(1)}, u32[]{:S(2)}, u32[]{:S(2)}) collective-permute-start(bf16[128,2048]{1,0:T(8,128)(2,1)S(1)} %collective-permute-done.7.split_ref), channel_id=1, source_target_pairs={{0,16},{16,0},{1,17},{17,1},{2,18},{18,2},{3,19},{19,3},{4,20},{20... | collective-permute-start | bytes 1572872 | tf_op jit(solution)/shard_map/ppermute | solution.py:243
  24.4 2.0 %collective-permute-start.4 = (bf16[3,7,64,128]{3,2,1,0:T(8,128)(2,1)}, bf16[3,7,64,128]{3,2,1,0:T(8,128)(2,1)}, u32[]{:S(2)}, u32[]{:S(2)}) collective-permute-start(bf16[3,7,64,128]{3,2,1,0:T(8,128)(2,1)} %collective-permute-done.2.refs_1_), channel_id=1, source_target_pairs={{0,1},{1,0},{2,3},{3,2},{4,5},{5,4},{6,7},{7,6},{8,9},{9,8},{10,11... | collective-permute-start | bytes 1032200 | tf_op jit(solution)/shard_map/ppermute | solution.py:242
  47.6 15.2 %collective-permute-start.9 = (bf16[256,1024]{1,0:T(8,128)(2,1)S(1)}, bf16[256,1024]{1,0:T(8,128)(2,1)S(1)}, u32[]{:S(2)}, u32[]{:S(2)}) collective-permute-start(bf16[256,1024]{1,0:T(8,128)(2,1)S(1)} %get-tuple-element.55), channel_id=1, source_target_pairs={{0,2},{2,0},{4,6},{6,4},{8,10},{10,8},{12,14},{14,12},{1,3},{3,1},... | collective-permute-start | bytes 1572872 | tf_op jit(solution)/shard_map/ppermute | solution.py:287
  50.0 26.7 %collective-permute-start.16 = (bf16[256,1024]{1,0:T(8,128)(2,1)S(1)}, bf16[256,1024]{1,0:T(8,128)(2,1)S(1)}, u32[]{:S(2)}, u32[]{:S(2)}) collective-permute-start(bf16[256,1024]{1,0:T(8,128)(2,1)S(1)} %get-tuple-element.79), channel_id=1, source_target_pairs={{0,4},{2,6},{4,0},{6,2},{8,12},{10,14},{12,8},{14,10},{1,5},{3,7},... | collective-permute-start | bytes 1572872 | tf_op jit(solution)/shard_map/ppermute | solution.py:290
  56.4 20.3 %collective-permute-start.12 = (bf16[256,1024]{1,0:T(8,128)(2,1)S(1)}, bf16[256,1024]{1,0:T(8,128)(2,1)S(1)}, u32[]{:S(2)}, u32[]{:S(2)}) collective-permute-start(bf16[256,1024]{1,0:T(8,128)(2,1)S(1)} %get-tuple-element.67), channel_id=1, source_target_pairs={{0,2},{2,0},{4,6},{6,4},{8,10},{10,8},{12,14},{14,12},{1,3},{3,1},... | collective-permute-start | bytes 1572872 | tf_op jit(solution)/shard_map/ppermute | solution.py:287
  62.9 14.9 %collective-permute-start.13 = (bf16[256,1024]{1,0:T(8,128)(2,1)S(1)}, bf16[256,1024]{1,0:T(8,128)(2,1)S(1)}, u32[]{:S(2)}, u32[]{:S(2)}) collective-permute-start(bf16[256,1024]{1,0:T(8,128)(2,1)S(1)} %add_convert_fusion.5), channel_id=1, source_target_pairs={{0,4},{2,6},{4,0},{6,2},{8,12},{10,14},{12,8},{14,10},{1,5},{3,7},... | collective-permute-start | bytes 1572872 | tf_op jit(solution)/shard_map/ppermute | solution.py:290
  64.5 20.7 %collective-permute-start.11 = (bf16[256,1024]{1,0:T(8,128)(2,1)S(1)}, bf16[256,1024]{1,0:T(8,128)(2,1)S(1)}, u32[]{:S(2)}, u32[]{:S(2)}) collective-permute-start(bf16[256,1024]{1,0:T(8,128)(2,1)S(1)} %get-tuple-element.65), channel_id=1, source_target_pairs={{0,2},{2,0},{4,6},{6,4},{8,10},{10,8},{12,14},{14,12},{1,3},{3,1},... | collective-permute-start | bytes 1572872 | tf_op jit(solution)/shard_map/ppermute | solution.py:287
  66.6 33.0 %collective-permute-start.10 = (bf16[256,1024]{1,0:T(8,128)(2,1)S(1)}, bf16[256,1024]{1,0:T(8,128)(2,1)S(1)}, u32[]{:S(2)}, u32[]{:S(2)}) collective-permute-start(bf16[256,1024]{1,0:T(8,128)(2,1)S(1)} %get-tuple-element.62), channel_id=1, source_target_pairs={{0,4},{2,6},{4,0},{6,2},{8,12},{10,14},{12,8},{14,10},{1,5},{3,7},... | collective-permute-start | bytes 1572872 | tf_op jit(solution)/shard_map/ppermute | solution.py:290
  76.7 32.5 %collective-permute-start.18 = (bf16[256,1024]{1,0:T(8,128)(2,1)S(1)}, bf16[256,1024]{1,0:T(8,128)(2,1)S(1)}, u32[]{:S(2)}, u32[]{:S(2)}) collective-permute-start(bf16[256,1024]{1,0:T(8,128)(2,1)S(1)} %get-tuple-element.83), channel_id=1, source_target_pairs={{0,2},{2,0},{4,6},{6,4},{8,10},{10,8},{12,14},{14,12},{1,3},{3,1},... | collective-permute-start | bytes 1572872 | tf_op jit(solution)/shard_map/ppermute | solution.py:287
  78.1 31.0 %collective-permute-start.14 = (bf16[256,1024]{1,0:T(8,128)(2,1)S(1)}, bf16[256,1024]{1,0:T(8,128)(2,1)S(1)}, u32[]{:S(2)}, u32[]{:S(2)}) collective-permute-start(bf16[256,1024]{1,0:T(8,128)(2,1)S(1)} %add_convert_fusion.4), channel_id=1, source_target_pairs={{0,8},{2,10},{4,12},{6,14},{8,0},{10,2},{12,4},{14,6},{1,9},{3,11}... | collective-permute-start | bytes 1572872 | tf_op jit(solution)/shard_map/ppermute | solution.py:296
  85.2 21.8 %collective-permute-start.15 = (bf16[256,1024]{1,0:T(8,128)(2,1)S(1)}, bf16[256,1024]{1,0:T(8,128)(2,1)S(1)}, u32[]{:S(2)}, u32[]{:S(2)}) collective-permute-start(bf16[256,1024]{1,0:T(8,128)(2,1)S(1)} %get-tuple-element.73), channel_id=1, source_target_pairs={{0,2},{2,0},{4,6},{6,4},{8,10},{10,8},{12,14},{14,12},{1,3},{3,1},... | collective-permute-start | bytes 1572872 | tf_op jit(solution)/shard_map/ppermute | solution.py:287
  87.4 21.9 %collective-permute-start.19 = (bf16[256,1024]{1,0:T(8,128)(2,1)S(1)}, bf16[256,1024]{1,0:T(8,128)(2,1)S(1)}, u32[]{:S(2)}, u32[]{:S(2)}) collective-permute-start(bf16[256,1024]{1,0:T(8,128)(2,1)S(1)} %add_convert_fusion.3), channel_id=1, source_target_pairs={{0,4},{2,6},{4,0},{6,2},{8,12},{10,14},{12,8},{14,10},{1,5},{3,7},... | collective-permute-start | bytes 1572872 | tf_op jit(solution)/shard_map/ppermute | solution.py:290
  107.2 14.9 %collective-permute-start.17 = (bf16[256,1024]{1,0:T(8,128)(2,1)S(1)}, bf16[256,1024]{1,0:T(8,128)(2,1)S(1)}, u32[]{:S(2)}, u32[]{:S(2)}) collective-permute-start(bf16[256,1024]{1,0:T(8,128)(2,1)S(1)} %add_convert_fusion.1), channel_id=1, source_target_pairs={{0,2},{2,0},{4,6},{6,4},{8,10},{10,8},{12,14},{14,12},{1,3},{3,1},... | collective-permute-start | bytes 1572872 | tf_op jit(solution)/shard_map/ppermute | solution.py:287
  109.6 26.0 %collective-permute-start.20 = (bf16[256,1024]{1,0:T(8,128)(2,1)S(1)}, bf16[256,1024]{1,0:T(8,128)(2,1)S(1)}, u32[]{:S(2)}, u32[]{:S(2)}) collective-permute-start(bf16[256,1024]{1,0:T(8,128)(2,1)S(1)} %add_convert_fusion), channel_id=1, source_target_pairs={{0,8},{2,10},{4,12},{6,14},{8,0},{10,2},{12,4},{14,6},{1,9},{3,11}... | collective-permute-start | bytes 1572872 | tf_op jit(solution)/shard_map/ppermute | solution.py:296
  113.9 21.9 %collective-permute-start.21 = (bf16[256,1024]{1,0:T(8,128)(2,1)S(1)}, bf16[256,1024]{1,0:T(8,128)(2,1)S(1)}, u32[]{:S(2)}, u32[]{:S(2)}) collective-permute-start(bf16[256,1024]{1,0:T(8,128)(2,1)S(1)} %add_convert_fusion.2), channel_id=1, source_target_pairs={{0,4},{2,6},{4,0},{6,2},{8,12},{10,14},{12,8},{14,10},{1,5},{3,7},... | collective-permute-start | bytes 1572872 | tf_op jit(solution)/shard_map/ppermute | solution.py:290
  115.6 20.2 %collective-permute-start.22 = (bf16[256,1024]{1,0:T(8,128)(2,1)S(1)}, bf16[256,1024]{1,0:T(8,128)(2,1)S(1)}, u32[]{:S(2)}, u32[]{:S(2)}) collective-permute-start(bf16[256,1024]{1,0:T(8,128)(2,1)S(1)} %get-tuple-element.88), channel_id=1, source_target_pairs={{0,2},{2,0},{4,6},{6,4},{8,10},{10,8},{12,14},{14,12},{1,3},{3,1},... | collective-permute-start | bytes 1572872 | tf_op jit(solution)/shard_map/ppermute | solution.py:287
  (5 other events, 53.0 us)

commit v8 on v7

--- a/solution.py
+++ b/solution.py
@@ -106,24 +106,27 @@
 
 def rim_rows(part, basis, halos, ops, tables, ids, lefts, index, size, begun):
     rows, width = basis.shape
-    block = halos[0].shape[0]
+    block = ops.shape[1]
     rim = REACH * block
     blocks = rows // block
-    steps = 2
+    steps = 1
     tile = width // 2 // steps
 
-    def kernel(nb_ref, mask_ref, sec_ref, col_ref, row_ref, index_ref, up_ref, down_ref, split_ref, swapped_ref,
-               head_ref, tail0_ref, tail1_ref, ops_ref, *refs):
+    def kernel(nb_ref, mask_ref, sec_ref, col_ref, row_ref, index_ref, up_ref, down_ref, far_ref, mid_ref,
+               far_swapped_ref, mid_swapped_ref, head_ref, tail0_ref, tail1_ref, ops_ref, *refs):
         left_refs, (begun_ref, out_ref, *unit_refs, ext) = refs[:8], refs[8:]
         mine, lower = sec_ref[0] == col_ref[0], sec_ref[0] == 0
-        split, swapped = split_ref[...], swapped_ref[...]
-        ext[:block, :] = jnp.where(lower, swapped, split)
-        ext[block:rim, :] = up_ref[...]
+        piece, direct = far_ref.shape[0], up_ref.shape[0]
+        for i, (here, there) in enumerate(((far_ref, far_swapped_ref), (mid_ref, mid_swapped_ref))):
+            here, there = here[...], there[...]
+            ext[i * piece : (i + 1) * piece, :] = jnp.where(lower, there, here)
+            end = 6 * rim - i * piece
+            ext[end - piece : end, :] = jnp.where(lower, here, there)
+        ext[2 * piece : rim, :] = up_ref[...]
         ext[rim : 3 * rim, :] = head_ref[...]
         ext[3 * rim : 4 * rim, :] = tail0_ref[...]
         ext[4 * rim : 5 * rim, :] = tail1_ref[...]
-        ext[5 * rim : 5 * rim + block, :] = down_ref[...]
-        ext[5 * rim + block :, :] = jnp.where(lower, split, swapped)
+        ext[5 * rim : 5 * rim + direct, :] = down_ref[...]
         for i, b in enumerate((0, 1, blocks - 2, blocks - 1)):
             shift = REACH if b < REACH else 5 * REACH - blocks
             out_ref[i * block : (i + 1) * block, :] = jnp.dot(
@@ -153,7 +156,7 @@
 
     return call(
         kernel, (*tables, *ids, index), (steps,),
-        [across(block)] * 4 + [across(2 * rim), across(rim, last - 1), across(rim, last), fixed(ops)]
+        [across(x.shape[0]) for x in halos] + [across(2 * rim), across(rim, last - 1), across(rim, last), fixed(ops)]
         + unit + [pl.BlockSpec((1, 2, size, tile), lambda j, *_: (part, 0, 0, j))],
         (*halos, basis, basis, basis, ops, *(lefts * 4), begun),
         [out(2 * rim), out(size), out(size)],
@@ -226,9 +229,15 @@
     def after(value, *earlier):
         return lax.optimization_barrier((value, earlier))[0]
 
-    split = lax.dynamic_slice_in_dim(basis, block + sec * (rows - 3 * block), block, 0)
+    direct = rim * 4 // 8
+    piece = (rim - direct) // 2
+    split = [
+        lax.dynamic_slice_in_dim(basis, near + sec * (rows - rim + i * piece - near), piece, 0)
+        for i, near in enumerate((direct + piece, direct))
+    ]
     behind = after(basis, split)
-    split = lax.ppermute(split, ("sec", "row"), down + [(count + i, count + j) for i, j in up])
+    inward = down + [(count + i, count + j) for i, j in up]
+    split = [lax.ppermute(x, ("sec", "row"), inward) for x in split]
     part = blocks // 2
     cuts = (0, part // 2, part)
     share = [
@@ -236,19 +245,19 @@
     ]
     behind = after(behind, share)
     share = [lax.ppermute(x, "sec", swap) for x in share]
-    from_before = lax.ppermute(behind[rows - block :], "row", up)
-    from_after = lax.ppermute(behind[:block], "row", down)
+    from_before = lax.ppermute(behind[rows - direct :], "row", up)
+    from_after = lax.ppermute(behind[:direct], "row", down)
     moved = lax.ppermute(behind, "col", swap)
     rest = [lax.ppermute(x, "col", swap) for x in share]
-    swapped = lax.ppermute(split, "sec", swap)
+    swapped = [lax.ppermute(after(x, moved), "sec", swap) for x in split]
 
     height = width * lax.axis_size("col") // lax.axis_size("sec") // count
     fars = count // 4
     far, pair, side = row // 4, row // 2 % 2, row % 2
     away = list(range(1, fars))
     plan = [
-        (away, 1 - pair, 1 - side), ([0], 1 - pair, 1 - side), (away, pair, 1 - side), ([0], 1 - pair, side),
-        (away, 1 - pair, side), ([0], pair, 1 - side), (away, pair, side), ([0], pair, side),
+        (away, 1 - pair, 1 - side), ([0], 1 - pair, 1 - side), (away, pair, 1 - side), (away, 1 - pair, side),
+        ([0], 1 - pair, side), ([0], pair, 1 - side), (away, pair, side), ([0], pair, side),
     ]
     where = [[((far + step) % fars * 2 + p) * 2 + s for step in steps] for steps, p, s in plan]
     lefts = (basis, moved)
@@ -271,7 +280,7 @@
     ids = tuple(x.astype(jnp.int32)[None] for x in (sec, col, row))
     tables = (neighbours, mask)
     inner, begun, ops = inner_rows(basis, own_ops, share, rest, tables, ids, lefts, index, size)
-    halos = (from_before, from_after, split, swapped)
+    halos = (from_before, from_after, *split, *swapped)
     swap_side = [(i, i ^ 1) for i in range(count)]
     swap_pair = [(i, i ^ 2) for i in range(count)]
 
@@ -306,24 +315,28 @@
 
     rim0, far_a0, near_a0 = rim_half(0, halos)
     far_a0, near_a0 = to_side(far_a0), to_pair(near_a0)
-    far_b0, near_b0, far_c0 = unit_half(0, (2, 3, 4), rim0, BF16, BF16, F32)
+    far_b0, far_c0 = unit_half(0, (2, 3), rim0, BF16, F32)
     rim1, far_a1, near_a1 = rim_half(1, (after(halos[0], far_c0), *halos[1:]))
     far_b0 = to_side(far_b0)
     far_c0 = add(far_c0, after(far_a0, rim1))
-    near_c0, far_d0, own0 = unit_half(0, (5, 6, 7), after(rim0, far_c0), F32, F32, F32)
+    near_b0, near_c0, far_d0, own0 = unit_half(
+        0, (4, 5, 6, 7), after(rim0, far_c0), BF16, F32, F32, F32
+    )
     far_c0_sum = far_c0
     far_c0 = to_pair(far_c0)
     far_a1 = to_side(far_a1)
-    far_b1, near_b1, far_c1 = unit_half(1, (2, 3, 4), after(rim1, own0), BF16, F32, F32)
+    far_b1, far_c1 = unit_half(1, (2, 3), after(rim1, own0), BF16, F32)
     near_c0 = add(near_c0, after(near_a0, far_c1))
     far_b1 = to_side(far_b1)
     far_d0 = add(far_d0, after(far_b0, far_c1), far_c0)
-    near_b0 = to_pair(after(near_b0, far_c0_sum))
+    near_b0 = to_pair(near_b0)
     near_a1 = to_side(after(near_a1, far_d0))
     far_c1 = add(far_c1, after(far_a1, far_d0))
     own0 = add32(own0, after(near_b0, far_c1))
     far_d0 = to_far(far_d0)
-    near_c1, far_d1, own1 = unit_half(1, (5, 6, 7), after(rim1, own0), BF16, F32, F32)
+    near_b1, near_c1, far_d1, own1 = unit_half(
+        1, (4, 5, 6, 7), after(rim1, own0), F32, BF16, F32, F32
+    )
     far_c1 = to_pair(far_c1)
     near_b1 = add(near_b1, after(near_a1, far_d1))
     near_c0, near_c1 = after((near_c0, near_c1), near_b1)

time: 138 us -> 135 us (0.978)
  Pallas kernels: 38.8 us -> 31.5 us
  local copies, waits for them, and re-layouts: 9.83 us -> 14.6 us
  starting transfers between devices: 39.7 us -> 44.4 us
  waiting for transfers between devices: 47 us -> 42.6 us
    ppermute x4 -> x6, starting transfers between devices: 11.2 us -> 19.1 us  [the longest x2 9.72 us: per_device(): swapped = [lax.ppermute(after(x, moved), 'sec', swap) for x in split]]
    ppermute x5, waiting for transfers between devices: 11.5 us -> 18.8 us  [to_pair(): return lax.ppermute(x, 'row', swap_pair)]
    pallas_call x8, Pallas kernels: 38.8 us -> 31.5 us  [call(): pl.pallas_call(kernel, grid_spec=pltpu.PrefetchScalarGridSpec(num_scalar_...]
    ppermute x2, waiting for transfers between devices: 13.3 us -> 8.01 us  [to_far(): parts.append(lax.ppermute(x[i * height:(i + 1) * height], 'row', route))]
    unnamed x14 -> x18, local copies, waits for them, and re-layouts: 4.32 us -> 9.11 us
    ppermute x4 -> x6, waiting for transfers between devices: 5.94 us -> 1.21 us  [the longest x2 1.2 us: per_device(): split = [lax.ppermute(x, ('sec', 'row'), inward) for x in split]]
    ppermute x2, starting transfers between devices: 8.34 us -> 4.32 us  [to_far(): parts.append(lax.ppermute(x[i * height:(i + 1) * height], 'row', route))]
    ppermute x2, waiting for transfers between devices: 1.71 us -> 0.01 us  [per_device(): rest = [lax.ppermute(x, 'col', swap) for x in share]]
  transfers between devices with their start and end apart: 23 -> 25, of which waited for: 13 -> 8; matrix products, arithmetic and copies ran while one was open for 3% -> 3% of each run, Pallas kernels for 24% -> 20%
where the time goes in v8:
time: 135 us
  starting transfers between devices  44.4 us (33%)
  waiting for transfers between devices  42.6 us (32%)
  Pallas kernels  31.5 us (23%)
  local copies, waits for them, and re-layouts  14.6 us (11%)
  other arithmetic  1.76 us (1%)
    pallas_call x8, Pallas kernels, call(): pl.pallas_call(kernel, grid_spec=pltpu.PrefetchScalarGridSpec(num_scalar_...  31.5 us
    ppermute x5, waiting for transfers between devices, to_pair(): return lax.ppermute(x, 'row', swap_pair)  18.8 us
    ppermute x7, waiting for transfers between devices, to_side(): return lax.ppermute(x, 'row', swap_side)  12.9 us
    ppermute x2, starting transfers between devices, per_device(): swapped = [lax.ppermute(after(x, moved), 'sec', swap) for x in split]  9.72 us
    unnamed x18, local copies, waits for them, and re-layouts  9.11 us
    ppermute x7, starting transfers between devices, to_side(): return lax.ppermute(x, 'row', swap_side)  8.7 us
    ppermute x5, starting transfers between devices, to_pair(): return lax.ppermute(x, 'row', swap_pair)  8.56 us
    ppermute x2, waiting for transfers between devices, to_far(): parts.append(lax.ppermute(x[i * height:(i + 1) * height], 'row', route))  8.01 us
  transfers between devices with their start and end apart: 25, of which 8 were waited for; matrix products, arithmetic and copies ran while one was open for 3% of the time, Pallas kernels for 20%

profile of v8, /device:TPU:0, one launch (start us, length us, event | category | flops | bytes accessed | tf_op | source)
XLA Modules:
  0.0 135.1 jit_solution(14784375830449753877)
XLA Ops:
  3.7 2.6 %collective-permute-start.1 = (bf16[2,7,64,128]{3,2,1,0:T(8,128)(2,1)S(1)}, bf16[2,7,64,128]{3,2,1,0:T(8,128)(2,1)S(1)}, u32[]{:S(2)}, u32[]{:S(2)}) collective-permute-start(bf16[2,7,64,128]{3,2,1,0:T(8,128)(2,1)S(1)} %constant_dynamic-slice_fusion.1), channel_id=1, source_target_pairs={{0,16},{16,0},{1,17},{17,1},{2,18},{18,2},{3,19},{19,3},{4,20},{20... | collective-permute-start | bytes 688136 | tf_op jit(solution)/shard_map/ppermute | solution.py:247
  6.4 4.9 %collective-permute-start.8 = (bf16[64,2048]{1,0:T(8,128)(2,1)S(1)}, bf16[64,2048]{1,0:T(8,128)(2,1)S(1)}, u32[]{:S(2)}, u32[]{:S(2)}) collective-permute-start(bf16[64,2048]{1,0:T(8,128)(2,1)S(1)} %get-tuple-element.95), channel_id=1, source_target_pairs={{2,0},{4,2},{6,4},{8,6},{10,8},{12,10},{14,12},{0,14},{16,18},{18,... | collective-permute-start | bytes 786440 | tf_op jit(solution)/shard_map/ppermute | solution.py:240
  11.8 2.3 %fusion = (bf16[128,2048]{1,0:T(8,128)(2,1)}, bf16[128,2048]{1,0:T(8,128)(2,1)}) fusion(bf16[1280,2048]{1,0:T(8,128)(2,1)} %here.7), kind=kLoop, calls=%fused_computation.14 | loop fusion | bytes 2097152 | tf_op jit(solution)/shard_map/slice | solution.py:249
  14.1 3.6 %collective-permute-start.6 = (bf16[128,2048]{1,0:T(8,128)(2,1)}, bf16[128,2048]{1,0:T(8,128)(2,1)S(1)}, u32[]{:S(2)}, u32[]{:S(2)}) collective-permute-start(bf16[128,2048]{1,0:T(8,128)(2,1)} %get-tuple-element.93), channel_id=1, source_target_pairs={{2,0},{4,2},{6,4},{8,6},{10,8},{12,10},{14,12},{0,14},{3,1},{5,3},... | collective-permute-start | bytes 1572872 | tf_op jit(solution)/shard_map/ppermute | solution.py:249
  20.0 2.3 %copy-done.1 = bf16[1280,2048]{1,0:T(8,128)(2,1)} copy-done((bf16[1280,2048]{1,0:T(8,128)(2,1)}, bf16[1280,2048]{1,0:T(8,128)(2,1)S(1)}, u32[]{:S(2)}) %copy-start.1) | copy-done | bytes 5242904
  23.6 9.7 %collective-permute-start.9 = (bf16[64,2048]{1,0:T(8,128)(2,1)S(1)}, bf16[64,2048]{1,0:T(8,128)(2,1)S(1)}, u32[]{:S(2)}, u32[]{:S(2)}) collective-permute-start(bf16[64,2048]{1,0:T(8,128)(2,1)S(1)} %collective-permute-done.7.far_ref), channel_id=1, source_target_pairs={{0,16},{16,0},{1,17},{17,1},{2,18},{18,2},{3,19},{19,3},{4,20},{20... | collective-permute-start | bytes 786440 | tf_op jit(solution)/shard_map/ppermute | solution.py:252
  34.4 2.5 %copy-done = bf16[1280,2048]{1,0:T(8,128)(2,1)S(1)} copy-done((bf16[1280,2048]{1,0:T(8,128)(2,1)S(1)}, bf16[1280,2048]{1,0:T(8,128)(2,1)}, u32[]{:S(2)}) %copy-start) | copy-done | bytes 5242904
  36.9 2.5 %copy-done.2 = bf16[1280,2048]{1,0:T(8,128)(2,1)S(1)} copy-done((bf16[1280,2048]{1,0:T(8,128)(2,1)S(1)}, bf16[1280,2048]{1,0:T(8,128)(2,1)}, u32[]{:S(2)}) %copy-start.2) | copy-done | bytes 5242904
  40.3 8.0 %inner_rows.1 = (bf16[2,768,1024]{2,1,0:T(8,128)(2,1)S(1)}, f32[2,2,256,1024]{3,2,1,0:T(8,128)S(1)}, bf16[4,128,896]{2,1,0:T(8,128)(2,1)S(1)}) custom-call(s32[10,7]{1,0:T(8,128)S(1)} %copy.5.nb_ref, s32[10,7]{1,0:T(8,128)S(1)} %copy.6.mask_ref, s32[1]{0:T(128)} %bitcast.sec_ref, s32[1]{0:T(128)} %bitcast.1.col_ref, s32[1]{0:T(128)} %bitcast.2.row_ref, ...), custom_call_target="tpu_custom_call" | custom-call | flops 1 | bytes 1 | tf_op jit(solution)/shard_map/inner_rows/pallas_call | solution.py:16
  48.3 3.0 %rim_rows.2 = (bf16[512,1024]{1,0:T(8,128)(2,1)S(1)}, bf16[256,1024]{1,0:T(8,128)(2,1)S(1)}, bf16[256,1024]{1,0:T(8,128)(2,1)S(1)}) custom-call(s32[10,7]{1,0:T(8,128)S(1)} %copy.5.nb_ref, s32[10,7]{1,0:T(8,128)S(1)} %copy.6.mask_ref, s32[1]{0:T(128)} %bitcast.sec_ref, s32[1]{0:T(128)} %bitcast.1.col_ref, s32[1]{0:T(128)} %bitcast.2.row_ref, ...), custom_call_target="tpu_custom_call" | custom-call | flops 1 | bytes 1 | tf_op jit(solution)/shard_map/rim_rows/pallas_call | solution.py:16
  51.3 2.5 %collective-permute-start.11 = (bf16[256,1024]{1,0:T(8,128)(2,1)S(1)}, bf16[256,1024]{1,0:T(8,128)(2,1)S(1)}, u32[]{:S(2)}, u32[]{:S(2)}) collective-permute-start(bf16[256,1024]{1,0:T(8,128)(2,1)S(1)} %get-tuple-element.58), channel_id=1, source_target_pairs={{0,2},{2,0},{4,6},{6,4},{8,10},{10,8},{12,14},{14,12},{1,3},{3,1},... | collective-permute-start | bytes 1572872 | tf_op jit(solution)/shard_map/ppermute | solution.py:296
  55.3 2.8 %units.4 = (bf16[256,1024]{1,0:T(8,128)(2,1)S(1)}, f32[256,1024]{1,0:T(8,128)S(1)}) custom-call(s32[1]{0:T(128)} %bitcast.sec_ref, s32[1]{0:T(128)} %bitcast.1.col_ref, s32[1]{0:T(128)} %bitcast.2.row_ref, s32[8]{0:T(128)S(1)} %stack.35.index_ref, bf16[1280,2048]{1,0:T(8,128)(2,1)S(1)} %copy-done, bf16[1280,2048]{1,0:T(8,128)(2,1)S(1)} %copy-done.2, ...), custom_call_target="tpu_custom_call" | custom-call | flops 1 | bytes 1 | tf_op jit(solution)/shard_map/units/pallas_call | solution.py:16
  59.3 2.9 %rim_rows.3 = (bf16[512,1024]{1,0:T(8,128)(2,1)S(1)}, bf16[256,1024]{1,0:T(8,128)(2,1)S(1)}, bf16[256,1024]{1,0:T(8,128)(2,1)S(1)}) custom-call(s32[10,7]{1,0:T(8,128)S(1)} %copy.5.nb_ref, s32[10,7]{1,0:T(8,128)S(1)} %copy.6.mask_ref, s32[1]{0:T(128)} %bitcast.sec_ref, s32[1]{0:T(128)} %bitcast.1.col_ref, s32[1]{0:T(128)} %bitcast.2.row_ref, ...), custom_call_target="tpu_custom_call" | custom-call | flops 1 | bytes 1 | tf_op jit(solution)/shard_map/rim_rows/pallas_call | solution.py:16
  62.3 4.4 %collective-permute-done.11 = bf16[256,1024]{1,0:T(8,128)(2,1)S(1)} collective-permute-done((bf16[256,1024]{1,0:T(8,128)(2,1)S(1)}, bf16[256,1024]{1,0:T(8,128)(2,1)S(1)}, u32[]{:S(2)}, u32[]{:S(2)}) %collective-permute-start.11) | collective-permute-done | bytes 524320 | tf_op jit(solution)/shard_map/ppermute | solution.py:296
  66.8 2.6 %collective-permute-start.15 = (bf16[256,1024]{1,0:T(8,128)(2,1)S(1)}, bf16[256,1024]{1,0:T(8,128)(2,1)S(1)}, u32[]{:S(2)}, u32[]{:S(2)}) collective-permute-start(bf16[256,1024]{1,0:T(8,128)(2,1)S(1)} %add_convert_fusion.5), channel_id=1, source_target_pairs={{0,4},{2,6},{4,0},{6,2},{8,12},{10,14},{12,8},{14,10},{1,5},{3,7},... | collective-permute-start | bytes 1572872 | tf_op jit(solution)/shard_map/ppermute | solution.py:299
  70.4 5.2 %units.5 = (bf16[256,1024]{1,0:T(8,128)(2,1)S(1)}, f32[256,1024]{1,0:T(8,128)S(1)}, f32[256,1024]{1,0:T(8,128)S(1)}, f32[256,1024]{1,0:T(8,128)S(1)}) custom-call(s32[1]{0:T(128)} %bitcast.sec_ref, s32[1]{0:T(128)} %bitcast.1.col_ref, s32[1]{0:T(128)} %bitcast.2.row_ref, s32[8]{0:T(128)S(1)} %stack.35.index_ref, bf16[1280,2048]{1,0:T(8,128)(2,1)S(1)} %copy-done, ...), custom_call_target="tpu_custom_call" | custom-call | flops 1 | bytes 1 | tf_op jit(solution)/shard_map/units/pallas_call | solution.py:16
  76.1 2.8 %units.6 = (bf16[256,1024]{1,0:T(8,128)(2,1)S(1)}, f32[256,1024]{1,0:T(8,128)S(1)}) custom-call(s32[1]{0:T(128)} %bitcast.sec_ref, s32[1]{0:T(128)} %bitcast.1.col_ref, s32[1]{0:T(128)} %bitcast.2.row_ref, s32[8]{0:T(128)S(1)} %stack.35.index_ref, bf16[1280,2048]{1,0:T(8,128)(2,1)S(1)} %copy-done, bf16[1280,2048]{1,0:T(8,128)(2,1)S(1)} %copy-done.2, ...), custom_call_target="tpu_custom_call" | custom-call | flops 1 | bytes 1 | tf_op jit(solution)/shard_map/units/pallas_call | solution.py:16
  80.0 7.7 %collective-permute-done.15 = bf16[256,1024]{1,0:T(8,128)(2,1)S(1)} collective-permute-done((bf16[256,1024]{1,0:T(8,128)(2,1)S(1)}, bf16[256,1024]{1,0:T(8,128)(2,1)S(1)}, u32[]{:S(2)}, u32[]{:S(2)}) %collective-permute-start.15) | collective-permute-done | bytes 524320 | tf_op jit(solution)/shard_map/ppermute | solution.py:299
  91.3 2.3 %collective-permute-start.21 = (bf16[256,1024]{1,0:T(8,128)(2,1)S(1)}, bf16[256,1024]{1,0:T(8,128)(2,1)S(1)}, u32[]{:S(2)}, u32[]{:S(2)}) collective-permute-start(bf16[256,1024]{1,0:T(8,128)(2,1)S(1)} %add_convert_fusion.3), channel_id=1, source_target_pairs={{0,4},{2,6},{4,0},{6,2},{8,12},{10,14},{12,8},{14,10},{1,5},{3,7},... | collective-permute-start | bytes 1572872 | tf_op jit(solution)/shard_map/ppermute | solution.py:299
  93.6 11.1 %collective-permute-done.12 = bf16[256,1024]{1,0:T(8,128)(2,1)S(1)} collective-permute-done((bf16[256,1024]{1,0:T(8,128)(2,1)S(1)}, bf16[256,1024]{1,0:T(8,128)(2,1)S(1)}, u32[]{:S(2)}, u32[]{:S(2)}) %collective-permute-start.12) | collective-permute-done | bytes 524320 | tf_op jit(solution)/shard_map/ppermute | solution.py:299
  104.8 5.3 %units.7 = (f32[256,1024]{1,0:T(8,128)S(1)}, bf16[256,1024]{1,0:T(8,128)(2,1)S(1)}, f32[256,1024]{1,0:T(8,128)S(1)}, f32[256,1024]{1,0:T(8,128)S(1)}) custom-call(s32[1]{0:T(128)} %bitcast.sec_ref, s32[1]{0:T(128)} %bitcast.1.col_ref, s32[1]{0:T(128)} %bitcast.2.row_ref, s32[8]{0:T(128)S(1)} %stack.35.index_ref, bf16[1280,2048]{1,0:T(8,128)(2,1)S(1)} %copy-done, ...), custom_call_target="tpu_custom_call" | custom-call | flops 1 | bytes 1 | tf_op jit(solution)/shard_map/units/pallas_call | solution.py:16
  111.4 2.5 %collective-permute-start.22 = (bf16[256,1024]{1,0:T(8,128)(2,1)S(1)}, bf16[256,1024]{1,0:T(8,128)(2,1)S(1)}, u32[]{:S(2)}, u32[]{:S(2)}) collective-permute-start(bf16[256,1024]{1,0:T(8,128)(2,1)S(1)} %add_convert_fusion), channel_id=1, source_target_pairs={{0,8},{2,10},{4,12},{6,14},{8,0},{10,2},{12,4},{14,6},{1,9},{3,11}... | collective-permute-start | bytes 1572872 | tf_op jit(solution)/shard_map/ppermute | solution.py:305
  116.7 8.5 %collective-permute-done.19 = bf16[256,1024]{1,0:T(8,128)(2,1)S(1)} collective-permute-done((bf16[256,1024]{1,0:T(8,128)(2,1)S(1)}, bf16[256,1024]{1,0:T(8,128)(2,1)S(1)}, u32[]{:S(2)}, u32[]{:S(2)}) %collective-permute-start.19) | collective-permute-done | bytes 524320 | tf_op jit(solution)/shard_map/ppermute | solution.py:296
  125.4 8.0 %collective-permute-done.22 = bf16[256,1024]{1,0:T(8,128)(2,1)S(1)} collective-permute-done((bf16[256,1024]{1,0:T(8,128)(2,1)S(1)}, bf16[256,1024]{1,0:T(8,128)(2,1)S(1)}, u32[]{:S(2)}, u32[]{:S(2)}) %collective-permute-start.22) | collective-permute-done | bytes 524320 | tf_op jit(solution)/shard_map/ppermute | solution.py:305
  (67 shorter events, 24.7 us)
Async XLA Ops:
  3.1 16.8 %collective-permute-start = (bf16[1280,2048]{1,0:T(8,128)(2,1)}, bf16[1280,2048]{1,0:T(8,128)(2,1)S(1)}, u32[]{:S(2)}, u32[]{:S(2)}) collective-permute-start(bf16[1280,2048]{1,0:T(8,128)(2,1)} %here.7), channel_id=1, source_target_pairs={{0,1},{1,0},{2,3},{3,2},{4,5},{5,4},{6,7},{7,6},{8,9},{9,8},{10,11... | collective-permute-start | bytes 15728648 | tf_op jit(solution)/shard_map/ppermute | solution.py:250
  6.3 13.7 %collective-permute-start.2 = (bf16[3,7,64,128]{3,2,1,0:T(8,128)(2,1)S(1)}, bf16[3,7,64,128]{3,2,1,0:T(8,128)(2,1)}, u32[]{:S(2)}, u32[]{:S(2)}) collective-permute-start(bf16[3,7,64,128]{3,2,1,0:T(8,128)(2,1)S(1)} %constant_dynamic-slice_fusion), channel_id=1, source_target_pairs={{0,16},{16,0},{1,17},{17,1},{2,18},{18,2},{3,19},{19,3},{4,20},{20... | collective-permute-start | bytes 1032200 | tf_op jit(solution)/shard_map/ppermute | solution.py:247
  6.4 11.7 %collective-permute-start.8 = (bf16[64,2048]{1,0:T(8,128)(2,1)S(1)}, bf16[64,2048]{1,0:T(8,128)(2,1)S(1)}, u32[]{:S(2)}, u32[]{:S(2)}) collective-permute-start(bf16[64,2048]{1,0:T(8,128)(2,1)S(1)} %get-tuple-element.95), channel_id=1, source_target_pairs={{2,0},{4,2},{6,4},{8,6},{10,8},{12,10},{14,12},{0,14},{16,18},{18,... | collective-permute-start | bytes 786440 | tf_op jit(solution)/shard_map/ppermute | solution.py:240
  11.3 12.3 %collective-permute-start.7 = (bf16[64,2048]{1,0:T(8,128)(2,1)S(1)}, bf16[64,2048]{1,0:T(8,128)(2,1)S(1)}, u32[]{:S(2)}, u32[]{:S(2)}) collective-permute-start(bf16[64,2048]{1,0:T(8,128)(2,1)S(1)} %get-tuple-element.96), channel_id=1, source_target_pairs={{2,0},{4,2},{6,4},{8,6},{10,8},{12,10},{14,12},{0,14},{16,18},{18,... | collective-permute-start | bytes 786440 | tf_op jit(solution)/shard_map/ppermute | solution.py:240
  14.1 34.2 %collective-permute-start.6 = (bf16[128,2048]{1,0:T(8,128)(2,1)}, bf16[128,2048]{1,0:T(8,128)(2,1)S(1)}, u32[]{:S(2)}, u32[]{:S(2)}) collective-permute-start(bf16[128,2048]{1,0:T(8,128)(2,1)} %get-tuple-element.93), channel_id=1, source_target_pairs={{2,0},{4,2},{6,4},{8,6},{10,8},{12,10},{14,12},{0,14},{3,1},{5,3},... | collective-permute-start | bytes 1572872 | tf_op jit(solution)/shard_map/ppermute | solution.py:249
  18.0 30.3 %collective-permute-start.5 = (bf16[128,2048]{1,0:T(8,128)(2,1)}, bf16[128,2048]{1,0:T(8,128)(2,1)S(1)}, u32[]{:S(2)}, u32[]{:S(2)}) collective-permute-start(bf16[128,2048]{1,0:T(8,128)(2,1)} %get-tuple-element.94), channel_id=1, source_target_pairs={{0,2},{2,4},{4,6},{6,8},{8,10},{10,12},{12,14},{14,0},{1,3},{3,5},... | collective-permute-start | bytes 1572872 | tf_op jit(solution)/shard_map/ppermute | solution.py:248
  19.9 13.4 %collective-permute-start.3 = (bf16[2,7,64,128]{3,2,1,0:T(8,128)(2,1)S(1)}, bf16[2,7,64,128]{3,2,1,0:T(8,128)(2,1)S(1)}, u32[]{:S(2)}, u32[]{:S(2)}) collective-permute-start(bf16[2,7,64,128]{3,2,1,0:T(8,128)(2,1)S(1)} %collective-permute-done.1.refs_0_), channel_id=1, source_target_pairs={{0,1},{1,0},{2,3},{3,2},{4,5},{5,4},{6,7},{7,6},{8,9},{9,8},{10,11... | collective-permute-start | bytes 688136 | tf_op jit(solution)/shard_map/ppermute | solution.py:251
  22.3 12.1 %collective-permute-start.4 = (bf16[3,7,64,128]{3,2,1,0:T(8,128)(2,1)}, bf16[3,7,64,128]{3,2,1,0:T(8,128)(2,1)}, u32[]{:S(2)}, u32[]{:S(2)}) collective-permute-start(bf16[3,7,64,128]{3,2,1,0:T(8,128)(2,1)} %collective-permute-done.2.refs_1_), channel_id=1, source_target_pairs={{0,1},{1,0},{2,3},{3,2},{4,5},{5,4},{6,7},{7,6},{8,9},{9,8},{10,11... | collective-permute-start | bytes 1032200 | tf_op jit(solution)/shard_map/ppermute | solution.py:251
  23.6 24.6 %collective-permute-start.9 = (bf16[64,2048]{1,0:T(8,128)(2,1)S(1)}, bf16[64,2048]{1,0:T(8,128)(2,1)S(1)}, u32[]{:S(2)}, u32[]{:S(2)}) collective-permute-start(bf16[64,2048]{1,0:T(8,128)(2,1)S(1)} %collective-permute-done.7.far_ref), channel_id=1, source_target_pairs={{0,16},{16,0},{1,17},{17,1},{2,18},{18,2},{3,19},{19,3},{4,20},{20... | collective-permute-start | bytes 786440 | tf_op jit(solution)/shard_map/ppermute | solution.py:252
  34.1 14.2 %collective-permute-start.10 = (bf16[64,2048]{1,0:T(8,128)(2,1)S(1)}, bf16[64,2048]{1,0:T(8,128)(2,1)S(1)}, u32[]{:S(2)}, u32[]{:S(2)}) collective-permute-start(bf16[64,2048]{1,0:T(8,128)(2,1)S(1)} %collective-permute-done.8.mid_ref), channel_id=1, source_target_pairs={{0,16},{16,0},{1,17},{17,1},{2,18},{18,2},{3,19},{19,3},{4,20},{20... | collective-permute-start | bytes 786440 | tf_op jit(solution)/shard_map/ppermute | solution.py:252
  51.3 15.4 %collective-permute-start.11 = (bf16[256,1024]{1,0:T(8,128)(2,1)S(1)}, bf16[256,1024]{1,0:T(8,128)(2,1)S(1)}, u32[]{:S(2)}, u32[]{:S(2)}) collective-permute-start(bf16[256,1024]{1,0:T(8,128)(2,1)S(1)} %get-tuple-element.58), channel_id=1, source_target_pairs={{0,2},{2,0},{4,6},{6,4},{8,10},{10,8},{12,14},{14,12},{1,3},{3,1},... | collective-permute-start | bytes 1572872 | tf_op jit(solution)/shard_map/ppermute | solution.py:296
  53.8 25.2 %collective-permute-start.18 = (bf16[256,1024]{1,0:T(8,128)(2,1)S(1)}, bf16[256,1024]{1,0:T(8,128)(2,1)S(1)}, u32[]{:S(2)}, u32[]{:S(2)}) collective-permute-start(bf16[256,1024]{1,0:T(8,128)(2,1)S(1)} %get-tuple-element.81), channel_id=1, source_target_pairs={{0,4},{2,6},{4,0},{6,2},{8,12},{10,14},{12,8},{14,10},{1,5},{3,7},... | collective-permute-start | bytes 1572872 | tf_op jit(solution)/shard_map/ppermute | solution.py:299
  58.2 20.8 %collective-permute-start.14 = (bf16[256,1024]{1,0:T(8,128)(2,1)S(1)}, bf16[256,1024]{1,0:T(8,128)(2,1)S(1)}, u32[]{:S(2)}, u32[]{:S(2)}) collective-permute-start(bf16[256,1024]{1,0:T(8,128)(2,1)S(1)} %get-tuple-element.69), channel_id=1, source_target_pairs={{0,2},{2,0},{4,6},{6,4},{8,10},{10,8},{12,14},{14,12},{1,3},{3,1},... | collective-permute-start | bytes 1572872 | tf_op jit(solution)/shard_map/ppermute | solution.py:296
  66.8 21.0 %collective-permute-start.15 = (bf16[256,1024]{1,0:T(8,128)(2,1)S(1)}, bf16[256,1024]{1,0:T(8,128)(2,1)S(1)}, u32[]{:S(2)}, u32[]{:S(2)}) collective-permute-start(bf16[256,1024]{1,0:T(8,128)(2,1)S(1)} %add_convert_fusion.5), channel_id=1, source_target_pairs={{0,4},{2,6},{4,0},{6,2},{8,12},{10,14},{12,8},{14,10},{1,5},{3,7},... | collective-permute-start | bytes 1572872 | tf_op jit(solution)/shard_map/ppermute | solution.py:299
  69.4 20.4 %collective-permute-start.13 = (bf16[256,1024]{1,0:T(8,128)(2,1)S(1)}, bf16[256,1024]{1,0:T(8,128)(2,1)S(1)}, u32[]{:S(2)}, u32[]{:S(2)}) collective-permute-start(bf16[256,1024]{1,0:T(8,128)(2,1)S(1)} %get-tuple-element.67), channel_id=1, source_target_pairs={{0,2},{2,0},{4,6},{6,4},{8,10},{10,8},{12,14},{14,12},{1,3},{3,1},... | collective-permute-start | bytes 1572872 | tf_op jit(solution)/shard_map/ppermute | solution.py:296
  75.6 29.1 %collective-permute-start.12 = (bf16[256,1024]{1,0:T(8,128)(2,1)S(1)}, bf16[256,1024]{1,0:T(8,128)(2,1)S(1)}, u32[]{:S(2)}, u32[]{:S(2)}) collective-permute-start(bf16[256,1024]{1,0:T(8,128)(2,1)S(1)} %get-tuple-element.64), channel_id=1, source_target_pairs={{0,4},{2,6},{4,0},{6,2},{8,12},{10,14},{12,8},{14,10},{1,5},{3,7},... | collective-permute-start | bytes 1572872 | tf_op jit(solution)/shard_map/ppermute | solution.py:299
  79.0 32.1 %collective-permute-start.20 = (bf16[256,1024]{1,0:T(8,128)(2,1)S(1)}, bf16[256,1024]{1,0:T(8,128)(2,1)S(1)}, u32[]{:S(2)}, u32[]{:S(2)}) collective-permute-start(bf16[256,1024]{1,0:T(8,128)(2,1)S(1)} %get-tuple-element.85), channel_id=1, source_target_pairs={{0,2},{2,0},{4,6},{6,4},{8,10},{10,8},{12,14},{14,12},{1,3},{3,1},... | collective-permute-start | bytes 1572872 | tf_op jit(solution)/shard_map/ppermute | solution.py:296
  88.0 22.9 %collective-permute-start.16 = (bf16[256,1024]{1,0:T(8,128)(2,1)S(1)}, bf16[256,1024]{1,0:T(8,128)(2,1)S(1)}, u32[]{:S(2)}, u32[]{:S(2)}) collective-permute-start(bf16[256,1024]{1,0:T(8,128)(2,1)S(1)} %add_convert_fusion.4), channel_id=1, source_target_pairs={{0,8},{2,10},{4,12},{6,14},{8,0},{10,2},{12,4},{14,6},{1,9},{3,11}... | collective-permute-start | bytes 1572872 | tf_op jit(solution)/shard_map/ppermute | solution.py:305
  89.8 20.4 %collective-permute-start.17 = (bf16[256,1024]{1,0:T(8,128)(2,1)S(1)}, bf16[256,1024]{1,0:T(8,128)(2,1)S(1)}, u32[]{:S(2)}, u32[]{:S(2)}) collective-permute-start(bf16[256,1024]{1,0:T(8,128)(2,1)S(1)} %get-tuple-element.76), channel_id=1, source_target_pairs={{0,2},{2,0},{4,6},{6,4},{8,10},{10,8},{12,14},{14,12},{1,3},{3,1},... | collective-permute-start | bytes 1572872 | tf_op jit(solution)/shard_map/ppermute | solution.py:296
  91.3 19.9 %collective-permute-start.21 = (bf16[256,1024]{1,0:T(8,128)(2,1)S(1)}, bf16[256,1024]{1,0:T(8,128)(2,1)S(1)}, u32[]{:S(2)}, u32[]{:S(2)}) collective-permute-start(bf16[256,1024]{1,0:T(8,128)(2,1)S(1)} %add_convert_fusion.3), channel_id=1, source_target_pairs={{0,4},{2,6},{4,0},{6,2},{8,12},{10,14},{12,8},{14,10},{1,5},{3,7},... | collective-permute-start | bytes 1572872 | tf_op jit(solution)/shard_map/ppermute | solution.py:299
  110.3 14.9 %collective-permute-start.19 = (bf16[256,1024]{1,0:T(8,128)(2,1)S(1)}, bf16[256,1024]{1,0:T(8,128)(2,1)S(1)}, u32[]{:S(2)}, u32[]{:S(2)}) collective-permute-start(bf16[256,1024]{1,0:T(8,128)(2,1)S(1)} %add_convert_fusion.1), channel_id=1, source_target_pairs={{0,2},{2,0},{4,6},{6,4},{8,10},{10,8},{12,14},{14,12},{1,3},{3,1},... | collective-permute-start | bytes 1572872 | tf_op jit(solution)/shard_map/ppermute | solution.py:296
  111.4 22.0 %collective-permute-start.22 = (bf16[256,1024]{1,0:T(8,128)(2,1)S(1)}, bf16[256,1024]{1,0:T(8,128)(2,1)S(1)}, u32[]{:S(2)}, u32[]{:S(2)}) collective-permute-start(bf16[256,1024]{1,0:T(8,128)(2,1)S(1)} %add_convert_fusion), channel_id=1, source_target_pairs={{0,8},{2,10},{4,12},{6,14},{8,0},{10,2},{12,4},{14,6},{1,9},{3,11}... | collective-permute-start | bytes 1572872 | tf_op jit(solution)/shard_map/ppermute | solution.py:305
  113.9 19.7 %collective-permute-start.23 = (bf16[256,1024]{1,0:T(8,128)(2,1)S(1)}, bf16[256,1024]{1,0:T(8,128)(2,1)S(1)}, u32[]{:S(2)}, u32[]{:S(2)}) collective-permute-start(bf16[256,1024]{1,0:T(8,128)(2,1)S(1)} %add_convert_fusion.2), channel_id=1, source_target_pairs={{0,4},{2,6},{4,0},{6,2},{8,12},{10,14},{12,8},{14,10},{1,5},{3,7},... | collective-permute-start | bytes 1572872 | tf_op jit(solution)/shard_map/ppermute | solution.py:299
  115.5 18.2 %collective-permute-start.24 = (bf16[256,1024]{1,0:T(8,128)(2,1)S(1)}, bf16[256,1024]{1,0:T(8,128)(2,1)S(1)}, u32[]{:S(2)}, u32[]{:S(2)}) collective-permute-start(bf16[256,1024]{1,0:T(8,128)(2,1)S(1)} %get-tuple-element.90), channel_id=1, source_target_pairs={{0,2},{2,0},{4,6},{6,4},{8,10},{10,8},{12,14},{14,12},{1,3},{3,1},... | collective-permute-start | bytes 1572872 | tf_op jit(solution)/shard_map/ppermute | solution.py:296
  (9 other events, 121.9 us)

commit v9 on v8

--- a/solution.py
+++ b/solution.py
@@ -245,8 +245,9 @@
     ]
     behind = after(behind, share)
     share = [lax.ppermute(x, "sec", swap) for x in share]
-    from_before = lax.ppermute(behind[rows - direct :], "row", up)
-    from_after = lax.ppermute(behind[:direct], "row", down)
+    nearby = after(behind, split[1])
+    from_before = lax.ppermute(nearby[rows - direct :], "row", up)
+    from_after = lax.ppermute(nearby[:direct], "row", down)
     moved = lax.ppermute(behind, "col", swap)
     rest = [lax.ppermute(x, "col", swap) for x in share]
     swapped = [lax.ppermute(after(x, moved), "sec", swap) for x in split]

time: 135 us -> 133 us (0.985)
  starting transfers between devices: 44.4 us -> 32.5 us
  waiting for transfers between devices: 42.6 us -> 52.4 us
    ppermute x2, starting transfers between devices: 9.72 us -> 2.03 us  [per_device(): swapped = [lax.ppermute(after(x, moved), 'sec', swap) for x in split]]
    ppermute x7, waiting for transfers between devices: 12.9 us -> 20.3 us  [to_side(): return lax.ppermute(x, 'row', swap_side)]
    ppermute x7, starting transfers between devices: 8.7 us -> 5.81 us  [to_side(): return lax.ppermute(x, 'row', swap_side)]
    ppermute x2, waiting for transfers between devices: 1.2 us -> 4.07 us  [per_device(): split = [lax.ppermute(x, ('sec', 'row'), inward) for x in split]]
    ppermute x2, waiting for transfers between devices: 8.01 us -> 10.6 us  [to_far(): parts.append(lax.ppermute(x[i * height:(i + 1) * height], 'row', route))]
    ppermute x5, waiting for transfers between devices: 18.8 us -> 16.4 us  [to_pair(): return lax.ppermute(x, 'row', swap_pair)]
    ppermute x5, starting transfers between devices: 8.56 us -> 7.02 us  [to_pair(): return lax.ppermute(x, 'row', swap_pair)]
  transfers between devices with their start and end apart: 25 -> 25, of which waited for: 8 -> 12; matrix products, arithmetic and copies ran while one was open for 3% -> 3% of each run, Pallas kernels for 20% -> 20%
where the time goes in v9:
time: 133 us
  waiting for transfers between devices  52.4 us (39%)
  starting transfers between devices  32.5 us (24%)
  Pallas kernels  31.5 us (24%)
  local copies, waits for them, and re-layouts  14.6 us (11%)
  other arithmetic  1.76 us (1%)
    pallas_call x8, Pallas kernels, call(): pl.pallas_call(kernel, grid_spec=pltpu.PrefetchScalarGridSpec(num_scalar_...  31.5 us
    ppermute x7, waiting for transfers between devices, to_side(): return lax.ppermute(x, 'row', swap_side)  20.3 us
    ppermute x5, waiting for transfers between devices, to_pair(): return lax.ppermute(x, 'row', swap_pair)  16.4 us
    ppermute x2, waiting for transfers between devices, to_far(): parts.append(lax.ppermute(x[i * height:(i + 1) * height], 'row', route))  10.6 us
    unnamed x18, local copies, waits for them, and re-layouts  9.11 us
    ppermute x5, starting transfers between devices, to_pair(): return lax.ppermute(x, 'row', swap_pair)  7.02 us
    ppermute x2, starting transfers between devices, per_device(): split = [lax.ppermute(x, ('sec', 'row'), inward) for x in split]  6.13 us
    ppermute x7, starting transfers between devices, to_side(): return lax.ppermute(x, 'row', swap_side)  5.81 us
  transfers between devices with their start and end apart: 25, of which 12 were waited for; matrix products, arithmetic and copies ran while one was open for 3% of the time, Pallas kernels for 20%

profile of v9, /device:TPU:0, one launch (start us, length us, event | category | flops | bytes accessed | tf_op | source)
XLA Modules:
  0.0 133.0 jit_solution(2742181075451896315)
XLA Ops:
  3.7 5.6 %collective-permute-start.5 = (bf16[64,2048]{1,0:T(8,128)(2,1)S(1)}, bf16[64,2048]{1,0:T(8,128)(2,1)S(1)}, u32[]{:S(2)}, u32[]{:S(2)}) collective-permute-start(bf16[64,2048]{1,0:T(8,128)(2,1)S(1)} %get-tuple-element.97), channel_id=1, source_target_pairs={{2,0},{4,2},{6,4},{8,6},{10,8},{12,10},{14,12},{0,14},{16,18},{18,... | collective-permute-start | bytes 786440 | tf_op jit(solution)/shard_map/ppermute | solution.py:240
  9.3 2.0 %collective-permute-start.2 = (bf16[3,7,64,128]{3,2,1,0:T(8,128)(2,1)S(1)}, bf16[3,7,64,128]{3,2,1,0:T(8,128)(2,1)}, u32[]{:S(2)}, u32[]{:S(2)}) collective-permute-start(bf16[3,7,64,128]{3,2,1,0:T(8,128)(2,1)S(1)} %constant_dynamic-slice_fusion), channel_id=1, source_target_pairs={{0,16},{16,0},{1,17},{17,1},{2,18},{18,2},{3,19},{19,3},{4,20},{20... | collective-permute-start | bytes 1032200 | tf_op jit(solution)/shard_map/ppermute | solution.py:247
  11.8 4.1 %collective-permute-done.5.mid_ref = bf16[64,2048]{1,0:T(8,128)(2,1)S(1)} collective-permute-done((bf16[64,2048]{1,0:T(8,128)(2,1)S(1)}, bf16[64,2048]{1,0:T(8,128)(2,1)S(1)}, u32[]{:S(2)}, u32[]{:S(2)}) %collective-permute-start.5) | collective-permute-done | bytes 262176 | tf_op jit(solution)/shard_map/ppermute | solution.py:240
  15.9 2.3 %fusion = (bf16[128,2048]{1,0:T(8,128)(2,1)}, bf16[128,2048]{1,0:T(8,128)(2,1)}) fusion(bf16[1280,2048]{1,0:T(8,128)(2,1)} %here.7), kind=kLoop, calls=%fused_computation.14 | loop fusion | bytes 2097152 | tf_op jit(solution)/shard_map/slice | solution.py:250
  18.2 5.2 %collective-permute-start.7 = (bf16[128,2048]{1,0:T(8,128)(2,1)}, bf16[128,2048]{1,0:T(8,128)(2,1)S(1)}, u32[]{:S(2)}, u32[]{:S(2)}) collective-permute-start(bf16[128,2048]{1,0:T(8,128)(2,1)} %get-tuple-element.95), channel_id=1, source_target_pairs={{2,0},{4,2},{6,4},{8,6},{10,8},{12,10},{14,12},{0,14},{3,1},{5,3},... | collective-permute-start | bytes 1572872 | tf_op jit(solution)/shard_map/ppermute | solution.py:250
  24.4 2.3 %copy-done.1 = bf16[1280,2048]{1,0:T(8,128)(2,1)} copy-done((bf16[1280,2048]{1,0:T(8,128)(2,1)}, bf16[1280,2048]{1,0:T(8,128)(2,1)S(1)}, u32[]{:S(2)}) %copy-start.1) | copy-done | bytes 5242904
  30.3 2.5 %copy-done = bf16[1280,2048]{1,0:T(8,128)(2,1)S(1)} copy-done((bf16[1280,2048]{1,0:T(8,128)(2,1)S(1)}, bf16[1280,2048]{1,0:T(8,128)(2,1)}, u32[]{:S(2)}) %copy-start) | copy-done | bytes 5242904
  32.8 2.5 %copy-done.2 = bf16[1280,2048]{1,0:T(8,128)(2,1)S(1)} copy-done((bf16[1280,2048]{1,0:T(8,128)(2,1)S(1)}, bf16[1280,2048]{1,0:T(8,128)(2,1)}, u32[]{:S(2)}) %copy-start.2) | copy-done | bytes 5242904
  36.2 8.0 %inner_rows.1 = (bf16[2,768,1024]{2,1,0:T(8,128)(2,1)S(1)}, f32[2,2,256,1024]{3,2,1,0:T(8,128)S(1)}, bf16[4,128,896]{2,1,0:T(8,128)(2,1)S(1)}) custom-call(s32[10,7]{1,0:T(8,128)S(1)} %copy.5.nb_ref, s32[10,7]{1,0:T(8,128)S(1)} %copy.6.mask_ref, s32[1]{0:T(128)} %bitcast.sec_ref, s32[1]{0:T(128)} %bitcast.1.col_ref, s32[1]{0:T(128)} %bitcast.2.row_ref, ...), custom_call_target="tpu_custom_call" | custom-call | flops 1 | bytes 1 | tf_op jit(solution)/shard_map/inner_rows/pallas_call | solution.py:16
  44.2 3.0 %rim_rows.2 = (bf16[512,1024]{1,0:T(8,128)(2,1)S(1)}, bf16[256,1024]{1,0:T(8,128)(2,1)S(1)}, bf16[256,1024]{1,0:T(8,128)(2,1)S(1)}) custom-call(s32[10,7]{1,0:T(8,128)S(1)} %copy.5.nb_ref, s32[10,7]{1,0:T(8,128)S(1)} %copy.6.mask_ref, s32[1]{0:T(128)} %bitcast.sec_ref, s32[1]{0:T(128)} %bitcast.1.col_ref, s32[1]{0:T(128)} %bitcast.2.row_ref, ...), custom_call_target="tpu_custom_call" | custom-call | flops 1 | bytes 1 | tf_op jit(solution)/shard_map/rim_rows/pallas_call | solution.py:16
  48.4 2.8 %units.4 = (bf16[256,1024]{1,0:T(8,128)(2,1)S(1)}, f32[256,1024]{1,0:T(8,128)S(1)}) custom-call(s32[1]{0:T(128)} %bitcast.sec_ref, s32[1]{0:T(128)} %bitcast.1.col_ref, s32[1]{0:T(128)} %bitcast.2.row_ref, s32[8]{0:T(128)S(1)} %stack.35.index_ref, bf16[1280,2048]{1,0:T(8,128)(2,1)S(1)} %copy-done, bf16[1280,2048]{1,0:T(8,128)(2,1)S(1)} %copy-done.2, ...), custom_call_target="tpu_custom_call" | custom-call | flops 1 | bytes 1 | tf_op jit(solution)/shard_map/units/pallas_call | solution.py:16
  52.2 2.9 %rim_rows.3 = (bf16[512,1024]{1,0:T(8,128)(2,1)S(1)}, bf16[256,1024]{1,0:T(8,128)(2,1)S(1)}, bf16[256,1024]{1,0:T(8,128)(2,1)S(1)}) custom-call(s32[10,7]{1,0:T(8,128)S(1)} %copy.5.nb_ref, s32[10,7]{1,0:T(8,128)S(1)} %copy.6.mask_ref, s32[1]{0:T(128)} %bitcast.sec_ref, s32[1]{0:T(128)} %bitcast.1.col_ref, s32[1]{0:T(128)} %bitcast.2.row_ref, ...), custom_call_target="tpu_custom_call" | custom-call | flops 1 | bytes 1 | tf_op jit(solution)/shard_map/rim_rows/pallas_call | solution.py:16
  55.1 7.0 %collective-permute-done.11 = bf16[256,1024]{1,0:T(8,128)(2,1)S(1)} collective-permute-done((bf16[256,1024]{1,0:T(8,128)(2,1)S(1)}, bf16[256,1024]{1,0:T(8,128)(2,1)S(1)}, u32[]{:S(2)}, u32[]{:S(2)}) %collective-permute-start.11) | collective-permute-done | bytes 524320 | tf_op jit(solution)/shard_map/ppermute | solution.py:297
  63.4 5.2 %units.5 = (bf16[256,1024]{1,0:T(8,128)(2,1)S(1)}, f32[256,1024]{1,0:T(8,128)S(1)}, f32[256,1024]{1,0:T(8,128)S(1)}, f32[256,1024]{1,0:T(8,128)S(1)}) custom-call(s32[1]{0:T(128)} %bitcast.sec_ref, s32[1]{0:T(128)} %bitcast.1.col_ref, s32[1]{0:T(128)} %bitcast.2.row_ref, s32[8]{0:T(128)S(1)} %stack.35.index_ref, bf16[1280,2048]{1,0:T(8,128)(2,1)S(1)} %copy-done, ...), custom_call_target="tpu_custom_call" | custom-call | flops 1 | bytes 1 | tf_op jit(solution)/shard_map/units/pallas_call | solution.py:16
  69.6 2.8 %units.6 = (bf16[256,1024]{1,0:T(8,128)(2,1)S(1)}, f32[256,1024]{1,0:T(8,128)S(1)}) custom-call(s32[1]{0:T(128)} %bitcast.sec_ref, s32[1]{0:T(128)} %bitcast.1.col_ref, s32[1]{0:T(128)} %bitcast.2.row_ref, s32[8]{0:T(128)S(1)} %stack.35.index_ref, bf16[1280,2048]{1,0:T(8,128)(2,1)S(1)} %copy-done, bf16[1280,2048]{1,0:T(8,128)(2,1)S(1)} %copy-done.2, ...), custom_call_target="tpu_custom_call" | custom-call | flops 1 | bytes 1 | tf_op jit(solution)/shard_map/units/pallas_call | solution.py:16
  74.7 8.1 %collective-permute-done.15 = bf16[256,1024]{1,0:T(8,128)(2,1)S(1)} collective-permute-done((bf16[256,1024]{1,0:T(8,128)(2,1)S(1)}, bf16[256,1024]{1,0:T(8,128)(2,1)S(1)}, u32[]{:S(2)}, u32[]{:S(2)}) %collective-permute-start.15) | collective-permute-done | bytes 524320 | tf_op jit(solution)/shard_map/ppermute | solution.py:300
  86.3 2.5 %collective-permute-start.21 = (bf16[256,1024]{1,0:T(8,128)(2,1)S(1)}, bf16[256,1024]{1,0:T(8,128)(2,1)S(1)}, u32[]{:S(2)}, u32[]{:S(2)}) collective-permute-start(bf16[256,1024]{1,0:T(8,128)(2,1)S(1)} %add_convert_fusion.3), channel_id=1, source_target_pairs={{0,4},{2,6},{4,0},{6,2},{8,12},{10,14},{12,8},{14,10},{1,5},{3,7},... | collective-permute-start | bytes 1572872 | tf_op jit(solution)/shard_map/ppermute | solution.py:300
  88.9 7.6 %collective-permute-done.12 = bf16[256,1024]{1,0:T(8,128)(2,1)S(1)} collective-permute-done((bf16[256,1024]{1,0:T(8,128)(2,1)S(1)}, bf16[256,1024]{1,0:T(8,128)(2,1)S(1)}, u32[]{:S(2)}, u32[]{:S(2)}) %collective-permute-start.12) | collective-permute-done | bytes 524320 | tf_op jit(solution)/shard_map/ppermute | solution.py:300
  96.6 5.3 %units.7 = (f32[256,1024]{1,0:T(8,128)S(1)}, bf16[256,1024]{1,0:T(8,128)(2,1)S(1)}, f32[256,1024]{1,0:T(8,128)S(1)}, f32[256,1024]{1,0:T(8,128)S(1)}) custom-call(s32[1]{0:T(128)} %bitcast.sec_ref, s32[1]{0:T(128)} %bitcast.1.col_ref, s32[1]{0:T(128)} %bitcast.2.row_ref, s32[8]{0:T(128)S(1)} %stack.35.index_ref, bf16[1280,2048]{1,0:T(8,128)(2,1)S(1)} %copy-done, ...), custom_call_target="tpu_custom_call" | custom-call | flops 1 | bytes 1 | tf_op jit(solution)/shard_map/units/pallas_call | solution.py:16
  102.0 3.5 %collective-permute-done.17 = bf16[256,1024]{1,0:T(8,128)(2,1)S(1)} collective-permute-done((bf16[256,1024]{1,0:T(8,128)(2,1)S(1)}, bf16[256,1024]{1,0:T(8,128)(2,1)S(1)}, u32[]{:S(2)}, u32[]{:S(2)}) %collective-permute-start.17) | collective-permute-done | bytes 524320 | tf_op jit(solution)/shard_map/ppermute | solution.py:297
  107.1 2.1 %collective-permute-start.22 = (bf16[256,1024]{1,0:T(8,128)(2,1)S(1)}, bf16[256,1024]{1,0:T(8,128)(2,1)S(1)}, u32[]{:S(2)}, u32[]{:S(2)}) collective-permute-start(bf16[256,1024]{1,0:T(8,128)(2,1)S(1)} %add_convert_fusion), channel_id=1, source_target_pairs={{0,8},{2,10},{4,12},{6,14},{8,0},{10,2},{12,4},{14,6},{1,9},{3,11}... | collective-permute-start | bytes 1572872 | tf_op jit(solution)/shard_map/ppermute | solution.py:306
  109.2 2.2 %collective-permute-start.23 = (bf16[256,1024]{1,0:T(8,128)(2,1)S(1)}, bf16[256,1024]{1,0:T(8,128)(2,1)S(1)}, u32[]{:S(2)}, u32[]{:S(2)}) collective-permute-start(bf16[256,1024]{1,0:T(8,128)(2,1)S(1)} %add_convert_fusion.2), channel_id=1, source_target_pairs={{0,4},{2,6},{4,0},{6,2},{8,12},{10,14},{12,8},{14,10},{1,5},{3,7},... | collective-permute-start | bytes 1572872 | tf_op jit(solution)/shard_map/ppermute | solution.py:300
  112.0 8.6 %collective-permute-done.19 = bf16[256,1024]{1,0:T(8,128)(2,1)S(1)} collective-permute-done((bf16[256,1024]{1,0:T(8,128)(2,1)S(1)}, bf16[256,1024]{1,0:T(8,128)(2,1)S(1)}, u32[]{:S(2)}, u32[]{:S(2)}) %collective-permute-start.19) | collective-permute-done | bytes 524320 | tf_op jit(solution)/shard_map/ppermute | solution.py:297
  120.7 10.6 %collective-permute-done.22 = bf16[256,1024]{1,0:T(8,128)(2,1)S(1)} collective-permute-done((bf16[256,1024]{1,0:T(8,128)(2,1)S(1)}, bf16[256,1024]{1,0:T(8,128)(2,1)S(1)}, u32[]{:S(2)}, u32[]{:S(2)}) %collective-permute-start.22) | collective-permute-done | bytes 524320 | tf_op jit(solution)/shard_map/ppermute | solution.py:306
  (67 shorter events, 24.1 us)
Async XLA Ops:
  3.1 21.3 %collective-permute-start = (bf16[1280,2048]{1,0:T(8,128)(2,1)}, bf16[1280,2048]{1,0:T(8,128)(2,1)S(1)}, u32[]{:S(2)}, u32[]{:S(2)}) collective-permute-start(bf16[1280,2048]{1,0:T(8,128)(2,1)} %here.7), channel_id=1, source_target_pairs={{0,1},{1,0},{2,3},{3,2},{4,5},{5,4},{6,7},{7,6},{8,9},{9,8},{10,11... | collective-permute-start | bytes 15728648 | tf_op jit(solution)/shard_map/ppermute | solution.py:251
  3.7 12.2 %collective-permute-start.5 = (bf16[64,2048]{1,0:T(8,128)(2,1)S(1)}, bf16[64,2048]{1,0:T(8,128)(2,1)S(1)}, u32[]{:S(2)}, u32[]{:S(2)}) collective-permute-start(bf16[64,2048]{1,0:T(8,128)(2,1)S(1)} %get-tuple-element.97), channel_id=1, source_target_pairs={{2,0},{4,2},{6,4},{8,6},{10,8},{12,10},{14,12},{0,14},{16,18},{18,... | collective-permute-start | bytes 786440 | tf_op jit(solution)/shard_map/ppermute | solution.py:240
  9.3 14.1 %collective-permute-start.1 = (bf16[2,7,64,128]{3,2,1,0:T(8,128)(2,1)S(1)}, bf16[2,7,64,128]{3,2,1,0:T(8,128)(2,1)S(1)}, u32[]{:S(2)}, u32[]{:S(2)}) collective-permute-start(bf16[2,7,64,128]{3,2,1,0:T(8,128)(2,1)S(1)} %constant_dynamic-slice_fusion.1), channel_id=1, source_target_pairs={{0,16},{16,0},{1,17},{17,1},{2,18},{18,2},{3,19},{19,3},{4,20},{20... | collective-permute-start | bytes 688136 | tf_op jit(solution)/shard_map/ppermute | solution.py:247
  9.3 15.1 %collective-permute-start.2 = (bf16[3,7,64,128]{3,2,1,0:T(8,128)(2,1)S(1)}, bf16[3,7,64,128]{3,2,1,0:T(8,128)(2,1)}, u32[]{:S(2)}, u32[]{:S(2)}) collective-permute-start(bf16[3,7,64,128]{3,2,1,0:T(8,128)(2,1)S(1)} %constant_dynamic-slice_fusion), channel_id=1, source_target_pairs={{0,16},{16,0},{1,17},{17,1},{2,18},{18,2},{3,19},{19,3},{4,20},{20... | collective-permute-start | bytes 1032200 | tf_op jit(solution)/shard_map/ppermute | solution.py:247
  11.3 15.9 %collective-permute-start.8 = (bf16[64,2048]{1,0:T(8,128)(2,1)S(1)}, bf16[64,2048]{1,0:T(8,128)(2,1)S(1)}, u32[]{:S(2)}, u32[]{:S(2)}) collective-permute-start(bf16[64,2048]{1,0:T(8,128)(2,1)S(1)} %get-tuple-element.98), channel_id=1, source_target_pairs={{2,0},{4,2},{6,4},{8,6},{10,8},{12,10},{14,12},{0,14},{16,18},{18,... | collective-permute-start | bytes 786440 | tf_op jit(solution)/shard_map/ppermute | solution.py:240
  18.2 26.0 %collective-permute-start.7 = (bf16[128,2048]{1,0:T(8,128)(2,1)}, bf16[128,2048]{1,0:T(8,128)(2,1)S(1)}, u32[]{:S(2)}, u32[]{:S(2)}) collective-permute-start(bf16[128,2048]{1,0:T(8,128)(2,1)} %get-tuple-element.95), channel_id=1, source_target_pairs={{2,0},{4,2},{6,4},{8,6},{10,8},{12,10},{14,12},{0,14},{3,1},{5,3},... | collective-permute-start | bytes 1572872 | tf_op jit(solution)/shard_map/ppermute | solution.py:250
  23.3 20.8 %collective-permute-start.6 = (bf16[128,2048]{1,0:T(8,128)(2,1)}, bf16[128,2048]{1,0:T(8,128)(2,1)S(1)}, u32[]{:S(2)}, u32[]{:S(2)}) collective-permute-start(bf16[128,2048]{1,0:T(8,128)(2,1)} %get-tuple-element.96), channel_id=1, source_target_pairs={{0,2},{2,4},{4,6},{6,8},{8,10},{10,12},{12,14},{14,0},{1,3},{3,5},... | collective-permute-start | bytes 1572872 | tf_op jit(solution)/shard_map/ppermute | solution.py:249
  26.7 3.5 %collective-permute-start.4 = (bf16[3,7,64,128]{3,2,1,0:T(8,128)(2,1)}, bf16[3,7,64,128]{3,2,1,0:T(8,128)(2,1)}, u32[]{:S(2)}, u32[]{:S(2)}) collective-permute-start(bf16[3,7,64,128]{3,2,1,0:T(8,128)(2,1)} %collective-permute-done.2.refs_1_), channel_id=1, source_target_pairs={{0,1},{1,0},{2,3},{3,2},{4,5},{5,4},{6,7},{7,6},{8,9},{9,8},{10,11... | collective-permute-start | bytes 1032200 | tf_op jit(solution)/shard_map/ppermute | solution.py:252
  27.2 16.9 %collective-permute-start.9 = (bf16[64,2048]{1,0:T(8,128)(2,1)S(1)}, bf16[64,2048]{1,0:T(8,128)(2,1)S(1)}, u32[]{:S(2)}, u32[]{:S(2)}) collective-permute-start(bf16[64,2048]{1,0:T(8,128)(2,1)S(1)} %collective-permute-done.8.far_ref), channel_id=1, source_target_pairs={{0,16},{16,0},{1,17},{17,1},{2,18},{18,2},{3,19},{19,3},{4,20},{20... | collective-permute-start | bytes 786440 | tf_op jit(solution)/shard_map/ppermute | solution.py:253
  28.2 16.0 %collective-permute-start.10 = (bf16[64,2048]{1,0:T(8,128)(2,1)S(1)}, bf16[64,2048]{1,0:T(8,128)(2,1)S(1)}, u32[]{:S(2)}, u32[]{:S(2)}) collective-permute-start(bf16[64,2048]{1,0:T(8,128)(2,1)S(1)} %collective-permute-done.5.mid_ref), channel_id=1, source_target_pairs={{0,16},{16,0},{1,17},{17,1},{2,18},{18,2},{3,19},{19,3},{4,20},{20... | collective-permute-start | bytes 786440 | tf_op jit(solution)/shard_map/ppermute | solution.py:253
  47.2 14.9 %collective-permute-start.11 = (bf16[256,1024]{1,0:T(8,128)(2,1)S(1)}, bf16[256,1024]{1,0:T(8,128)(2,1)S(1)}, u32[]{:S(2)}, u32[]{:S(2)}) collective-permute-start(bf16[256,1024]{1,0:T(8,128)(2,1)S(1)} %get-tuple-element.60), channel_id=1, source_target_pairs={{0,2},{2,0},{4,6},{6,4},{8,10},{10,8},{12,14},{14,12},{1,3},{3,1},... | collective-permute-start | bytes 1572872 | tf_op jit(solution)/shard_map/ppermute | solution.py:297
  47.3 25.2 %collective-permute-start.18 = (bf16[256,1024]{1,0:T(8,128)(2,1)S(1)}, bf16[256,1024]{1,0:T(8,128)(2,1)S(1)}, u32[]{:S(2)}, u32[]{:S(2)}) collective-permute-start(bf16[256,1024]{1,0:T(8,128)(2,1)S(1)} %get-tuple-element.83), channel_id=1, source_target_pairs={{0,4},{2,6},{4,0},{6,2},{8,12},{10,14},{12,8},{14,10},{1,5},{3,7},... | collective-permute-start | bytes 1572872 | tf_op jit(solution)/shard_map/ppermute | solution.py:300
  51.3 22.1 %collective-permute-start.14 = (bf16[256,1024]{1,0:T(8,128)(2,1)S(1)}, bf16[256,1024]{1,0:T(8,128)(2,1)S(1)}, u32[]{:S(2)}, u32[]{:S(2)}) collective-permute-start(bf16[256,1024]{1,0:T(8,128)(2,1)S(1)} %get-tuple-element.71), channel_id=1, source_target_pairs={{0,2},{2,0},{4,6},{6,4},{8,10},{10,8},{12,14},{14,12},{1,3},{3,1},... | collective-permute-start | bytes 1572872 | tf_op jit(solution)/shard_map/ppermute | solution.py:297
  62.2 20.5 %collective-permute-start.15 = (bf16[256,1024]{1,0:T(8,128)(2,1)S(1)}, bf16[256,1024]{1,0:T(8,128)(2,1)S(1)}, u32[]{:S(2)}, u32[]{:S(2)}) collective-permute-start(bf16[256,1024]{1,0:T(8,128)(2,1)S(1)} %add_convert_fusion.5), channel_id=1, source_target_pairs={{0,4},{2,6},{4,0},{6,2},{8,12},{10,14},{12,8},{14,10},{1,5},{3,7},... | collective-permute-start | bytes 1572872 | tf_op jit(solution)/shard_map/ppermute | solution.py:300
  62.3 22.2 %collective-permute-start.13 = (bf16[256,1024]{1,0:T(8,128)(2,1)S(1)}, bf16[256,1024]{1,0:T(8,128)(2,1)S(1)}, u32[]{:S(2)}, u32[]{:S(2)}) collective-permute-start(bf16[256,1024]{1,0:T(8,128)(2,1)S(1)} %get-tuple-element.69), channel_id=1, source_target_pairs={{0,2},{2,0},{4,6},{6,4},{8,10},{10,8},{12,14},{14,12},{1,3},{3,1},... | collective-permute-start | bytes 1572872 | tf_op jit(solution)/shard_map/ppermute | solution.py:297
  68.6 27.9 %collective-permute-start.12 = (bf16[256,1024]{1,0:T(8,128)(2,1)S(1)}, bf16[256,1024]{1,0:T(8,128)(2,1)S(1)}, u32[]{:S(2)}, u32[]{:S(2)}) collective-permute-start(bf16[256,1024]{1,0:T(8,128)(2,1)S(1)} %get-tuple-element.66), channel_id=1, source_target_pairs={{0,4},{2,6},{4,0},{6,2},{8,12},{10,14},{12,8},{14,10},{1,5},{3,7},... | collective-permute-start | bytes 1572872 | tf_op jit(solution)/shard_map/ppermute | solution.py:300
  73.3 32.8 %collective-permute-start.20 = (bf16[256,1024]{1,0:T(8,128)(2,1)S(1)}, bf16[256,1024]{1,0:T(8,128)(2,1)S(1)}, u32[]{:S(2)}, u32[]{:S(2)}) collective-permute-start(bf16[256,1024]{1,0:T(8,128)(2,1)S(1)} %get-tuple-element.87), channel_id=1, source_target_pairs={{0,2},{2,0},{4,6},{6,4},{8,10},{10,8},{12,14},{14,12},{1,3},{3,1},... | collective-permute-start | bytes 1572872 | tf_op jit(solution)/shard_map/ppermute | solution.py:297
  83.0 22.9 %collective-permute-start.16 = (bf16[256,1024]{1,0:T(8,128)(2,1)S(1)}, bf16[256,1024]{1,0:T(8,128)(2,1)S(1)}, u32[]{:S(2)}, u32[]{:S(2)}) collective-permute-start(bf16[256,1024]{1,0:T(8,128)(2,1)S(1)} %add_convert_fusion.4), channel_id=1, source_target_pairs={{0,8},{2,10},{4,12},{6,14},{8,0},{10,2},{12,4},{14,6},{1,9},{3,11}... | collective-permute-start | bytes 1572872 | tf_op jit(solution)/shard_map/ppermute | solution.py:306
  84.6 20.9 %collective-permute-start.17 = (bf16[256,1024]{1,0:T(8,128)(2,1)S(1)}, bf16[256,1024]{1,0:T(8,128)(2,1)S(1)}, u32[]{:S(2)}, u32[]{:S(2)}) collective-permute-start(bf16[256,1024]{1,0:T(8,128)(2,1)S(1)} %get-tuple-element.78), channel_id=1, source_target_pairs={{0,2},{2,0},{4,6},{6,4},{8,10},{10,8},{12,14},{14,12},{1,3},{3,1},... | collective-permute-start | bytes 1572872 | tf_op jit(solution)/shard_map/ppermute | solution.py:297
  86.3 20.5 %collective-permute-start.21 = (bf16[256,1024]{1,0:T(8,128)(2,1)S(1)}, bf16[256,1024]{1,0:T(8,128)(2,1)S(1)}, u32[]{:S(2)}, u32[]{:S(2)}) collective-permute-start(bf16[256,1024]{1,0:T(8,128)(2,1)S(1)} %add_convert_fusion.3), channel_id=1, source_target_pairs={{0,4},{2,6},{4,0},{6,2},{8,12},{10,14},{12,8},{14,10},{1,5},{3,7},... | collective-permute-start | bytes 1572872 | tf_op jit(solution)/shard_map/ppermute | solution.py:300
  105.6 14.9 %collective-permute-start.19 = (bf16[256,1024]{1,0:T(8,128)(2,1)S(1)}, bf16[256,1024]{1,0:T(8,128)(2,1)S(1)}, u32[]{:S(2)}, u32[]{:S(2)}) collective-permute-start(bf16[256,1024]{1,0:T(8,128)(2,1)S(1)} %add_convert_fusion.1), channel_id=1, source_target_pairs={{0,2},{2,0},{4,6},{6,4},{8,10},{10,8},{12,14},{14,12},{1,3},{3,1},... | collective-permute-start | bytes 1572872 | tf_op jit(solution)/shard_map/ppermute | solution.py:297
  107.1 24.3 %collective-permute-start.22 = (bf16[256,1024]{1,0:T(8,128)(2,1)S(1)}, bf16[256,1024]{1,0:T(8,128)(2,1)S(1)}, u32[]{:S(2)}, u32[]{:S(2)}) collective-permute-start(bf16[256,1024]{1,0:T(8,128)(2,1)S(1)} %add_convert_fusion), channel_id=1, source_target_pairs={{0,8},{2,10},{4,12},{6,14},{8,0},{10,2},{12,4},{14,6},{1,9},{3,11}... | collective-permute-start | bytes 1572872 | tf_op jit(solution)/shard_map/ppermute | solution.py:306
  109.2 22.4 %collective-permute-start.23 = (bf16[256,1024]{1,0:T(8,128)(2,1)S(1)}, bf16[256,1024]{1,0:T(8,128)(2,1)S(1)}, u32[]{:S(2)}, u32[]{:S(2)}) collective-permute-start(bf16[256,1024]{1,0:T(8,128)(2,1)S(1)} %add_convert_fusion.2), channel_id=1, source_target_pairs={{0,4},{2,6},{4,0},{6,2},{8,12},{10,14},{12,8},{14,10},{1,5},{3,7},... | collective-permute-start | bytes 1572872 | tf_op jit(solution)/shard_map/ppermute | solution.py:300
  111.4 20.1 %collective-permute-start.24 = (bf16[256,1024]{1,0:T(8,128)(2,1)S(1)}, bf16[256,1024]{1,0:T(8,128)(2,1)S(1)}, u32[]{:S(2)}, u32[]{:S(2)}) collective-permute-start(bf16[256,1024]{1,0:T(8,128)(2,1)S(1)} %get-tuple-element.92), channel_id=1, source_target_pairs={{0,2},{2,0},{4,6},{6,4},{8,10},{10,8},{12,14},{14,12},{1,3},{3,1},... | collective-permute-start | bytes 1572872 | tf_op jit(solution)/shard_map/ppermute | solution.py:297
  (9 other events, 102.4 us)
